TPU v7x, 32 devices: a whole 2x2x4 slice. The times are simulated.
32 devices in a mesh: rows: 4 (over y, x), cols: 8 (over z, core).
Axes of the slice: x: 2, y: 2, z: 4, core: 2. Of those that a mesh axis runs over, the one named last changes fastest.
Arguments:
- features: bfloat16 [2, 4096, 100], P(None, ('rows', 'cols')), may hold values from -6 to 6
- adjacency: bfloat16 [2, 4096, 4, 8, 128], P(None, 'rows', None, 'cols'), may hold values from -0.125 to 0.125
- block_mask: int32 [2, 32, 4, 8, 1], P(None, 'rows', None, 'cols'), may hold values 0 or 1
- diagonal: float32 [2, 4096], P(None, ('rows', 'cols')), may hold values from 0.2 to 1
- labels: int32 [2, 4096], P(None, ('rows', 'cols')), may hold values from 0 to 46
- train_mask: int32 [2, 4096], P(None, ('rows', 'cols')), may hold values from 0 to 1, as said below
- params: float32 [4501504], P(('rows', 'cols')), as said below
- first_moment: float32 [4501504], P(('rows', 'cols'))
- second_moment: float32 [4501504], P(('rows', 'cols')), as said below
Outputs:
- new_params: float32 [4501504], P(('rows', 'cols'))
- new_first: float32 [4501504], P(('rows', 'cols'))
- new_second: float32 [4501504], P(('rows', 'cols'))
- grad_norm: float32 [], replicated
- loss_sum: float32 [], replicated
- node_total: float32 [], replicated
- class_bias_grad: float32 [47], replicated
Inputs may be any that keep to these rules, and one draw needn't show every extreme that they name: `train_mask`: the share of ones rises with the node's index within a micro-batch. `params`: entries beyond 4499503 are padding. `second_moment`: positive.
All inputs are finite; a program needn't handle non-finite values. No bound on the sum of `block_mask` on one device may be relied on, other than what follows from the above.
Results may differ from a plain program's by a relative error of at most 0.0068.
Values may be sent and summed in bfloat16 or wider, within the bound.
No kernel may reach another device: no remote copies, remote signals or barrier semaphores. Data moves between devices by JAX's collectives and lax.ppermute only.
A program may use at most 192 MiB of HBM per device.

v0:
```python
import math

import jax
import jax.numpy as jnp
from jax import lax
from jax.experimental import pallas as pl
from jax.experimental.pallas import tpu as pltpu
from jax.sharding import PartitionSpec as P

FIN = 100
HID = 2048
NCLS = 47
BLK = 128
MB = 2
STEP = 10
PARAMS = FIN * HID + HID * HID + HID * NCLS + 2 * HID + NCLS

LAMBDA = 1.0
CLIP_NORM = 0.01
BETA_ONE = 0.9
BETA_TWO = 0.95
EPSILON = 1e-08
WEIGHT_DECAY = 0.1
LEARN_RATE = 0.02

LANES = 128
UNIT = HID // LANES
BOTH = ("rows", "cols")
GELU_ONE = 0.7978845608028654
GELU_THREE = GELU_ONE * 0.044715
F32 = jnp.float32
FAR_BYTES = 1 << 17
BF16 = jnp.bfloat16


def swap(x, axis, bit):
    size = lax.axis_size(axis)
    return lax.ppermute(x, axis, [(i, i ^ bit) for i in range(size)])


def bits_of(size):
    return [1 << i for i in range(size.bit_length() - 1)]


def mm(left, right):
    return jnp.dot(left, right, preferred_element_type=F32)


def mm_t(left, right):
    return lax.dot_general(left, right, (((0,), (0,)), ((), ())), preferred_element_type=F32)


def mm_nt(left, right):
    return lax.dot_general(left, right, (((1,), (1,)), ((), ())), preferred_element_type=F32)


def take(x, axis, picks):
    return jnp.concatenate([lax.slice_in_dim(x, p, p + 1, axis=axis) for p in picks], axis)


def split_bit(x, axis, order, bit):
    keep = [j for j in order if not j & bit]
    run = next(i for i, j in enumerate(order) if j & bit)
    if any(bool(j & bit) != bool(i // run % 2) or j & ~bit != order[i - i // run % 2 * run] & ~bit for i, j in enumerate(order)):
        at = {j: i for i, j in enumerate(order)}
        return take(x, axis, [at[j] for j in keep]), take(x, axis, [at[j | bit] for j in keep]), keep
    shape = x.shape[:axis] + (len(order) // (2 * run), 2, run) + x.shape[axis + 1 :]
    kept_shape = x.shape[:axis] + (len(keep),) + x.shape[axis + 1 :]
    x = x.reshape(shape)
    pair = [lax.index_in_dim(x, i, axis + 1, keepdims=False).reshape(kept_shape) for i in (0, 1)]
    return pair[0], pair[1], keep


ANYWHERE = pl.BlockSpec(memory_space=pl.ANY)
IN_VMEM = pl.BlockSpec(memory_space=pltpu.VMEM)
IN_SMEM = pl.BlockSpec(memory_space=pltpu.SMEM)


def tip(x):
    while x.ndim > 2:
        x = x[0]
    return x[:8, :128].astype(F32)


def after_kernel(*refs):
    pass


def after(x, *earlier):
    earlier = [tip(e) for e in earlier]
    return pl.pallas_call(
        after_kernel,
        out_shape=jax.ShapeDtypeStruct(x.shape, x.dtype),
        in_specs=[ANYWHERE] * (1 + len(earlier)),
        out_specs=ANYWHERE,
        input_output_aliases={0: 0},
        name="after",
    )(x, *earlier)


def padded_bytes(shape, dtype):
    *front, rows, lanes = (1, 1, *shape)
    size = -(-rows // 16) * 16 * -(-lanes // LANES) * LANES * jnp.dtype(dtype).itemsize
    for n in front:
        size *= n
    return size


def call(kernel, name, out_shape, in_specs, out_specs, grid=None, room=4, scratch=()):
    more = {} if grid is None else {"grid": grid}

    def run(*args):
        outs = out_shape if isinstance(out_shape, tuple) else (out_shape,)
        specs = (*in_specs, *(out_specs if isinstance(out_specs, tuple) else (out_specs,)))
        total = room << 20
        for spec, x in zip(specs, (*args, *outs)):
            if spec.block_shape is not None:
                total += 2 * padded_bytes(spec.block_shape, x.dtype)
            elif spec.memory_space == pltpu.VMEM:
                total += padded_bytes(x.shape, x.dtype)
        large = lambda x: math.prod(x.shape) * x.dtype.itemsize >= FAR_BYTES
        args = [pltpu.with_memory_space_constraint(x, pltpu.HBM) if large(x) else x for x in args]
        placed = [
            pltpu.HBM(x.shape, x.dtype) if large(x) and spec.block_shape is not None else x
            for spec, x in zip(specs[len(args) :], outs)
        ]
        return pl.pallas_call(
            kernel,
            out_shape=tuple(placed) if isinstance(out_shape, tuple) else placed[0],
            in_specs=in_specs,
            out_specs=out_specs,
            scratch_shapes=list(scratch),
            compiler_params=pltpu.CompilerParams(vmem_limit_bytes=total),
            cost_estimate=pl.CostEstimate(flops=0, bytes_accessed=0, transcendentals=0),
            name=name,
            **more,
        )(*args)

    return run


def shaped(shape, dtype=F32):
    return jax.ShapeDtypeStruct(shape, dtype)


def lane_of(shape):
    return lax.broadcasted_iota(jnp.int32, shape, len(shape) - 1)


def masked_tile_kernel(row_order, n_across, n_pieces, where_ref, mask_ref, tile_ref, *refs):
    out_refs, wide_ref = refs[:-1], refs[-1]
    col, row = where_ref[0], where_ref[1]
    tall = BLK * n_across
    per_piece = len(row_order) // n_pieces
    for m in range(MB):
        for i, j in enumerate(row_order):
            block = col ^ j
            wide_ref[...] = tile_ref[m, pl.ds(pl.multiple_of(block * tall, tall), tall), :].astype(F32)
            piece, low = i // per_piece, i % per_piece * BLK
            for k in range(n_across):
                keep = mask_ref[(m * len(row_order) + block) * n_across + k].astype(F32)
                part = (wide_ref[pl.ds(k, BLK, n_across), :] * keep).astype(BF16)
                lanes = pl.ds(pl.multiple_of((row ^ k) * BLK, BLK), BLK)
                out_refs[m * n_pieces + piece][low : low + BLK, lanes] = part
                if piece:
                    at = MB * n_pieces + m * (n_pieces - 1) + piece - 1
                    out_refs[at][low : low + BLK, lanes] = part


def masked_tile(adjacency, block_mask, row_order, my_col, my_row):
    n_across = adjacency.shape[2]
    n_pieces = len(row_order) // 2
    piece = shaped((2 * BLK, n_across * BLK), BF16)
    n_out = MB * (2 * n_pieces - 1)
    out = call(
        lambda *refs: masked_tile_kernel(row_order, n_across, n_pieces, *refs),
        "masked_tile",
        (piece,) * n_out,
        [IN_SMEM, IN_SMEM, pl.BlockSpec((MB, adjacency.shape[1] * n_across, LANES), lambda i: (0, 0, 0))],
        (pl.BlockSpec((2 * BLK, n_across * BLK), lambda i: (0, 0)),) * n_out,
        grid=(1,),
        room=4,
        scratch=[pltpu.VMEM((n_across * BLK, LANES), F32)],
    )(
        jnp.stack([my_col, my_row]).astype(jnp.int32),
        block_mask.reshape(-1),
        adjacency.reshape(MB, -1, LANES),
    )
    tile = [out[m * n_pieces : (m + 1) * n_pieces] for m in range(MB)]
    leave = out[MB * n_pieces :]
    return tile, [leave[m * (n_pieces - 1) : (m + 1) * (n_pieces - 1)] for m in range(MB)]


def layer_one_kernel(n_z, *refs):
    tile_refs, feat_refs, (near_ref, far_ref) = refs[: MB * n_z], refs[MB * n_z : -2], refs[-2:]
    ns = near_ref.shape[2]
    for m in range(MB):
        feats = jnp.concatenate([f[m] for f in feat_refs], 0)
        for i in range(n_z):
            out = mm(tile_refs[m * n_z + i][...], feats)
            near_ref[i, m] = out[:ns]
            far_ref[i, m] = out[ns:]


def layer_one(tile, feats):
    n_z = len(tile[0])
    half, across = tile[0][0].shape
    out = shaped((n_z, MB, half // 2, LANES))
    return call(
        lambda *refs: layer_one_kernel(n_z, *refs),
        "layer_one",
        (out, out),
        [pl.BlockSpec((half, across), lambda i: (0, 0))] * (MB * n_z) + [IN_VMEM] * len(feats),
        (IN_VMEM, IN_VMEM),
        grid=(1,),
    )(*tile[0], *tile[1], *feats)


def twice_gelu(z):
    return z + z * jnp.tanh(z * (GELU_ONE + GELU_THREE * (z * z)))


def twice_gelu_both(z):
    square = z * z
    t = jnp.tanh(z * (GELU_ONE + GELU_THREE * square))
    slope = z * (GELU_ONE + (3 * GELU_THREE) * square)
    return z + z * t, (1.0 + t) * (1.0 + (1.0 - t) * slope)


def forward_kernel(n_z, n_rows, m, *refs):
    g_refs, strip_refs = refs[:n_rows], refs[n_rows : n_rows + n_z]
    w_ref, near_ref, far_ref, slope_ref = refs[n_rows + n_z :]
    half = near_ref.shape[0]
    total = None
    for i in range(n_z):
        g = jnp.concatenate([g_ref[i, m] for g_ref in g_refs], 0)
        h, slope = twice_gelu_both(mm(g, w_ref[...]))
        n = g.shape[0]
        slope_ref[i * n : (i + 1) * n] = slope.astype(BF16)
        part = mm(strip_refs[i][...], h.astype(BF16))
        total = part if total is None else total + part
    near_ref[...] = 0.5 * total[:half]
    far_ref[...] = (0.5 * total[half:]).astype(BF16)


def forward_two(g_all, w_pad, strip, m, wide=256):
    n_rows, n_z = len(g_all), len(strip)
    rows, across = strip[0].shape
    span = w_pad.shape[1]
    n = n_z * across
    return call(
        lambda *refs: forward_kernel(n_z, n_rows, m, *refs),
        "forward_two",
        (shaped((rows // 2, span)), shaped((rows // 2, span), BF16), shaped((n, span), BF16)),
        [pl.BlockSpec(g_all[0].shape, lambda f: (0, 0, 0, 0))] * n_rows
        + [pl.BlockSpec((rows, across), lambda f: (0, 0))] * n_z
        + [pl.BlockSpec((LANES, wide), lambda f: (0, f))],
        (pl.BlockSpec((rows // 2, wide), lambda f: (0, f)),) * 2 + (pl.BlockSpec((n, wide), lambda f: (0, f)),),
        grid=(span // wide,),
        room=2 + 8 * across // 1024,
    )(*g_all, *strip, w_pad)


def one_hot(here, there):
    return jnp.where(here == there, 1.0, 0.0).astype(BF16)


def spread_kernel(n_m, n_blocks, *refs):
    near_parts, far_parts = refs[:n_m], refs[n_m : 2 * n_m]
    g_one_ref, w_ref, diag_ref, which_ref, gn_ref, gf_ref, g_ref = refs[2 * n_m :]
    ns = near_parts[0].shape[0]

    @pl.when(pl.program_id(0) == 0)
    def _():
        step = 256
        for at in range(0, HID, step):
            cut = slice(at, at + step)
            h = (0.5 * twice_gelu(mm(g_one_ref[...], w_ref[:, cut]))).astype(BF16)
            for m in range(n_m):
                g_ref[m * ns : (m + 1) * ns, cut] = (
                    near_parts[m][:, cut]
                    + far_parts[m][:, cut].astype(F32)
                    + LAMBDA * diag_ref[:, m : m + 1] * h[m * ns : (m + 1) * ns].astype(F32)
                ).astype(BF16)

    which = which_ref[...]
    hot = one_hot(lax.broadcasted_iota(jnp.int32, (HID, which.shape[1]), 0), which)
    out = mm(g_ref[...], hot).astype(BF16)

    @pl.when(pl.program_id(0) < n_blocks)
    def _():
        gn_ref[...] = out

    @pl.when(pl.program_id(0) >= n_blocks)
    def _():
        gf_ref[...] = out


def block_width(n):
    return 384 if n % 384 == 0 else LANES


def spread_two(near_parts, far_parts, g_one, w_pad, diag, which):
    ns = near_parts[0].shape[0]
    n_m = len(near_parts)
    n_near = which.shape[1] // 2
    rows = n_m * ns
    wide = block_width(n_near)
    n = n_near // wide
    whole = lambda k: (0, 0)
    out = shaped((rows, n_near), BF16)
    return call(
        lambda *refs: spread_kernel(n_m, n, *refs),
        "spread_two",
        (out, out),
        [pl.BlockSpec((ns, HID), whole)] * (2 * n_m)
        + [
            pl.BlockSpec((rows, LANES), whole),
            pl.BlockSpec((LANES, HID), whole),
            pl.BlockSpec((ns, n_m), whole),
            pl.BlockSpec((1, wide), lambda k: (0, k)),
        ],
        (
            pl.BlockSpec((rows, wide), lambda k: (0, jnp.minimum(k, n - 1))),
            pl.BlockSpec((rows, wide), lambda k: (0, jnp.maximum(k - n, 0))),
        ),
        grid=(2 * n,),
        scratch=[pltpu.VMEM((rows, HID), BF16)],
        room=8,
    )(*near_parts, *far_parts, g_one, w_pad, diag, which)


def layer_two_kernel(gn_ref, gf_ref, wn_ref, wf_ref, b_ref, w3_ref, here_ref, z_ref, h_ref, q_ref, sum_ref):
    ns = sum_ref.shape[0]

    @pl.when(pl.program_id(0) == 0)
    def _():
        sum_ref[...] = jnp.zeros_like(sum_ref)

    z = mm(gn_ref[...], wn_ref[...]) + mm(gf_ref[...], wf_ref[...]) + b_ref[...]
    z_ref[...] = z
    h = (0.5 * twice_gelu(z)).astype(BF16)
    h_ref[...] = h
    q = mm(h, w3_ref[...])
    lane = lane_of(sum_ref.shape)
    sum_ref[...] += jnp.where(lane < LANES // 2, q[:ns], q[ns:])

    @pl.when(pl.program_id(0) == pl.num_programs(0) - 1)
    def _():
        q_ref[...] = jnp.where(lane == LANES - 1, here_ref[...], sum_ref[...]).astype(BF16)


def layer_two(g_near, g_far, near, far, b_second, w3, here, wide=512):
    rows, n_near = g_near.shape
    ns = rows // MB
    whole = lambda f: (0, 0)
    return call(
        layer_two_kernel,
        "layer_two",
        (shaped((rows, HID)), shaped((rows, HID), BF16), shaped((ns, LANES), BF16)),
        [
            pl.BlockSpec((rows, n_near), whole),
            pl.BlockSpec((rows, n_near), whole),
            pl.BlockSpec((n_near, wide), lambda f: (0, f)),
            pl.BlockSpec((n_near, wide), lambda f: (0, f)),
            pl.BlockSpec((1, wide), lambda f: (0, f)),
            pl.BlockSpec((wide, LANES), lambda f: (f, 0)),
            pl.BlockSpec((1, LANES), whole),
        ],
        (
            pl.BlockSpec((rows, wide), lambda f: (0, f)),
            pl.BlockSpec((rows, wide), lambda f: (0, f)),
            pl.BlockSpec((ns, LANES), whole),
        ),
        grid=(HID // wide,),
        scratch=[pltpu.VMEM((ns, LANES), F32)],
    )(g_near, g_far, near, far, b_second, w3, here)


def logits_kernel(n_z, *refs):
    strips, q_refs, (near_ref, far_ref) = refs[: MB * n_z], refs[MB * n_z : -2], refs[-2:]
    half = near_ref.shape[0]
    lane = lane_of((2 * half, LANES))
    sums = [None] * MB
    for i in range(n_z):
        all_q = jnp.concatenate([q[i] for q in q_refs], 0)
        for m in range(MB):
            part = mm(strips[m * n_z + i][...], all_q)
            sums[m] = part if sums[m] is None else sums[m] + part
    out = jnp.where(lane < LANES // 2, sums[0], sums[1])
    count = sum(jnp.sum(q[:, 0:1, :].astype(F32), axis=0) for q in q_refs)
    out = jnp.where(lane == LANES - 1, count, out)
    near_ref[...] = out[:half]
    far_ref[...] = out[half:]


def logits_parts(strips, q_rows):
    n_z = len(strips[0])
    rows, across = strips[0][0].shape
    out = shaped((rows // 2, LANES))
    return call(
        lambda *refs: logits_kernel(n_z, *refs),
        "logits_parts",
        (out, out),
        [pl.BlockSpec((rows, across), lambda i: (0, 0))] * (MB * n_z) + [IN_VMEM] * len(q_rows),
        (IN_VMEM, IN_VMEM),
        grid=(1,),
    )(*strips[0], *strips[1], *q_rows)


def loss_kernel(near_ref, got_ref, q_ref, diag_ref, bias_ref, labels_ref, counted_ref, ds_ref, row_ref):
    total = near_ref[...] + got_ref[...]
    node_total = total[0:1, LANES - 1 :]
    lane = lane_of(total.shape)
    low = lane < LANES // 2
    at = jnp.where(low, lane, lane - LANES // 2)
    real = at < NCLS
    pick = lambda ref: jnp.where(low, ref[:, 0:1], ref[:, 1:2])
    logits = total + LAMBDA * pick(diag_ref) * q_ref[...].astype(F32) + bias_ref[...]
    least = jnp.float32(-3.0e38)
    hits = jnp.logical_and(real, at == pick(labels_ref))
    counted = pick(counted_ref)
    parts = []
    for side in (jnp.logical_and(real, low), jnp.logical_and(real, jnp.logical_not(low))):
        top = jnp.max(jnp.where(side, logits, least), axis=1, keepdims=True)
        powers = jnp.where(side, jnp.exp(jnp.where(side, logits - top, 0.0)), 0.0)
        parts.append((top, jnp.sum(powers, axis=1, keepdims=True)))
    log_total = jnp.where(
        low, parts[0][0] + jnp.log(parts[0][1]), parts[1][0] + jnp.log(parts[1][1])
    )
    loss = jnp.where(hits, counted * (log_total - logits), 0.0)
    soft = jnp.exp(jnp.where(real, logits - log_total, 0.0))
    d_logits = jnp.where(real, counted * (soft - hits.astype(F32)) / node_total, 0.0)
    ds_ref[...] = d_logits.astype(BF16)
    row_ref[0:1] = jnp.sum(d_logits, axis=0, keepdims=True)
    row_ref[1:2] = jnp.broadcast_to(jnp.sum(jnp.sum(loss, axis=0, keepdims=True), axis=1, keepdims=True), (1, LANES))
    row_ref[2:3] = jnp.broadcast_to(node_total, (1, LANES))
    row_ref[3:8] = jnp.zeros((5, LANES), F32)


def d_q_kernel(n_z, *refs):
    tile_refs, s_refs, out_refs = refs[: MB * n_z], refs[MB * n_z : (MB + 1) * n_z], refs[(MB + 1) * n_z :]
    side = out_refs[0].shape[0]
    lane = lane_of((side * len(out_refs), LANES))
    sums = [None] * MB
    for i in range(n_z):
        all_s = jnp.concatenate([s_refs[i][core] for core in (0, 1)], 0)
        for m in range(MB):
            part = mm_t(tile_refs[m * n_z + i][...], all_s)
            sums[m] = part if sums[m] is None else sums[m] + part
    out = jnp.where(lane < LANES // 2, sums[0], sums[1])
    for k, out_ref in enumerate(out_refs):
        out_ref[...] = out[k * side : (k + 1) * side]


def d_q_parts(tile, pieces):
    n_z = len(pieces)
    rows, across = tile[0][0].shape
    n = across // BLK
    return call(
        lambda *refs: d_q_kernel(n_z, *refs),
        "d_q_parts",
        (shaped((BLK, LANES)),) * n,
        [pl.BlockSpec((rows, across), lambda i: (0, 0))] * (MB * n_z) + [IN_VMEM] * n_z,
        (IN_VMEM,) * n,
        grid=(1,),
    )(*tile[0], *tile[1], *pieces)


def d_two_kernel(n_q, *refs):
    q_refs = refs[:n_q]
    ds_ref, diag_ref, z_ref, h_ref, w3_ref, g_ref, dz_ref, db_ref, dw3_ref, far_ref = refs[n_q:]
    ns = ds_ref.shape[0]
    d_q = q_refs[0][...]
    for q in q_refs[1:]:
        d_q = d_q + q[...]
    low = lane_of(d_q.shape) < LANES // 2
    d_q = d_q + LAMBDA * jnp.where(low, diag_ref[:, 0:1], diag_ref[:, 1:2]) * ds_ref[...].astype(F32)
    d_q = jnp.concatenate([jnp.where(low, d_q, 0.0), jnp.where(low, 0.0, d_q)], 0).astype(BF16)
    d_z = mm_nt(d_q, w3_ref[...]) * (0.5 * twice_gelu_both(z_ref[...])[1])
    db_ref[...] = jnp.sum(d_z.reshape(-1, 8, d_z.shape[1]), axis=0)
    d_zb = d_z.astype(BF16)
    dz_ref[...] = d_zb
    dw3_ref[...] = mm_t(h_ref[...], d_q)
    far_ref[...] = mm_t(g_ref[...], d_zb).astype(BF16)


def d_two(d_q, d_s, diag, z_two, h_two, w3, g_far, lo, hi, wide=256):
    rows = z_two.shape[0]
    ns, n_far = d_s.shape[0], g_far.shape[1]
    whole = lambda f: (0, 0)
    start = lo // wide
    small = pl.BlockSpec((ns, LANES), whole)
    column = pl.BlockSpec((rows, wide), lambda f: (0, start + f))
    span = hi - lo
    return call(
        lambda *refs: d_two_kernel(len(d_q), *refs),
        "d_two",
        (
            shaped((rows, span), BF16),
            shaped((8, span)),
            shaped((span, LANES)),
            shaped((n_far, span), BF16),
        ),
        [small] * (len(d_q) + 1)
        + [
            pl.BlockSpec((ns, MB), whole),
            column,
            column,
            pl.BlockSpec((wide, LANES), lambda f: (start + f, 0)),
            pl.BlockSpec((rows, n_far), whole),
        ],
        (
            pl.BlockSpec((rows, wide), lambda f: (0, f)),
            pl.BlockSpec((8, wide), lambda f: (0, f)),
            pl.BlockSpec((wide, LANES), lambda f: (f, 0)),
            pl.BlockSpec((n_far, wide), lambda f: (0, f)),
        ),
        grid=(span // wide,),
        room=4,
    )(*d_q, d_s, diag, z_two, h_two, w3, g_far)


def near_kernel(keep, send, rows, g_ref, dz_ref, got_ref, keep_ref, send_ref):
    total = mm_t(g_ref[...], dz_ref[...]) + got_ref[...].astype(F32)
    for out_ref, picks in ((keep_ref, keep), (send_ref, send)):
        for i, j in enumerate(picks):
            out_ref[i * rows : (i + 1) * rows] = total[j * rows : (j + 1) * rows].astype(out_ref.dtype)


def near_part(g_near, d_zb, got, n_rows, bit, wide=256):
    n_near, span = got.shape
    rows = n_near // n_rows
    keep = [j for j in range(n_rows) if not j & bit]
    send = [j | bit for j in keep]
    column = lambda n: pl.BlockSpec((n, wide), lambda f: (0, f))
    return call(
        lambda *refs: near_kernel(keep, send, rows, *refs),
        "near_part",
        (shaped((n_near // 2, span)), shaped((n_near // 2, span), BF16)),
        [pl.BlockSpec(g_near.shape, lambda f: (0, 0)), column(g_near.shape[0]), column(n_near)],
        (column(n_near // 2), column(n_near // 2)),
        grid=(span // wide,),
    )(g_near, d_zb, got)


def backward_kernel(n_z, n_rows, *refs):
    g_refs, strip_refs = refs[:n_rows], refs[n_rows : n_rows + MB * n_z]
    slope_refs, (dgn_ref, dgf_ref, diag_ref, dw_ref) = refs[-4 - MB : -4], refs[-4:]
    own = dgn_ref.shape[1]
    total = None
    for m in range(MB):
        d_g = jnp.concatenate([dgn_ref[m], dgf_ref[m]], 0)
        for i in range(n_z):
            d_h = mm_t(strip_refs[m * n_z + i][...], d_g)
            n = d_h.shape[0]
            if i == 0:
                more = LAMBDA * diag_ref[:, m : m + 1] * dgn_ref[m].astype(F32)
                d_h = jnp.concatenate([d_h[:own] + more, d_h[own:]], 0)
            g = jnp.concatenate([g_ref[i, m] for g_ref in g_refs], 0)
            d_z = d_h * slope_refs[m][i * n : (i + 1) * n].astype(F32)
            part = mm_t(g, d_z.astype(BF16))
            total = part if total is None else total + part
    dw_ref[...] = (0.5 * total).astype(BF16)


def backward_one(g_all, strips, slopes, d_g_near, d_g_far, diag, lo, hi, wide=256):
    n_rows, n_z = len(g_all), len(strips[0])
    rows, across = strips[0][0].shape
    span = hi - lo
    start = lo // wide
    column = pl.BlockSpec((MB, rows // 2, wide), lambda f: (0, 0, start + f))
    return call(
        lambda *refs: backward_kernel(n_z, n_rows, *refs),
        "backward_one",
        shaped((LANES, span), BF16),
        [pl.BlockSpec(g_all[0].shape, lambda f: (0, 0, 0, 0))] * n_rows
        + [pl.BlockSpec((rows, across), lambda f: (0, 0))] * (MB * n_z)
        + [pl.BlockSpec((n_z * across, wide), lambda f: (0, start + f))] * MB
        + [column, column, pl.BlockSpec((rows // 2, MB), lambda f: (0, 0))],
        pl.BlockSpec((LANES, wide), lambda f: (0, f)),
        grid=(span // wide,),
        room=2 + 8 * across // 1024,
    )(*g_all, *strips[0], *strips[1], *slopes, d_g_near, d_g_far, diag)


def d_g_kernel(n_blocks, cuts, *refs):
    dz_refs, (which_ref, wn_ref, wf_ref, out_ref, sum_ref) = refs[: len(cuts)], refs[len(cuts) :]
    step = pl.program_id(0)

    @pl.when(step == 0)
    def _():
        sum_ref[...] = jnp.zeros_like(sum_ref)

    def add(w_ref):
        part = sum(mm_nt(dz[...], w_ref[:, lo:hi]) for dz, (lo, hi) in zip(dz_refs, cuts)).astype(BF16)
        which = which_ref[...]
        hot = one_hot(lax.broadcasted_iota(jnp.int32, (which.shape[0], HID), 1), which)
        sum_ref[...] += mm(part, hot)

    @pl.when(step < n_blocks)
    def _():
        add(wn_ref)

    @pl.when(step >= n_blocks)
    def _():
        add(wf_ref)

    @pl.when(step == pl.num_programs(0) - 1)
    def _():
        out_ref[...] = sum_ref[...].astype(BF16)


def d_g_two(d_zb, cuts, which, near, far):
    rows, n_near = d_zb[0].shape[0], near.shape[0]
    wide = block_width(n_near)
    n = n_near // wide
    return call(
        lambda *refs: d_g_kernel(n, cuts, *refs),
        "d_g_two",
        shaped((rows, HID), BF16),
        [pl.BlockSpec(d.shape, lambda k: (0, 0)) for d in d_zb]
        + [
            pl.BlockSpec((wide, 1), lambda k: (k, 0)),
            pl.BlockSpec((wide, HID), lambda k: (jnp.minimum(k, n - 1), 0)),
            pl.BlockSpec((wide, HID), lambda k: (jnp.maximum(k - n, 0), 0)),
        ],
        pl.BlockSpec((rows, HID), lambda k: (0, 0)),
        grid=(2 * n,),
        scratch=[pltpu.VMEM((rows, HID), F32)],
        room=8,
    )(*d_zb, which, near, far)


def thirds_kernel(row_ref, out_ref):
    rest = row_ref[...]
    out_ref[...] = jnp.zeros_like(out_ref)
    for i in range(3):
        low = rest.astype(BF16)
        out_ref[i : i + 1] = low
        rest = rest - low.astype(F32)


def thirds(row):
    return call(thirds_kernel, "thirds", shaped((16, LANES), BF16), [IN_VMEM], IN_VMEM)(row)


def join_kernel(sizes, *refs):
    pieces, out_ref, sems = refs[: len(sizes)], refs[len(sizes)], refs[-1]
    at, copies = 0, []
    for i, (piece, size) in enumerate(zip(pieces, sizes)):
        copies.append(pltpu.make_async_copy(piece, out_ref.at[pl.ds(at, size)], sems.at[i]))
        copies[-1].start()
        at += size
    for copy in copies:
        copy.wait()


def join(pieces):
    sizes = [p.shape[0] for p in pieces]
    return call(
        lambda *refs: join_kernel(sizes, *refs),
        "join",
        shaped((sum(sizes),) + pieces[0].shape[1:], pieces[0].dtype),
        [ANYWHERE] * len(pieces),
        IN_VMEM,
        room=2,
        scratch=[pltpu.SemaphoreType.DMA((len(pieces),))],
    )(*pieces)


def per_device(features, adjacency, block_mask, diagonal, labels, train_mask, params, first_moment, second_moment):
    n_rows, n_cols = lax.axis_size("rows"), lax.axis_size("cols")
    n_z = n_cols // 2
    n_dev = n_rows * n_cols
    my_row, my_col = lax.axis_index("rows"), lax.axis_index("cols")
    me = my_row * n_cols + my_col
    ns = features.shape[1]
    z_bits, row_bits = bits_of(n_z), bits_of(n_rows)
    turned = row_bits[1:] + row_bits[:1]
    single = z_bits[::-1]
    several = [j for j in range(1, n_z) if j not in single]
    z_order = [0] + single + several

    def over_z(x):
        return [x] + [swap(x, "cols", 2 * j) for j in z_order[1:]]

    def over_rows(x):
        return [x] + [swap(x, "rows", j) for j in range(1, n_rows)]

    n_own = params.shape[0] // LANES
    slot = -(-((n_own + UNIT - 2) // UNIT + 1) // 8) * 8
    shift = lax.rem(n_own * me, UNIT)
    own = lax.dynamic_update_slice(
        jnp.zeros((slot * UNIT, LANES), BF16), params.reshape(n_own, LANES).astype(BF16), (shift, 0)
    ).reshape(1, slot, HID)
    wide_feats = jnp.pad(features, ((0, 0), (0, 0), (0, LANES - FIN)))
    ones = lax.broadcasted_iota(jnp.int32, (1, 1, LANES), 2) == FIN
    feats = over_rows(wide_feats)
    tile, leave = masked_tile(
        adjacency.reshape(MB, -1, n_rows, LANES), block_mask, [2 * j + core for j in z_order for core in (0, 1)], my_col, my_row
    )

    part_near, part_far = layer_one(tile, feats)
    own = after(own, part_far)
    by_z = {0: own}
    for j in single:
        by_z[j] = swap(own, "cols", 2 * j)
    partial = part_near + swap(part_far, "cols", 1)
    g_one = partial[0] + LAMBDA * diagonal[:, :, None] * wide_feats.astype(F32)
    low = partial.astype(BF16)
    for i, j in enumerate(z_order[1:], 1):
        g_one = g_one + swap(low[i], "cols", 2 * j).astype(F32)
    g_one = jnp.where(ones, 1.0, g_one).astype(BF16)

    def units_of(core):
        owner = (my_row ^ jnp.arange(n_rows))[:, None] * n_cols + (
            my_col ^ (2 * jnp.array(z_order) + core)
        )[None, :]
        start = (n_own * owner) // UNIT
        return (start[:, :, None] + jnp.arange(slot)[None, None, :]).reshape(-1)

    near_units = units_of(0)
    units = jnp.concatenate([near_units, units_of(1)])
    which = units - FIN

    middle = after(join([by_z[j] for j in single]), g_one)
    for j in several:
        bit = j & -j
        by_z[j] = swap(by_z[j - bit], "cols", 2 * bit)
    last = by_z[several[0]] if len(several) == 1 else join([by_z[j] for j in several])
    g_z = over_z(g_one)
    last = after(last, *g_z[1:])
    groups = [own, middle, last]
    g_all = over_rows(jnp.stack(g_z))
    strips = [[tile[m][0]] for m in range(MB)]
    for i, j in enumerate(z_order[1:]):
        strips[0].append(swap(after(leave[0][i], *g_all[1:]), "cols", 2 * j))
    passed = {0: groups}
    for j in range(1, n_rows):
        lowest = j & -j
        highest = 1 << (j.bit_length() - 1)
        hop = [passed[j - bit][i] for i, bit in enumerate((highest, lowest, highest))]
        if lowest != highest:
            hop = [after(h, *g_all[1:]) for h in hop]
        passed[j] = [swap(h, "rows", bit) for h, bit in zip(hop, (highest, lowest, highest))]
    for m in range(1, MB):
        for i, j in enumerate(z_order[1:]):
            strips[m].append(swap(after(leave[m][i], *strips[m - 1][1:]), "cols", 2 * j))
    passed[0][0] = after(passed[0][0], *strips[0][1:])
    near = join([g.reshape(-1, HID) for j in range(n_rows) for g in passed[j]])
    far = swap(near, "cols", 1)
    n_near = near.shape[0]

    per_small = -(-(FIN + NCLS + 3) // n_dev)
    n_small = per_small * n_dev
    small_unit = jnp.arange(n_small)
    small_unit = jnp.where(small_unit < FIN, small_unit, small_unit + HID)
    pick = (small_unit[:, None] == near_units[None, :]).astype(BF16)
    small = mm(pick, near).astype(BF16)
    small = small + swap(small, "cols", 1)
    w_pad = jnp.concatenate(
        [small[:FIN], small[FIN + NCLS : FIN + NCLS + 1], jnp.zeros((LANES - FIN - 1, HID), BF16)], 0
    )
    w_third = small[FIN : FIN + NCLS].reshape(HID, NCLS)
    gap = jnp.zeros((HID, LANES // 2 - NCLS), BF16)
    w_third = jnp.concatenate([w_third, gap, w_third, gap], 1)
    b_second = small[FIN + NCLS + 1].astype(F32)[None]
    b_third = small[FIN + NCLS + 2].astype(F32)[: LANES // 2]
    b_third = jnp.concatenate([b_third, b_third])[None]

    near_parts, far_parts, slopes = [], [], []
    for m in range(MB):
        if m == MB - 1:
            w_pad = after(w_pad, w_third)
        part_near, part_far, slope = forward_two(g_all, w_pad, strips[m], m)
        slopes.append(slope)
        near_parts.append(part_near)
        far_parts.append(swap(part_far, "cols", 1))

    diag = diagonal.T
    counted = train_mask.T.astype(F32)
    here = jnp.broadcast_to(jnp.sum(counted), (1, LANES))
    g_near, g_far = spread_two(
        near_parts, far_parts, g_one.reshape(MB * ns, LANES), w_pad, diag, which[None]
    )
    z_two, h_two, q = layer_two(g_near, g_far, near, far, b_second, w_third, here)

    part_near, part_far = logits_parts(strips, over_rows(jnp.stack(over_z(q))))
    d_s, sums = call(
        loss_kernel,
        "loss",
        (shaped((ns, LANES), BF16), shaped((8, LANES))),
        [IN_VMEM] * 7,
        (IN_VMEM, IN_VMEM),
    )(part_near, swap(part_far, "cols", 1), q, diag, b_third, labels.T, counted)
    d_bias_three = sums[0, :NCLS] + sums[0, LANES // 2 : LANES // 2 + NCLS]
    loss, node_total = sums[1, 0], sums[2, 0]

    d_q = d_q_parts(tile, over_z(jnp.stack([d_s, swap(d_s, "cols", 1)])))
    d_q = [d_q[0]] + [swap(d_q[j], "rows", j) for j in range(1, n_rows)]

    def split(item, axis, bit):
        dim = 0 if axis == "rows" else 1
        kept, send, item["orders"][axis] = split_bit(item["part"], dim, item["orders"][axis], bit)
        item["kept"], item["send"] = kept, send.astype(BF16)
        item["to"] = (axis, bit * (dim + 1))

    half = HID // 2
    work = []
    for k, bits in enumerate((row_bits, turned)):
        lo, hi = k * half, (k + 1) * half
        wait = d_s if k == 0 else after(d_s, work[0]["dz"])
        d_zb, d_b, d_w3, d_far = d_two(d_q, wait, diag, z_two, h_two, w_third, g_far, lo, hi)
        item = {"bits": bits, "dz": d_zb, "db": d_b, "dw3": d_w3}
        item["got"] = swap(d_far, "cols", 1)
        item["orders"] = {"rows": [j for j in range(n_rows) if not j & bits[0]], "cols": z_order}
        item["to"] = ("rows", bits[0])
        work.append(item)
    for item in work:
        kept, send = near_part(g_near, item["dz"], item["got"], n_rows, item["bits"][0])
        item["kept"], item["send"] = (x.reshape(n_rows // 2, n_z, slot, half) for x in (kept, send))
    d_zb = [item["dz"] for item in work]
    d_bias_two = jnp.concatenate([jnp.sum(item["db"], axis=0) for item in work])
    d_w_three = jnp.concatenate([item["dw3"] for item in work], 0)
    d_w_three = d_w_three[:, :NCLS] + d_w_three[:, LANES // 2 : LANES // 2 + NCLS]

    n_cuts = 3
    cuts = [0, 3 * (HID // 8), 6 * (HID // 8), HID]
    d_zb[0] = after(d_zb[0], *[item["send"] for item in work])
    d_g_near = d_g_two(d_zb, [(0, half), (half, HID)], which[:, None], near, far).reshape(MB, ns, HID)
    d_g_far = swap(d_g_near, "cols", 1)
    d_first = []

    def another_cut():
        i = len(d_first)
        if i < n_cuts:
            d_first.append(
                backward_one(g_all, strips, slopes, d_g_near, d_g_far, diag, cuts[i], cuts[i + 1])
            )

    for i in range(len(row_bits)):
        for item in work:
            item["part"] = item["kept"] + swap(item["send"], *item["to"]).astype(F32)
            if i + 1 < len(row_bits):
                split(item, "rows", item["bits"][i + 1])
        if i + 1 < len(row_bits):
            d_g_near = after(d_g_near, *[item["send"] for item in work])
            another_cut()
    item = {"orders": {"cols": z_order}, "part": jnp.concatenate([item["part"] for item in work], 3)}
    for bit in z_bits:
        split(item, "cols", bit)
        d_g_near = after(d_g_near, item["send"])
        another_cut()
        item["part"] = item["kept"] + swap(item["send"], *item["to"]).astype(F32)
        if bit == z_bits[0]:
            early = item["part"]
    own_grad = item["part"][0, 0]
    d_first = jnp.concatenate(d_first, 1)
    d_w_one, d_bias_one = d_first[:FIN], d_first[FIN].astype(F32)

    d_small = jnp.concatenate(
        [
            d_w_one.astype(BF16),
            d_w_three.astype(BF16).reshape(NCLS, HID),
            jnp.stack([d_bias_one, d_bias_two, jnp.pad(d_bias_three, (0, HID - NCLS))]).astype(BF16),
            jnp.zeros((n_small - FIN - NCLS - 3, HID), BF16),
        ],
        0,
    )
    d_small = after(d_small.reshape(n_dev, per_small * UNIT, LANES), early)
    got = lax.all_to_all(d_small, BOTH, split_axis=0, concat_axis=0, tiled=True)
    got = jnp.sum(got.astype(F32), axis=0)
    low = got.astype(BF16)

    own_flat = lax.dynamic_slice(own_grad.reshape(slot * UNIT, LANES), (shift, 0), (n_own, LANES))
    squares = jnp.sum(own_flat * own_flat) + jnp.sum(low.astype(F32) ** 2)
    row = jnp.concatenate([squares[None], loss[None], d_bias_three, jnp.zeros((LANES - NCLS - 2,), F32)])
    sent = jnp.concatenate([low, thirds(row[None])], 0)
    sent = jnp.broadcast_to(sent[None], (n_dev,) + sent.shape)
    got = lax.all_to_all(sent, BOTH, split_axis=0, concat_axis=0, tiled=True)
    d_small = got[:, : per_small * UNIT].reshape(n_small, HID)
    row = jnp.sum(got[:, per_small * UNIT : per_small * UNIT + 3].astype(F32), axis=(0, 1))
    squares, loss_sum, class_sum = row[0], row[1], row[2 : 2 + NCLS]

    mine = (n_own * me) // UNIT + jnp.arange(slot)
    place = (mine[:, None] == small_unit[None, :]).astype(BF16)
    small_flat = lax.dynamic_slice(
        mm(place, d_small).reshape(slot * UNIT, LANES), (shift, 0), (n_own, LANES)
    )
    reduced = (own_flat + small_flat).reshape(-1)

    grad_norm = jnp.sqrt(squares)
    clip_scale = jnp.minimum(1.0, CLIP_NORM / (grad_norm + 1e-06))
    clipped = reduced * clip_scale
    class_bias_grad = class_sum * clip_scale
    new_first = BETA_ONE * first_moment + (1.0 - BETA_ONE) * clipped
    new_second = BETA_TWO * second_moment + (1.0 - BETA_TWO) * clipped * clipped
    correct_one = 1.0 - BETA_ONE**STEP
    correct_two = 1.0 - BETA_TWO**STEP
    step_size = new_first / correct_one / (jnp.sqrt(new_second / correct_two) + EPSILON)
    new_params = params - LEARN_RATE * (step_size + WEIGHT_DECAY * params)
    return (new_params, new_first, new_second, grad_norm, loss_sum, node_total, class_bias_grad)


def solution(mesh):
    in_specs = (
        P(None, ("rows", "cols"), None),
        P(None, "rows", None, "cols", None),
        P(None, "rows", None, "cols", None),
        P(None, ("rows", "cols")),
        P(None, ("rows", "cols")),
        P(None, ("rows", "cols")),
        P(("rows", "cols")),
        P(("rows", "cols")),
        P(("rows", "cols")),
    )
    out_specs = (P(("rows", "cols")), P(("rows", "cols")), P(("rows", "cols")), P(), P(), P(), P())
    return jax.shard_map(
        per_device, mesh=mesh, in_specs=in_specs, out_specs=out_specs, check_vma=False
    )
```

profile of v0, /device:TPU:0, one launch (start us, length us, event | category | flops | bytes accessed | tf_op | source)
XLA Modules:
  0.0 389.2 jit_solution(17982034888108264437)
XLA Ops:
  1.6 3.0 collective-permute-start
  4.6 1.5 collective-permute-start.1
  7.1 4.0 %masked_tile.1 = (bf16[256,512]{1,0:T(8,128)(2,1)}, bf16[256,512]{1,0:T(8,128)(2,1)}, bf16[256,512]{1,0:T(8,128)(2,1)}, bf16[256,512]{1,0:T(8,128)(2,1)}, bf16[2...) custom-call(s32[2]{0:T(128)S(1)} %pad_add_fusion.1.refs_0_, ...), custom_call_target="tpu_custom_call" | custom-call | tf_op jit(solution)/shard_map/masked_tile/pallas_call | solution.py:127
  11.3 2.2 layer_one.1
  16.1 2.9 collective-permute-start.16
  19.0 1.6 collective-permute-start.17
  21.3 3.9 collective-permute-start.6
  25.2 8.4 %collective-permute-done.16.refs_0_ = bf16[1,72,2048]{2,1,0:T(8,128)(2,1)S(1)} collective-permute-done((bf16[1,72,2048]{2,1,0:T(8,128)(2,1)}, bf16[1,72,2048]{2,1,0:T(8,128)(2,1)S(1)}, u32[]{:S(2)}, u32[]{:S(2)}) %collective-permute-start.16) | collective-permute-done | bytes 294944 | tf_op jit(solution)/shard_map/ppermute | solution.py:38
  33.6 1.7 collective-permute-start.19
  38.8 2.8 collective-permute-start.9
  43.9 4.2 %collective-permute-done.9 = bf16[2,128,128]{2,1,0:T(8,128)(2,1)S(1)} collective-permute-done((bf16[2,128,128]{2,1,0:T(8,128)(2,1)S(1)}, bf16[2,128,128]{2,1,0:T(8,128)(2,1)S(1)}, u32[]{:S(2)}, u32[]{:S(2)}) %collective-permute-start.9) | collective-permute-done | bytes 65568 | tf_op jit(solution)/shard_map/ppermute | solution.py:38
  48.1 1.5 collective-permute-start.23
  53.4 1.6 collective-permute-start.10
  55.0 4.3 %collective-permute-done.12.refs_3_ = bf16[4,2,128,128]{3,2,1,0:T(8,128)(2,1)S(1)} collective-permute-done((bf16[4,2,128,128]{3,2,1,0:T(8,128)(2,1)S(1)}, bf16[4,2,128,128]{3,2,1,0:T(8,128)(2,1)S(1)}, u32[]{:S(2)}, u32[]{:S(2)}) %collective-permute-start.12) | collective-permute-done | bytes 262176 | tf_op jit(solution)/shard_map/ppermute | solution.py:38
  60.7 12.0 %collective-permute-done.11.refs_2_ = bf16[4,2,128,128]{3,2,1,0:T(8,128)(2,1)S(1)} collective-permute-done((bf16[4,2,128,128]{3,2,1,0:T(8,128)(2,1)S(1)}, bf16[4,2,128,128]{3,2,1,0:T(8,128)(2,1)S(1)}, u32[]{:S(2)}, u32[]{:S(2)}) %collective-permute-start.11) | collective-permute-done | bytes 262176 | tf_op jit(solution)/shard_map/ppermute | solution.py:38
  73.9 2.5 collective-permute-start.15
  76.4 1.5 collective-permute-start.22
  77.9 1.9 collective-permute-start.13
  79.8 1.7 copy.105.refs_0_
  81.5 1.7 copy.107.refs_0_
  88.2 2.6 collective-permute-done.14.refs_6_.refs_2_
  90.8 2.0 collective-permute-start.25
  92.9 3.0 collective-permute-done.13.refs_5_.refs_1_
  100.9 5.7 %collective-permute-done.27 = bf16[1,72,2048]{2,1,0:T(8,128)(2,1)} collective-permute-done((bf16[1,72,2048]{2,1,0:T(8,128)(2,1)}, bf16[1,72,2048]{2,1,0:T(8,128)(2,1)}, u32[]{:S(2)}, u32[]{:S(2)}) %collective-permute-start.27) | collective-permute-done | bytes 294944 | tf_op jit(solution)/shard_map/ppermute | solution.py:38
  106.6 1.6 collective-permute-done.26
  109.0 4.6 %join.3.wn_ref.refs_3_ = bf16[1152,2048]{1,0:T(8,128)(2,1)} custom-call(bf16[72,2048]{1,0:T(8,128)(2,1)} %bitcast.187, bf16[144,2048]{1,0:T(8,128)(2,1)} %bitcast.168, bf16[72,2048]{1,0:T(8,128)(2,1)} %bitcast.192, bf16[72,2048]{1,0:T(8,128)(2,1)} %bitcast.26.refs_3_, bf16[144,2048]{1,0:T(8,128)(2,1)} %bitcast.27.refs_4_, bf16[72,2048]{1,0:T(8,128)(2,1)} %bitcast.28.refs_5_, ...), custom_call_target="tpu_custom_call" | custom-call | tf_op jit(solution)/shard_map/join/pallas_call | solution.py:127
  114.1 3.4 convolution_convert_fusion
  118.1 2.7 collective-permute-start.31
  126.0 14.6 %forward_two.2 = (f32[128,2048]{1,0:T(8,128)}, bf16[128,2048]{1,0:T(8,128)(2,1)}, bf16[2048,2048]{1,0:T(8,128)(2,1)}) custom-call(bf16[4,2,128,128]{3,2,1,0:T(8,128)(2,1)} %copy-done.4, bf16[4,2,128,128]{3,2,1,0:T(8,128)(2,1)} %copy-done.15, bf16[4,2,128,128]{3,2,1,0:T(8,128)(2,1)} %copy-done.14, bf16[4,2,128,128]{3,2,1,0:T(8,128)(2,1)} %copy-done.13, ...), custom_call_target="tpu_custom_call" | custom-call | tf_op jit(solution)/shard_map/forward_two/pallas_call | solution.py:127
  141.2 3.1 collective-permute-done.29.refs_5_.refs_9_
  145.0 14.4 %forward_two.3 = (f32[128,2048]{1,0:T(8,128)}, bf16[128,2048]{1,0:T(8,128)(2,1)}, bf16[2048,2048]{1,0:T(8,128)(2,1)}) custom-call(bf16[4,2,128,128]{3,2,1,0:T(8,128)(2,1)} %copy-done.4, bf16[4,2,128,128]{3,2,1,0:T(8,128)(2,1)} %copy-done.15, bf16[4,2,128,128]{3,2,1,0:T(8,128)(2,1)} %copy-done.14, bf16[4,2,128,128]{3,2,1,0:T(8,128)(2,1)} %copy-done.13, ...), custom_call_target="tpu_custom_call" | custom-call | tf_op jit(solution)/shard_map/forward_two/pallas_call | solution.py:127
  162.9 8.6 %spread_two.1 = (bf16[256,1152]{1,0:T(8,128)(2,1)}, bf16[256,1152]{1,0:T(8,128)(2,1)}) custom-call(f32[128,2048]{1,0:T(8,128)} %get-tuple-element.67.refs_0_, f32[128,2048]{1,0:T(8,128)} %get-tuple-element.71.refs_1_, bf16[128,2048]{1,0:T(8,128)(2,1)} %copy-done.37, bf16[128,2048]{1,0:T(8,128)(2,1)} %copy-done.36, bf16[256,128]{1,0:T(8,128)(2,1)S(1)} %bitcast.177, ...), custom_call_target="tpu_custom_call" | custom-call | tf_op jit(solution)/shard_map/spread_two/pallas_call | solution.py:127
  172.2 9.0 %layer_two.1 = (f32[256,2048]{1,0:T(8,128)}, bf16[256,2048]{1,0:T(8,128)(2,1)}, bf16[128,128]{1,0:T(8,128)(2,1)S(1)}) custom-call(bf16[256,1152]{1,0:T(8,128)(2,1)} %get-tuple-element.74.gn_ref.refs_0_, bf16[256,1152]{1,0:T(8,128)(2,1)} %get-tuple-element.75.gf_ref.refs_9_, bf16[1152,2048]{1,0:T(8,128)(2,1)} %join.3.wn_ref.refs_3_, ...), custom_call_target="tpu_custom_call" | custom-call | tf_op jit(solution)/shard_map/layer_two/pallas_call | solution.py:127
  181.6 2.8 collective-permute-start.36
  186.6 3.5 collective-permute-done.37
  191.6 2.1 collective-permute-start.40
  193.7 1.7 collective-permute-done.38.refs_9_
  198.2 2.3 logits_parts.1
  203.7 1.8 collective-permute-start.44
  205.5 2.6 collective-permute-start.45
  209.5 2.1 collective-permute-done.45.refs_11_
  211.6 2.3 d_q_parts.1
  213.8 2.6 collective-permute-start.46
  218.7 2.1 collective-permute-done.47.refs_2_
  220.8 1.9 collective-permute-done.48.refs_3_
  222.7 5.3 %d_two.2 = (bf16[256,1024]{1,0:T(8,128)(2,1)}, f32[8,1024]{1,0:T(8,128)S(1)}, f32[1024,128]{1,0:T(8,128)}, bf16[1152,1024]{1,0:T(8,128)(2,1)}) custom-call(f32[128,128]{1,0:T(8,128)S(1)} %get-tuple-element.80.refs_0_, f32[128,128]{1,0:T(8,128)S(1)} %collective-permute-done.46.refs_1_, f32[128,128]{1,0:T(8,128)S(1)} %collective-permute-done.47.refs_2_, ...), custom_call_target="tpu_custom_call" | custom-call | tf_op jit(solution)/shard_map/d_two/pallas_call | solution.py:127
  230.0 5.2 %d_two.3 = (bf16[256,1024]{1,0:T(8,128)(2,1)}, f32[8,1024]{1,0:T(8,128)S(1)}, f32[1024,128]{1,0:T(8,128)}, bf16[1152,1024]{1,0:T(8,128)(2,1)}) custom-call(f32[128,128]{1,0:T(8,128)S(1)} %get-tuple-element.80.refs_0_, f32[128,128]{1,0:T(8,128)S(1)} %collective-permute-done.46.refs_1_, f32[128,128]{1,0:T(8,128)S(1)} %collective-permute-done.47.refs_2_, ...), custom_call_target="tpu_custom_call" | custom-call | tf_op jit(solution)/shard_map/d_two/pallas_call | solution.py:127
  236.6 5.2 %near_part.2 = (f32[576,1024]{1,0:T(8,128)}, bf16[576,1024]{1,0:T(8,128)(2,1)}) custom-call(bf16[256,1152]{1,0:T(8,128)(2,1)} %get-tuple-element.74.gn_ref.refs_0_, bf16[256,1024]{1,0:T(8,128)(2,1)} %get-tuple-element.86.refs_1_.refs_0_, bf16[1152,1024]{1,0:T(8,128)(2,1)} %collective-permute-done.49.refs_2_), custom_call_target="tpu_custom_call" | custom-call | tf_op jit(solution)/shard_map/near_part/pallas_call | solution.py:127
  242.4 5.3 %near_part.3 = (f32[576,1024]{1,0:T(8,128)}, bf16[576,1024]{1,0:T(8,128)(2,1)}) custom-call(bf16[256,1152]{1,0:T(8,128)(2,1)} %get-tuple-element.74.gn_ref.refs_0_, bf16[256,1024]{1,0:T(8,128)(2,1)} %get-tuple-element.90.refs_1_, bf16[1152,1024]{1,0:T(8,128)(2,1)} %collective-permute-done.52.refs_2_), custom_call_target="tpu_custom_call" | custom-call | tf_op jit(solution)/shard_map/near_part/pallas_call | solution.py:127
  252.3 12.3 %d_g_two.1 = bf16[256,2048]{1,0:T(8,128)(2,1)} custom-call(bf16[256,1024]{1,0:T(8,128)(2,1)} %after.35.refs_0_, bf16[256,1024]{1,0:T(8,128)(2,1)} %get-tuple-element.90.refs_1_, s32[2304,1]{1,0:T(8,128)S(1)} %broadcast_add_fusion.refs_2_, bf16[1152,2048]{1,0:T(8,128)(2,1)} %join.3.wn_ref.refs_3_, bf16[1152,2048]{1,0:T(8,128)(2,1)} %collective-permute-done.34.wf_ref.refs_4_), custom_call_target="tpu_custom_call" | custom-call | tf_op jit(solution)/shard_map/d_g_two/pallas_call | solution.py:127
  264.5 5.4 %collective-permute-done.50 = bf16[2,4,72,1024]{3,2,1,0:T(8,128)(2,1)} collective-permute-done((bf16[2,4,72,1024]{3,2,1,0:T(8,128)(2,1)}, bf16[2,4,72,1024]{3,2,1,0:T(8,128)(2,1)}, u32[]{:S(2)}, u32[]{:S(2)}) %collective-permute-start.50) | collective-permute-done | bytes 1179680 | tf_op jit(solution)/shard_map/ppermute | solution.py:38
  270.0 2.0 add_bitcast_fusion.1
  273.1 3.6 collective-permute-done.53
  277.3 2.0 collective-permute-start.54
  281.6 8.1 %backward_one.3 = bf16[128,768]{1,0:T(8,128)(2,1)} custom-call(bf16[4,2,128,128]{3,2,1,0:T(8,128)(2,1)} %copy-done.4, bf16[4,2,128,128]{3,2,1,0:T(8,128)(2,1)} %copy-done.15, bf16[4,2,128,128]{3,2,1,0:T(8,128)(2,1)} %copy-done.14, bf16[4,2,128,128]{3,2,1,0:T(8,128)(2,1)} %copy-done.13, bf16[256,512]{1,0:T(8,128)(2,1)} %get-tuple-element.54.refs_0_.refs_4_, ...), custom_call_target="tpu_custom_call" | custom-call | tf_op jit(solution)/shard_map/backward_one/pallas_call | solution.py:127
  294.1 7.8 %backward_one.4 = bf16[128,768]{1,0:T(8,128)(2,1)} custom-call(bf16[4,2,128,128]{3,2,1,0:T(8,128)(2,1)} %copy-done.4, bf16[4,2,128,128]{3,2,1,0:T(8,128)(2,1)} %copy-done.15, bf16[4,2,128,128]{3,2,1,0:T(8,128)(2,1)} %copy-done.14, bf16[4,2,128,128]{3,2,1,0:T(8,128)(2,1)} %copy-done.13, bf16[256,512]{1,0:T(8,128)(2,1)} %get-tuple-element.54.refs_0_.refs_4_, ...), custom_call_target="tpu_custom_call" | custom-call | tf_op jit(solution)/shard_map/backward_one/pallas_call | solution.py:127
  302.0 4.2 %collective-permute-done.55 = bf16[1,2,72,2048]{3,2,1,0:T(8,128)(2,1)S(1)} collective-permute-done((bf16[1,2,72,2048]{3,2,1,0:T(8,128)(2,1)S(1)}, bf16[1,2,72,2048]{3,2,1,0:T(8,128)(2,1)S(1)}, u32[]{:S(2)}, u32[]{:S(2)}) %collective-permute-start.55) | collective-permute-done | bytes 589856 | tf_op jit(solution)/shard_map/ppermute | solution.py:38
  306.9 6.1 %backward_one.5 = bf16[128,512]{1,0:T(8,128)(2,1)} custom-call(bf16[4,2,128,128]{3,2,1,0:T(8,128)(2,1)} %copy-done.4, bf16[4,2,128,128]{3,2,1,0:T(8,128)(2,1)} %copy-done.15, bf16[4,2,128,128]{3,2,1,0:T(8,128)(2,1)} %copy-done.14, bf16[4,2,128,128]{3,2,1,0:T(8,128)(2,1)} %copy-done.13, bf16[256,512]{1,0:T(8,128)(2,1)} %get-tuple-element.54.refs_0_.refs_4_, ...), custom_call_target="tpu_custom_call" | custom-call | tf_op jit(solution)/shard_map/backward_one/pallas_call | solution.py:127
  317.4 4.1 %all-to-all-start = ((bf16[32,80,128]{2,1,0:T(8,128)(2,1)}), bf16[32,80,128]{2,1,0:T(8,128)(2,1)S(1)}, u32[]{:S(2)}, u32[]{:S(2)}) async-start(bf16[32,80,128]{2,1,0:T(8,128)(2,1)} %after.39), calls=%async_computation | async-start | bytes 1310720 | tf_op jit(solution)/shard_map/all_to_all | solution.py:872
  321.5 2.7 collective-permute-start.56
  324.7 27.2 %collective-permute-done.56 = bf16[1,1,72,2048]{3,2,1,0:T(8,128)(2,1)S(1)} collective-permute-done((bf16[1,1,72,2048]{3,2,1,0:T(8,128)(2,1)S(1)}, bf16[1,1,72,2048]{3,2,1,0:T(8,128)(2,1)S(1)}, u32[]{:S(2)}, u32[]{:S(2)}) %collective-permute-start.56) | collective-permute-done | bytes 294944 | tf_op jit(solution)/shard_map/ppermute | solution.py:38
  356.6 3.6 all-to-all-start.1
  360.3 21.9 %all-to-all-done.1 = bf16[32,96,128]{2,1,0:T(8,128)(2,1)S(1)} async-done(((bf16[32,96,128]{2,1,0:T(8,128)(2,1)}), bf16[32,96,128]{2,1,0:T(8,128)(2,1)S(1)}, u32[]{:S(2)}, u32[]{:S(2)}) %all-to-all-start.1) | async-done | bytes 786464 | tf_op jit(solution)/shard_map/all_to_all | solution.py:881
  385.4 2.6 multiply_subtract_fusion
  (322 shorter events, 81.5 us)
Async XLA Ops:
  1.6 9.5 %collective-permute-start = (bf16[2,128,128]{2,1,0:T(8,128)(2,1)S(1)}, bf16[2,128,128]{2,1,0:T(8,128)(2,1)S(1)}, u32[]{:S(2)}, u32[]{:S(2)}) collective-permute-start(bf16[2,128,128]{2,1,0:T(8,128)(2,1)S(1)} %pad.9.refs_8_), channel_id=1, source_target_pairs={{0,8},{8,0},{16,24},{24,16},{1,9},{9,1},{17,25},{25,17},{2,10},{10... | collective-permute-start | bytes 196616 | tf_op jit(solution)/shard_map/ppermute | solution.py:38
  4.6 6.5 %collective-permute-start.1 = (bf16[2,128,128]{2,1,0:T(8,128)(2,1)S(1)}, bf16[2,128,128]{2,1,0:T(8,128)(2,1)S(1)}, u32[]{:S(2)}, u32[]{:S(2)}) collective-permute-start(bf16[2,128,128]{2,1,0:T(8,128)(2,1)S(1)} %pad.9.refs_8_), channel_id=1, source_target_pairs={{0,16},{8,24},{16,0},{24,8},{1,17},{9,25},{17,1},{25,9},{2,18},{10... | collective-permute-start | bytes 196616 | tf_op jit(solution)/shard_map/ppermute | solution.py:38
  6.1 5.2 %collective-permute-start.2 = (bf16[2,128,128]{2,1,0:T(8,128)(2,1)S(1)}, bf16[2,128,128]{2,1,0:T(8,128)(2,1)S(1)}, u32[]{:S(2)}, u32[]{:S(2)}) collective-permute-start(bf16[2,128,128]{2,1,0:T(8,128)(2,1)S(1)} %pad.9.refs_8_), channel_id=1, source_target_pairs={{0,24},{8,16},{16,8},{24,0},{1,25},{9,17},{17,9},{25,1},{2,26},{10... | collective-permute-start | bytes 196616 | tf_op jit(solution)/shard_map/ppermute | solution.py:38
  13.5 7.1 %collective-permute-start.3 = (f32[4,2,128,128]{3,2,1,0:T(8,128)S(1)}, f32[4,2,128,128]{3,2,1,0:T(8,128)S(1)}, u32[]{:S(2)}, u32[]{:S(2)}) collective-permute-start(f32[4,2,128,128]{3,2,1,0:T(8,128)S(1)} %get-tuple-element.63), channel_id=1, source_target_pairs={{0,1},{1,0},{2,3},{3,2},{4,5},{5,4},{6,7},{7,6},{8,9},{9,8},{10,11... | collective-permute-start | bytes 1572872 | tf_op jit(solution)/shard_map/ppermute | solution.py:38
  16.1 17.4 %collective-permute-start.16 = (bf16[1,72,2048]{2,1,0:T(8,128)(2,1)}, bf16[1,72,2048]{2,1,0:T(8,128)(2,1)S(1)}, u32[]{:S(2)}, u32[]{:S(2)}) collective-permute-start(bf16[1,72,2048]{2,1,0:T(8,128)(2,1)} %after.23.refs_0_), channel_id=1, source_target_pairs={{0,4},{1,5},{2,6},{3,7},{4,0},{5,1},{6,2},{7,3},{8,12},{9,13},{10,... | collective-permute-start | bytes 884744 | tf_op jit(solution)/shard_map/ppermute | solution.py:38
  19.0 16.4 %collective-permute-start.17 = (bf16[1,72,2048]{2,1,0:T(8,128)(2,1)}, bf16[1,72,2048]{2,1,0:T(8,128)(2,1)S(1)}, u32[]{:S(2)}, u32[]{:S(2)}) collective-permute-start(bf16[1,72,2048]{2,1,0:T(8,128)(2,1)} %after.23.refs_0_), channel_id=1, source_target_pairs={{0,2},{1,3},{2,0},{3,1},{4,6},{5,7},{6,4},{7,5},{8,10},{9,11},{10,... | collective-permute-start | bytes 884744 | tf_op jit(solution)/shard_map/ppermute | solution.py:38
  20.7 17.3 %collective-permute-start.4 = (bf16[2,128,128]{2,1,0:T(8,128)(2,1)S(1)}, bf16[2,128,128]{2,1,0:T(8,128)(2,1)S(1)}, u32[]{:S(2)}, u32[]{:S(2)}) collective-permute-start(bf16[2,128,128]{2,1,0:T(8,128)(2,1)S(1)} %get-tuple-element.112), channel_id=1, source_target_pairs={{0,4},{1,5},{2,6},{3,7},{4,0},{5,1},{6,2},{7,3},{8,12},{9,13},{10,... | collective-permute-start | bytes 196616 | tf_op jit(solution)/shard_map/ppermute | solution.py:38
  21.1 16.9 %collective-permute-start.5 = (bf16[2,128,128]{2,1,0:T(8,128)(2,1)S(1)}, bf16[2,128,128]{2,1,0:T(8,128)(2,1)S(1)}, u32[]{:S(2)}, u32[]{:S(2)}) collective-permute-start(bf16[2,128,128]{2,1,0:T(8,128)(2,1)S(1)} %get-tuple-element.114), channel_id=1, source_target_pairs={{0,2},{1,3},{2,0},{3,1},{4,6},{5,7},{6,4},{7,5},{8,10},{9,11},{10,... | collective-permute-start | bytes 196616 | tf_op jit(solution)/shard_map/ppermute | solution.py:38
  21.3 17.4 %collective-permute-start.6 = (bf16[2,128,128]{2,1,0:T(8,128)(2,1)S(1)}, bf16[2,128,128]{2,1,0:T(8,128)(2,1)S(1)}, u32[]{:S(2)}, u32[]{:S(2)}) collective-permute-start(bf16[2,128,128]{2,1,0:T(8,128)(2,1)S(1)} %get-tuple-element.113), channel_id=1, source_target_pairs={{0,6},{1,7},{2,4},{3,5},{4,2},{5,3},{6,0},{7,1},{8,14},{9,15},{10,... | collective-permute-start | bytes 196616 | tf_op jit(solution)/shard_map/ppermute | solution.py:38
  33.6 44.3 %collective-permute-start.19 = (bf16[1,72,2048]{2,1,0:T(8,128)(2,1)S(1)}, bf16[1,72,2048]{2,1,0:T(8,128)(2,1)}, u32[]{:S(2)}, u32[]{:S(2)}) collective-permute-start(bf16[1,72,2048]{2,1,0:T(8,128)(2,1)S(1)} %copy-done.22), channel_id=1, source_target_pairs={{0,8},{8,0},{16,24},{24,16},{1,9},{9,1},{17,25},{25,17},{2,10},{10... | collective-permute-start | bytes 884744 | tf_op jit(solution)/shard_map/ppermute | solution.py:38
  35.4 18.1 %collective-permute-start.18 = (bf16[1,72,2048]{2,1,0:T(8,128)(2,1)S(1)}, bf16[1,72,2048]{2,1,0:T(8,128)(2,1)S(1)}, u32[]{:S(2)}, u32[]{:S(2)}) collective-permute-start(bf16[1,72,2048]{2,1,0:T(8,128)(2,1)S(1)} %collective-permute-done.16.refs_0_), channel_id=1, source_target_pairs={{0,2},{1,3},{2,0},{3,1},{4,6},{5,7},{6,4},{7,5},{8,10},{9,11},{10,... | collective-permute-start | bytes 884744 | tf_op jit(solution)/shard_map/ppermute | solution.py:38
  38.8 9.3 %collective-permute-start.9 = (bf16[2,128,128]{2,1,0:T(8,128)(2,1)S(1)}, bf16[2,128,128]{2,1,0:T(8,128)(2,1)S(1)}, u32[]{:S(2)}, u32[]{:S(2)}) collective-permute-start(bf16[2,128,128]{2,1,0:T(8,128)(2,1)S(1)} %fusion.18), channel_id=1, source_target_pairs={{0,6},{1,7},{2,4},{3,5},{4,2},{5,3},{6,0},{7,1},{8,14},{9,15},{10,... | collective-permute-start | bytes 196616 | tf_op jit(solution)/shard_map/ppermute | solution.py:38
  41.6 8.0 %collective-permute-start.8 = (bf16[2,128,128]{2,1,0:T(8,128)(2,1)S(1)}, bf16[2,128,128]{2,1,0:T(8,128)(2,1)S(1)}, u32[]{:S(2)}, u32[]{:S(2)}) collective-permute-start(bf16[2,128,128]{2,1,0:T(8,128)(2,1)S(1)} %fusion.18), channel_id=1, source_target_pairs={{0,2},{1,3},{2,0},{3,1},{4,6},{5,7},{6,4},{7,5},{8,10},{9,11},{10,... | collective-permute-start | bytes 196616 | tf_op jit(solution)/shard_map/ppermute | solution.py:38
  42.3 7.4 %collective-permute-start.7 = (bf16[2,128,128]{2,1,0:T(8,128)(2,1)S(1)}, bf16[2,128,128]{2,1,0:T(8,128)(2,1)S(1)}, u32[]{:S(2)}, u32[]{:S(2)}) collective-permute-start(bf16[2,128,128]{2,1,0:T(8,128)(2,1)S(1)} %fusion.18), channel_id=1, source_target_pairs={{0,4},{1,5},{2,6},{3,7},{4,0},{5,1},{6,2},{7,3},{8,12},{9,13},{10,... | collective-permute-start | bytes 196616 | tf_op jit(solution)/shard_map/ppermute | solution.py:38
  48.1 35.1 %collective-permute-start.23 = (bf16[2,72,2048]{2,1,0:T(8,128)(2,1)}, bf16[2,72,2048]{2,1,0:T(8,128)(2,1)S(1)}, u32[]{:S(2)}, u32[]{:S(2)}) collective-permute-start(bf16[2,72,2048]{2,1,0:T(8,128)(2,1)} %after.25), channel_id=1, source_target_pairs={{0,16},{8,24},{16,0},{24,8},{1,17},{9,25},{17,1},{25,9},{2,18},{10... | collective-permute-start | bytes 1769480 | tf_op jit(solution)/shard_map/ppermute | solution.py:38
  49.7 33.6 %copy-start.4 = (bf16[4,2,128,128]{3,2,1,0:T(8,128)(2,1)}, bf16[4,2,128,128]{3,2,1,0:T(8,128)(2,1)S(1)}, u32[]{:S(2)}) copy-start(bf16[4,2,128,128]{3,2,1,0:T(8,128)(2,1)S(1)} %pad_maximum_fusion.3.refs_0_) | copy-start | bytes 786436
  49.7 9.7 %collective-permute-start.12 = (bf16[4,2,128,128]{3,2,1,0:T(8,128)(2,1)S(1)}, bf16[4,2,128,128]{3,2,1,0:T(8,128)(2,1)S(1)}, u32[]{:S(2)}, u32[]{:S(2)}) collective-permute-start(bf16[4,2,128,128]{3,2,1,0:T(8,128)(2,1)S(1)} %pad_maximum_fusion.3.refs_0_), channel_id=1, source_target_pairs={{0,24},{8,16},{16,8},{24,0},{1,25},{9,17},{17,9},{25,1},{2,26},{10... | collective-permute-start | bytes 786440 | tf_op jit(solution)/shard_map/ppermute | solution.py:38
  50.8 21.8 %collective-permute-start.11 = (bf16[4,2,128,128]{3,2,1,0:T(8,128)(2,1)S(1)}, bf16[4,2,128,128]{3,2,1,0:T(8,128)(2,1)S(1)}, u32[]{:S(2)}, u32[]{:S(2)}) collective-permute-start(bf16[4,2,128,128]{3,2,1,0:T(8,128)(2,1)S(1)} %pad_maximum_fusion.3.refs_0_), channel_id=1, source_target_pairs={{0,16},{8,24},{16,0},{24,8},{1,17},{9,25},{17,1},{25,9},{2,18},{10... | collective-permute-start | bytes 786440 | tf_op jit(solution)/shard_map/ppermute | solution.py:38
  53.4 19.8 %collective-permute-start.10 = (bf16[4,2,128,128]{3,2,1,0:T(8,128)(2,1)S(1)}, bf16[4,2,128,128]{3,2,1,0:T(8,128)(2,1)S(1)}, u32[]{:S(2)}, u32[]{:S(2)}) collective-permute-start(bf16[4,2,128,128]{3,2,1,0:T(8,128)(2,1)S(1)} %pad_maximum_fusion.3.refs_0_), channel_id=1, source_target_pairs={{0,8},{8,0},{16,24},{24,16},{1,9},{9,1},{17,25},{25,17},{2,10},{10... | collective-permute-start | bytes 786440 | tf_op jit(solution)/shard_map/ppermute | solution.py:38
  55.0 28.2 %copy-start.1 = (bf16[2,72,2048]{2,1,0:T(8,128)(2,1)S(1)}, bf16[2,72,2048]{2,1,0:T(8,128)(2,1)}, u32[]{:S(2)}) copy-start(bf16[2,72,2048]{2,1,0:T(8,128)(2,1)} %after.25) | copy-start | bytes 1769476
  59.3 18.6 %collective-permute-start.21 = (bf16[1,72,2048]{2,1,0:T(8,128)(2,1)}, bf16[1,72,2048]{2,1,0:T(8,128)(2,1)}, u32[]{:S(2)}, u32[]{:S(2)}) collective-permute-start(bf16[1,72,2048]{2,1,0:T(8,128)(2,1)} %after.26), channel_id=1, source_target_pairs={{0,8},{8,0},{16,24},{24,16},{1,9},{9,1},{17,25},{25,17},{2,10},{10... | collective-permute-start | bytes 884744 | tf_op jit(solution)/shard_map/ppermute | solution.py:38
  73.9 11.3 %collective-permute-start.15 = (bf16[256,512]{1,0:T(8,128)(2,1)}, bf16[256,512]{1,0:T(8,128)(2,1)S(1)}, u32[]{:S(2)}, u32[]{:S(2)}) collective-permute-start(bf16[256,512]{1,0:T(8,128)(2,1)} %after.22), channel_id=1, source_target_pairs={{0,6},{1,7},{2,4},{3,5},{4,2},{5,3},{6,0},{7,1},{8,14},{9,15},{10,... | collective-permute-start | bytes 786440 | tf_op jit(solution)/shard_map/ppermute | solution.py:38
  76.4 10.5 %collective-permute-start.22 = (bf16[1,72,2048]{2,1,0:T(8,128)(2,1)S(1)}, bf16[1,72,2048]{2,1,0:T(8,128)(2,1)}, u32[]{:S(2)}, u32[]{:S(2)}) collective-permute-start(bf16[1,72,2048]{2,1,0:T(8,128)(2,1)S(1)} %copy-done.22), channel_id=1, source_target_pairs={{0,16},{8,24},{16,0},{24,8},{1,17},{9,25},{17,1},{25,9},{2,18},{10... | collective-permute-start | bytes 884744 | tf_op jit(solution)/shard_map/ppermute | solution.py:38
  77.9 12.9 %collective-permute-start.14 = (bf16[256,512]{1,0:T(8,128)(2,1)}, bf16[256,512]{1,0:T(8,128)(2,1)S(1)}, u32[]{:S(2)}, u32[]{:S(2)}) collective-permute-start(bf16[256,512]{1,0:T(8,128)(2,1)} %after.21), channel_id=1, source_target_pairs={{0,2},{1,3},{2,0},{3,1},{4,6},{5,7},{6,4},{7,5},{8,10},{9,11},{10,... | collective-permute-start | bytes 786440 | tf_op jit(solution)/shard_map/ppermute | solution.py:38
  77.9 18.0 %collective-permute-start.13 = (bf16[256,512]{1,0:T(8,128)(2,1)}, bf16[256,512]{1,0:T(8,128)(2,1)S(1)}, u32[]{:S(2)}, u32[]{:S(2)}) collective-permute-start(bf16[256,512]{1,0:T(8,128)(2,1)} %after.20), channel_id=1, source_target_pairs={{0,4},{1,5},{2,6},{3,7},{4,0},{5,1},{6,2},{7,3},{8,12},{9,13},{10,... | collective-permute-start | bytes 786440 | tf_op jit(solution)/shard_map/ppermute | solution.py:38
  83.2 16.4 %collective-permute-start.20 = (bf16[2,72,2048]{2,1,0:T(8,128)(2,1)S(1)}, bf16[2,72,2048]{2,1,0:T(8,128)(2,1)}, u32[]{:S(2)}, u32[]{:S(2)}) collective-permute-start(bf16[2,72,2048]{2,1,0:T(8,128)(2,1)S(1)} %copy-done.1), channel_id=1, source_target_pairs={{0,8},{8,0},{16,24},{24,16},{1,9},{9,1},{17,25},{25,17},{2,10},{10... | collective-permute-start | bytes 1769480 | tf_op jit(solution)/shard_map/ppermute | solution.py:38
  85.2 28.5 %copy-start.16 = (bf16[256,512]{1,0:T(8,128)(2,1)}, bf16[256,512]{1,0:T(8,128)(2,1)S(1)}, u32[]{:S(2)}) copy-start(bf16[256,512]{1,0:T(8,128)(2,1)S(1)} %collective-permute-done.15.refs_7_.refs_3_) | copy-start | bytes 786436
  85.2 23.0 %collective-permute-start.26 = (bf16[2,72,2048]{2,1,0:T(8,128)(2,1)}, bf16[2,72,2048]{2,1,0:T(8,128)(2,1)S(1)}, u32[]{:S(2)}, u32[]{:S(2)}) collective-permute-start(bf16[2,72,2048]{2,1,0:T(8,128)(2,1)} %after.28), channel_id=1, source_target_pairs={{0,8},{8,0},{16,24},{24,16},{1,9},{9,1},{17,25},{25,17},{2,10},{10... | collective-permute-start | bytes 1769480 | tf_op jit(solution)/shard_map/ppermute | solution.py:38
  86.8 11.6 %collective-permute-start.24 = (bf16[1,72,2048]{2,1,0:T(8,128)(2,1)}, bf16[1,72,2048]{2,1,0:T(8,128)(2,1)S(1)}, u32[]{:S(2)}, u32[]{:S(2)}) collective-permute-start(bf16[1,72,2048]{2,1,0:T(8,128)(2,1)} %after.26), channel_id=1, source_target_pairs={{0,16},{8,24},{16,0},{24,8},{1,17},{9,25},{17,1},{25,9},{2,18},{10... | collective-permute-start | bytes 884744 | tf_op jit(solution)/shard_map/ppermute | solution.py:38
  90.8 10.1 %collective-permute-start.25 = (bf16[1,72,2048]{2,1,0:T(8,128)(2,1)}, bf16[1,72,2048]{2,1,0:T(8,128)(2,1)S(1)}, u32[]{:S(2)}, u32[]{:S(2)}) collective-permute-start(bf16[1,72,2048]{2,1,0:T(8,128)(2,1)} %after.27), channel_id=1, source_target_pairs={{0,16},{8,24},{16,0},{24,8},{1,17},{9,25},{17,1},{25,9},{2,18},{10... | collective-permute-start | bytes 884744 | tf_op jit(solution)/shard_map/ppermute | solution.py:38
  95.9 10.7 %collective-permute-start.27 = (bf16[1,72,2048]{2,1,0:T(8,128)(2,1)}, bf16[1,72,2048]{2,1,0:T(8,128)(2,1)}, u32[]{:S(2)}, u32[]{:S(2)}) collective-permute-start(bf16[1,72,2048]{2,1,0:T(8,128)(2,1)} %after.29), channel_id=1, source_target_pairs={{0,16},{8,24},{16,0},{24,8},{1,17},{9,25},{17,1},{25,9},{2,18},{10... | collective-permute-start | bytes 884744 | tf_op jit(solution)/shard_map/ppermute | solution.py:38
  113.7 57.9 %collective-permute-start.34 = (bf16[1152,2048]{1,0:T(8,128)(2,1)}, bf16[1152,2048]{1,0:T(8,128)(2,1)}, u32[]{:S(2)}, u32[]{:S(2)}) collective-permute-start(bf16[1152,2048]{1,0:T(8,128)(2,1)} %join.3.wn_ref.refs_3_), channel_id=1, source_target_pairs={{0,1},{1,0},{2,3},{3,2},{4,5},{5,4},{6,7},{7,6},{8,9},{9,8},{10,11... | collective-permute-start | bytes 14155784 | tf_op jit(solution)/shard_map/ppermute | solution.py:38
  117.5 5.1 %collective-permute-start.28 = (bf16[160,2048]{1,0:T(8,128)(2,1)S(1)}, bf16[160,2048]{1,0:T(8,128)(2,1)S(1)}, u32[]{:S(2)}, u32[]{:S(2)}) collective-permute-start(bf16[160,2048]{1,0:T(8,128)(2,1)S(1)} %convolution_convert_fusion), channel_id=1, source_target_pairs={{0,1},{1,0},{2,3},{3,2},{4,5},{5,4},{6,7},{7,6},{8,9},{9,8},{10,11... | collective-permute-start | bytes 1966088 | tf_op jit(solution)/shard_map/ppermute | solution.py:38
  118.1 23.1 %collective-permute-start.31 = (bf16[256,512]{1,0:T(8,128)(2,1)}, bf16[256,512]{1,0:T(8,128)(2,1)S(1)}, u32[]{:S(2)}, u32[]{:S(2)}) collective-permute-start(bf16[256,512]{1,0:T(8,128)(2,1)} %after.32), channel_id=1, source_target_pairs={{0,6},{1,7},{2,4},{3,5},{4,2},{5,3},{6,0},{7,1},{8,14},{9,15},{10,... | collective-permute-start | bytes 786440 | tf_op jit(solution)/shard_map/ppermute | solution.py:38
  120.8 20.4 %collective-permute-start.30 = (bf16[256,512]{1,0:T(8,128)(2,1)}, bf16[256,512]{1,0:T(8,128)(2,1)S(1)}, u32[]{:S(2)}, u32[]{:S(2)}) collective-permute-start(bf16[256,512]{1,0:T(8,128)(2,1)} %after.31), channel_id=1, source_target_pairs={{0,2},{1,3},{2,0},{3,1},{4,6},{5,7},{6,4},{7,5},{8,10},{9,11},{10,... | collective-permute-start | bytes 786440 | tf_op jit(solution)/shard_map/ppermute | solution.py:38
  121.3 23.0 %collective-permute-start.29 = (bf16[256,512]{1,0:T(8,128)(2,1)}, bf16[256,512]{1,0:T(8,128)(2,1)S(1)}, u32[]{:S(2)}, u32[]{:S(2)}) collective-permute-start(bf16[256,512]{1,0:T(8,128)(2,1)} %after.30), channel_id=1, source_target_pairs={{0,4},{1,5},{2,6},{3,7},{4,0},{5,1},{6,2},{7,3},{8,12},{9,13},{10,... | collective-permute-start | bytes 786440 | tf_op jit(solution)/shard_map/ppermute | solution.py:38
  125.9 33.5 %copy-start.6 = (bf16[2048,128]{1,0:T(8,128)(2,1)}, bf16[2048,128]{1,0:T(8,128)(2,1)S(1)}, u32[]{:S(2)}) copy-start(bf16[2048,128]{1,0:T(8,128)(2,1)S(1)} %pad_maximum_fusion.1.w3_ref.refs_8_) | copy-start | bytes 1572868
  159.4 2.2 collective-permute-start.33
  159.5 2.6 collective-permute-start.32
  181.2 5.0 %collective-permute-start.35 = (bf16[128,128]{1,0:T(8,128)(2,1)S(1)}, bf16[128,128]{1,0:T(8,128)(2,1)S(1)}, u32[]{:S(2)}, u32[]{:S(2)}) collective-permute-start(bf16[128,128]{1,0:T(8,128)(2,1)S(1)} %get-tuple-element.76.q_ref), channel_id=1, source_target_pairs={{0,4},{1,5},{2,6},{3,7},{4,0},{5,1},{6,2},{7,3},{8,12},{9,13},{10,... | collective-permute-start | bytes 98312 | tf_op jit(solution)/shard_map/ppermute | solution.py:38
  181.6 5.0 %collective-permute-start.36 = (bf16[128,128]{1,0:T(8,128)(2,1)S(1)}, bf16[128,128]{1,0:T(8,128)(2,1)S(1)}, u32[]{:S(2)}, u32[]{:S(2)}) collective-permute-start(bf16[128,128]{1,0:T(8,128)(2,1)S(1)} %get-tuple-element.76.q_ref), channel_id=1, source_target_pairs={{0,2},{1,3},{2,0},{3,1},{4,6},{5,7},{6,4},{7,5},{8,10},{9,11},{10,... | collective-permute-start | bytes 98312 | tf_op jit(solution)/shard_map/ppermute | solution.py:38
  184.4 5.7 %collective-permute-start.37 = (bf16[128,128]{1,0:T(8,128)(2,1)S(1)}, bf16[128,128]{1,0:T(8,128)(2,1)S(1)}, u32[]{:S(2)}, u32[]{:S(2)}) collective-permute-start(bf16[128,128]{1,0:T(8,128)(2,1)S(1)} %get-tuple-element.76.q_ref), channel_id=1, source_target_pairs={{0,6},{1,7},{2,4},{3,5},{4,2},{5,3},{6,0},{7,1},{8,14},{9,15},{10,... | collective-permute-start | bytes 98312 | tf_op jit(solution)/shard_map/ppermute | solution.py:38
  190.1 5.3 %collective-permute-start.38 = (bf16[4,128,128]{2,1,0:T(8,128)(2,1)S(1)}, bf16[4,128,128]{2,1,0:T(8,128)(2,1)S(1)}, u32[]{:S(2)}, u32[]{:S(2)}) collective-permute-start(bf16[4,128,128]{2,1,0:T(8,128)(2,1)S(1)} %pad_maximum_fusion.4.refs_8_), channel_id=1, source_target_pairs={{0,8},{8,0},{16,24},{24,16},{1,9},{9,1},{17,25},{25,17},{2,10},{10... | collective-permute-start | bytes 393224 | tf_op jit(solution)/shard_map/ppermute | solution.py:38
  190.6 5.6 %collective-permute-start.39 = (bf16[4,128,128]{2,1,0:T(8,128)(2,1)S(1)}, bf16[4,128,128]{2,1,0:T(8,128)(2,1)S(1)}, u32[]{:S(2)}, u32[]{:S(2)}) collective-permute-start(bf16[4,128,128]{2,1,0:T(8,128)(2,1)S(1)} %pad_maximum_fusion.4.refs_8_), channel_id=1, source_target_pairs={{0,16},{8,24},{16,0},{24,8},{1,17},{9,25},{17,1},{25,9},{2,18},{10... | collective-permute-start | bytes 393224 | tf_op jit(solution)/shard_map/ppermute | solution.py:38
  191.6 6.0 %collective-permute-start.40 = (bf16[4,128,128]{2,1,0:T(8,128)(2,1)S(1)}, bf16[4,128,128]{2,1,0:T(8,128)(2,1)S(1)}, u32[]{:S(2)}, u32[]{:S(2)}) collective-permute-start(bf16[4,128,128]{2,1,0:T(8,128)(2,1)S(1)} %pad_maximum_fusion.4.refs_8_), channel_id=1, source_target_pairs={{0,24},{8,16},{16,8},{24,0},{1,25},{9,17},{17,9},{25,1},{2,26},{10... | collective-permute-start | bytes 393224 | tf_op jit(solution)/shard_map/ppermute | solution.py:38
  200.6 1.3 collective-permute-start.41
  202.4 1.2 collective-permute-start.42
  203.6 5.8 %collective-permute-start.43 = (bf16[2,128,128]{2,1,0:T(8,128)(2,1)S(1)}, bf16[2,128,128]{2,1,0:T(8,128)(2,1)S(1)}, u32[]{:S(2)}, u32[]{:S(2)}) collective-permute-start(bf16[2,128,128]{2,1,0:T(8,128)(2,1)S(1)} %pad_maximum_fusion.5.refs_8_), channel_id=1, source_target_pairs={{0,4},{1,5},{2,6},{3,7},{4,0},{5,1},{6,2},{7,3},{8,12},{9,13},{10,... | collective-permute-start | bytes 196616 | tf_op jit(solution)/shard_map/ppermute | solution.py:38
  203.7 5.8 %collective-permute-start.44 = (bf16[2,128,128]{2,1,0:T(8,128)(2,1)S(1)}, bf16[2,128,128]{2,1,0:T(8,128)(2,1)S(1)}, u32[]{:S(2)}, u32[]{:S(2)}) collective-permute-start(bf16[2,128,128]{2,1,0:T(8,128)(2,1)S(1)} %pad_maximum_fusion.5.refs_8_), channel_id=1, source_target_pairs={{0,2},{1,3},{2,0},{3,1},{4,6},{5,7},{6,4},{7,5},{8,10},{9,11},{10,... | collective-permute-start | bytes 196616 | tf_op jit(solution)/shard_map/ppermute | solution.py:38
  205.5 6.1 %collective-permute-start.45 = (bf16[2,128,128]{2,1,0:T(8,128)(2,1)S(1)}, bf16[2,128,128]{2,1,0:T(8,128)(2,1)S(1)}, u32[]{:S(2)}, u32[]{:S(2)}) collective-permute-start(bf16[2,128,128]{2,1,0:T(8,128)(2,1)S(1)} %pad_maximum_fusion.5.refs_8_), channel_id=1, source_target_pairs={{0,6},{1,7},{2,4},{3,5},{4,2},{5,3},{6,0},{7,1},{8,14},{9,15},{10,... | collective-permute-start | bytes 196616 | tf_op jit(solution)/shard_map/ppermute | solution.py:38
  213.8 4.9 %collective-permute-start.46 = (f32[128,128]{1,0:T(8,128)S(1)}, f32[128,128]{1,0:T(8,128)S(1)}, u32[]{:S(2)}, u32[]{:S(2)}) collective-permute-start(f32[128,128]{1,0:T(8,128)S(1)} %get-tuple-element.81), channel_id=1, source_target_pairs={{0,8},{8,0},{16,24},{24,16},{1,9},{9,1},{17,25},{25,17},{2,10},{10... | collective-permute-start | bytes 196616 | tf_op jit(solution)/shard_map/ppermute | solution.py:38
  216.5 4.3 %collective-permute-start.47 = (f32[128,128]{1,0:T(8,128)S(1)}, f32[128,128]{1,0:T(8,128)S(1)}, u32[]{:S(2)}, u32[]{:S(2)}) collective-permute-start(f32[128,128]{1,0:T(8,128)S(1)} %get-tuple-element.82), channel_id=1, source_target_pairs={{0,16},{8,24},{16,0},{24,8},{1,17},{9,25},{17,1},{25,9},{2,18},{10... | collective-permute-start | bytes 196616 | tf_op jit(solution)/shard_map/ppermute | solution.py:38
  217.5 5.2 %collective-permute-start.48 = (f32[128,128]{1,0:T(8,128)S(1)}, f32[128,128]{1,0:T(8,128)S(1)}, u32[]{:S(2)}, u32[]{:S(2)}) collective-permute-start(f32[128,128]{1,0:T(8,128)S(1)} %get-tuple-element.83), channel_id=1, source_target_pairs={{0,24},{8,16},{16,8},{24,0},{1,25},{9,17},{17,9},{25,1},{2,26},{10... | collective-permute-start | bytes 196616 | tf_op jit(solution)/shard_map/ppermute | solution.py:38
  227.9 8.6 %collective-permute-start.49 = (bf16[1152,1024]{1,0:T(8,128)(2,1)}, bf16[1152,1024]{1,0:T(8,128)(2,1)}, u32[]{:S(2)}, u32[]{:S(2)}) collective-permute-start(bf16[1152,1024]{1,0:T(8,128)(2,1)} %get-tuple-element.87), channel_id=1, source_target_pairs={{0,1},{1,0},{2,3},{3,2},{4,5},{5,4},{6,7},{7,6},{8,9},{9,8},{10,11... | collective-permute-start | bytes 7077896 | tf_op jit(solution)/shard_map/ppermute | solution.py:38
  235.2 7.1 %collective-permute-start.52 = (bf16[1152,1024]{1,0:T(8,128)(2,1)}, bf16[1152,1024]{1,0:T(8,128)(2,1)}, u32[]{:S(2)}, u32[]{:S(2)}) collective-permute-start(bf16[1152,1024]{1,0:T(8,128)(2,1)} %get-tuple-element.91), channel_id=1, source_target_pairs={{0,1},{1,0},{2,3},{3,2},{4,5},{5,4},{6,7},{7,6},{8,9},{9,8},{10,11... | collective-permute-start | bytes 7077896 | tf_op jit(solution)/shard_map/ppermute | solution.py:38
  241.8 28.2 %collective-permute-start.50 = (bf16[2,4,72,1024]{3,2,1,0:T(8,128)(2,1)}, bf16[2,4,72,1024]{3,2,1,0:T(8,128)(2,1)}, u32[]{:S(2)}, u32[]{:S(2)}) collective-permute-start(bf16[2,4,72,1024]{3,2,1,0:T(8,128)(2,1)} %bitcast.203), channel_id=1, source_target_pairs={{0,8},{8,0},{16,24},{24,16},{1,9},{9,1},{17,25},{25,17},{2,10},{10... | collective-permute-start | bytes 3538952 | tf_op jit(solution)/shard_map/ppermute | solution.py:38
  247.6 29.1 %collective-permute-start.53 = (bf16[2,4,72,1024]{3,2,1,0:T(8,128)(2,1)}, bf16[2,4,72,1024]{3,2,1,0:T(8,128)(2,1)S(1)}, u32[]{:S(2)}, u32[]{:S(2)}) collective-permute-start(bf16[2,4,72,1024]{3,2,1,0:T(8,128)(2,1)} %bitcast.204), channel_id=1, source_target_pairs={{0,16},{8,24},{16,0},{24,8},{1,17},{9,25},{17,1},{25,9},{2,18},{10... | collective-permute-start | bytes 3538952 | tf_op jit(solution)/shard_map/ppermute | solution.py:38
  264.5 16.1 %collective-permute-start.57 = (bf16[2,128,2048]{2,1,0:T(8,128)(2,1)}, bf16[2,128,2048]{2,1,0:T(8,128)(2,1)S(1)}, u32[]{:S(2)}, u32[]{:S(2)}) collective-permute-start(bf16[2,128,2048]{2,1,0:T(8,128)(2,1)} %bitcast.181), channel_id=1, source_target_pairs={{0,1},{1,0},{2,3},{3,2},{4,5},{5,4},{6,7},{7,6},{8,9},{9,8},{10,11... | collective-permute-start | bytes 3145736 | tf_op jit(solution)/shard_map/ppermute | solution.py:38
  272.1 17.6 %collective-permute-start.51 = (bf16[1,4,72,1024]{3,2,1,0:T(8,128)(2,1)S(1)}, bf16[1,4,72,1024]{3,2,1,0:T(8,128)(2,1)}, u32[]{:S(2)}, u32[]{:S(2)}) collective-permute-start(bf16[1,4,72,1024]{3,2,1,0:T(8,128)(2,1)S(1)} %fusion.5), channel_id=1, source_target_pairs={{0,16},{8,24},{16,0},{24,8},{1,17},{9,25},{17,1},{25,9},{2,18},{10... | collective-permute-start | bytes 1769480 | tf_op jit(solution)/shard_map/ppermute | solution.py:38
  277.3 13.7 %collective-permute-start.54 = (bf16[1,4,72,1024]{3,2,1,0:T(8,128)(2,1)S(1)}, bf16[1,4,72,1024]{3,2,1,0:T(8,128)(2,1)S(1)}, u32[]{:S(2)}, u32[]{:S(2)}) collective-permute-start(bf16[1,4,72,1024]{3,2,1,0:T(8,128)(2,1)S(1)} %fusion.6), channel_id=1, source_target_pairs={{0,8},{8,0},{16,24},{24,16},{1,9},{9,1},{17,25},{25,17},{2,10},{10... | collective-permute-start | bytes 1769480 | tf_op jit(solution)/shard_map/ppermute | solution.py:38
  293.4 12.7 %collective-permute-start.55 = (bf16[1,2,72,2048]{3,2,1,0:T(8,128)(2,1)S(1)}, bf16[1,2,72,2048]{3,2,1,0:T(8,128)(2,1)S(1)}, u32[]{:S(2)}, u32[]{:S(2)}) collective-permute-start(bf16[1,2,72,2048]{3,2,1,0:T(8,128)(2,1)S(1)} %fusion.7), channel_id=1, source_target_pairs={{0,2},{1,3},{2,0},{3,1},{4,6},{5,7},{6,4},{7,5},{8,10},{9,11},{10,... | collective-permute-start | bytes 1769480 | tf_op jit(solution)/shard_map/ppermute | solution.py:38
  317.4 35.5 %all-to-all-start = ((bf16[32,80,128]{2,1,0:T(8,128)(2,1)}), bf16[32,80,128]{2,1,0:T(8,128)(2,1)S(1)}, u32[]{:S(2)}, u32[]{:S(2)}) async-start(bf16[32,80,128]{2,1,0:T(8,128)(2,1)} %after.39), calls=%async_computation | async-start | bytes 1310720 | tf_op jit(solution)/shard_map/all_to_all | solution.py:872
  321.5 30.4 %collective-permute-start.56 = (bf16[1,1,72,2048]{3,2,1,0:T(8,128)(2,1)S(1)}, bf16[1,1,72,2048]{3,2,1,0:T(8,128)(2,1)S(1)}, u32[]{:S(2)}, u32[]{:S(2)}) collective-permute-start(bf16[1,1,72,2048]{3,2,1,0:T(8,128)(2,1)S(1)} %get-tuple-element.109), channel_id=1, source_target_pairs={{0,4},{1,5},{2,6},{3,7},{4,0},{5,1},{6,2},{7,3},{8,12},{9,13},{10,... | collective-permute-start | bytes 884744 | tf_op jit(solution)/shard_map/ppermute | solution.py:38
  356.6 25.6 %all-to-all-start.1 = ((bf16[32,96,128]{2,1,0:T(8,128)(2,1)}), bf16[32,96,128]{2,1,0:T(8,128)(2,1)S(1)}, u32[]{:S(2)}, u32[]{:S(2)}) async-start(bf16[32,96,128]{2,1,0:T(8,128)(2,1)} %broadcast_in_dim.74), calls=%async_computation.1 | async-start | bytes 1572864 | tf_op jit(solution)/shard_map/all_to_all | solution.py:881
  (47 other events, 376.1 us)
where the time goes:
time: 391 us; the launch traced here: 389 us
  waiting for transfers between devices  131 us (34%)
  Pallas kernels  119 us (30%)
  starting transfers between devices  76.3 us (20%)
  other arithmetic  28 us (7%)
  local copies, waits for them, and re-layouts  26.9 us (7%)
  between operations  4.79 us (1%)
    pallas_call x20, Pallas kernels, run(): pl.pallas_call(kernel, out_shape=tuple(placed) if isinstance(out_shape, t...  119 us
    ppermute x58, waiting for transfers between devices, swap(): return lax.ppermute(x, axis, [(i, i ^ bit) for i in range(size)])  109 us
    ppermute x58, starting transfers between devices, swap(): return lax.ppermute(x, axis, [(i, i ^ bit) for i in range(size)])  68.5 us
    all_to_all x1, waiting for transfers between devices, per_device(): got = lax.all_to_all(sent, BOTH, split_axis=0, concat_axis=0, tiled=True)  21.9 us
    unnamed x111, local copies, waits for them, and re-layouts  14.5 us
    convert_element_type x18, other arithmetic, tip(): return x[:8, :128].astype(F32)  12.8 us
  transfers between devices with their start and end apart: 60, of which 36 were waited for; matrix products, arithmetic and copies ran while one was open for 9% of the time, Pallas kernels for 22%

commit v1 on v0

--- a/solution.py
+++ b/solution.py
@@ -853,8 +853,6 @@
         d_g_near = after(d_g_near, item["send"])
         another_cut()
         item["part"] = item["kept"] + swap(item["send"], *item["to"]).astype(F32)
-        if bit == z_bits[0]:
-            early = item["part"]
     own_grad = item["part"][0, 0]
     d_first = jnp.concatenate(d_first, 1)
     d_w_one, d_bias_one = d_first[:FIN], d_first[FIN].astype(F32)
@@ -868,7 +866,7 @@
         ],
         0,
     )
-    d_small = after(d_small.reshape(n_dev, per_small * UNIT, LANES), early)
+    d_small = after(d_small.reshape(n_dev, per_small * UNIT, LANES), own_grad)
     got = lax.all_to_all(d_small, BOTH, split_axis=0, concat_axis=0, tiled=True)
     got = jnp.sum(got.astype(F32), axis=0)
     low = got.astype(BF16)

time: 391 us -> 381 us (0.974)
  waiting for transfers between devices: 131 us -> 123 us
    ppermute x58, waiting for transfers between devices: 109 us -> 82.8 us  [swap(): return lax.ppermute(x, axis, [(i, i ^ bit) for i in range(size)])]
    all_to_all x1, waiting for transfers between devices: 0.01 us -> 17.8 us  [per_device(): got = lax.all_to_all(d_small, BOTH, split_axis=0, concat_axis=0, tiled=True)]
  transfers between devices with their start and end apart: 60 -> 60, of which waited for: 36 -> 37; matrix products, arithmetic and copies ran while one was open for 9% -> 10% of each run, Pallas kernels for 22% -> 24%
where the time goes in v1:
time: 381 us; the launch traced here: 379 us
  waiting for transfers between devices  123 us (32%)
  Pallas kernels  119 us (31%)
  starting transfers between devices  74.7 us (20%)
  other arithmetic  28 us (7%)
  local copies, waits for them, and re-layouts  26.9 us (7%)
  between operations  4.78 us (1%)
    pallas_call x20, Pallas kernels, run(): pl.pallas_call(kernel, out_shape=tuple(placed) if isinstance(out_shape, t...  119 us
    ppermute x58, waiting for transfers between devices, swap(): return lax.ppermute(x, axis, [(i, i ^ bit) for i in range(size)])  82.8 us
    ppermute x58, starting transfers between devices, swap(): return lax.ppermute(x, axis, [(i, i ^ bit) for i in range(size)])  67.3 us
    all_to_all x1, waiting for transfers between devices, per_device(): got = lax.all_to_all(sent, BOTH, split_axis=0, concat_axis=0, tiled=True)  21.9 us
    all_to_all x1, waiting for transfers between devices, per_device(): got = lax.all_to_all(d_small, BOTH, split_axis=0, concat_axis=0, tiled=True)  17.8 us
    unnamed x111, local copies, waits for them, and re-layouts  14.5 us
    convert_element_type x18, other arithmetic, tip(): return x[:8, :128].astype(F32)  12.8 us
  transfers between devices with their start and end apart: 60, of which 37 were waited for; matrix products, arithmetic and copies ran while one was open for 10% of the time, Pallas kernels for 24%

profile of v1, /device:TPU:0, one launch (start us, length us, event | category | flops | bytes accessed | tf_op | source)
XLA Modules:
  0.0 379.5 jit_solution(252848002864552072)
XLA Ops:
  1.6 3.0 collective-permute-start
  4.6 1.5 collective-permute-start.1
  7.1 4.0 %masked_tile.1 = (bf16[256,512]{1,0:T(8,128)(2,1)}, bf16[256,512]{1,0:T(8,128)(2,1)}, bf16[256,512]{1,0:T(8,128)(2,1)}, bf16[256,512]{1,0:T(8,128)(2,1)}, bf16[2...) custom-call(s32[2]{0:T(128)S(1)} %pad_add_fusion.1.refs_0_, ...), custom_call_target="tpu_custom_call" | custom-call | tf_op jit(solution)/shard_map/masked_tile/pallas_call | solution.py:127
  11.3 2.2 layer_one.1
  16.1 2.9 collective-permute-start.16
  19.0 1.6 collective-permute-start.17
  21.3 3.9 %collective-permute-start.6 = (bf16[2,128,128]{2,1,0:T(8,128)(2,1)S(1)}, bf16[2,128,128]{2,1,0:T(8,128)(2,1)S(1)}, u32[]{:S(2)}, u32[]{:S(2)}) collective-permute-start(bf16[2,128,128]{2,1,0:T(8,128)(2,1)S(1)} %get-tuple-element.113), channel_id=1, source_target_pairs={{0,6},{1,7},{2,4},{3,5},{4,2},{5,3},{6,0},{7,1},{8,14},{9,15},{10,... | collective-permute-start | bytes 196616 | tf_op jit(solution)/shard_map/ppermute | solution.py:38
  25.2 8.4 %collective-permute-done.16.refs_0_ = bf16[1,72,2048]{2,1,0:T(8,128)(2,1)S(1)} collective-permute-done((bf16[1,72,2048]{2,1,0:T(8,128)(2,1)}, bf16[1,72,2048]{2,1,0:T(8,128)(2,1)S(1)}, u32[]{:S(2)}, u32[]{:S(2)}) %collective-permute-start.16) | collective-permute-done | bytes 294944 | tf_op jit(solution)/shard_map/ppermute | solution.py:38
  33.6 1.7 collective-permute-start.19
  38.8 2.8 collective-permute-start.9
  43.9 4.2 %collective-permute-done.9 = bf16[2,128,128]{2,1,0:T(8,128)(2,1)S(1)} collective-permute-done((bf16[2,128,128]{2,1,0:T(8,128)(2,1)S(1)}, bf16[2,128,128]{2,1,0:T(8,128)(2,1)S(1)}, u32[]{:S(2)}, u32[]{:S(2)}) %collective-permute-start.9) | collective-permute-done | bytes 65568 | tf_op jit(solution)/shard_map/ppermute | solution.py:38
  48.1 1.5 collective-permute-start.23
  53.4 1.6 collective-permute-start.10
  55.0 4.3 %collective-permute-done.12.refs_3_ = bf16[4,2,128,128]{3,2,1,0:T(8,128)(2,1)S(1)} collective-permute-done((bf16[4,2,128,128]{3,2,1,0:T(8,128)(2,1)S(1)}, bf16[4,2,128,128]{3,2,1,0:T(8,128)(2,1)S(1)}, u32[]{:S(2)}, u32[]{:S(2)}) %collective-permute-start.12) | collective-permute-done | bytes 262176 | tf_op jit(solution)/shard_map/ppermute | solution.py:38
  60.7 12.0 %collective-permute-done.11.refs_2_ = bf16[4,2,128,128]{3,2,1,0:T(8,128)(2,1)S(1)} collective-permute-done((bf16[4,2,128,128]{3,2,1,0:T(8,128)(2,1)S(1)}, bf16[4,2,128,128]{3,2,1,0:T(8,128)(2,1)S(1)}, u32[]{:S(2)}, u32[]{:S(2)}) %collective-permute-start.11) | collective-permute-done | bytes 262176 | tf_op jit(solution)/shard_map/ppermute | solution.py:38
  73.9 2.5 collective-permute-start.15
  76.4 1.5 collective-permute-start.22
  77.9 1.9 collective-permute-start.13
  79.8 1.7 copy.98.refs_0_
  81.5 1.7 copy.100.refs_0_
  88.2 2.6 collective-permute-done.14.refs_6_.refs_2_
  90.8 2.0 collective-permute-start.25
  92.9 3.0 collective-permute-done.13.refs_5_.refs_1_
  100.9 5.7 %collective-permute-done.27 = bf16[1,72,2048]{2,1,0:T(8,128)(2,1)} collective-permute-done((bf16[1,72,2048]{2,1,0:T(8,128)(2,1)}, bf16[1,72,2048]{2,1,0:T(8,128)(2,1)}, u32[]{:S(2)}, u32[]{:S(2)}) %collective-permute-start.27) | collective-permute-done | bytes 294944 | tf_op jit(solution)/shard_map/ppermute | solution.py:38
  106.6 1.6 collective-permute-done.26
  109.0 4.6 %join.3.wn_ref.refs_3_ = bf16[1152,2048]{1,0:T(8,128)(2,1)} custom-call(bf16[72,2048]{1,0:T(8,128)(2,1)} %bitcast.185, bf16[144,2048]{1,0:T(8,128)(2,1)} %bitcast.168, bf16[72,2048]{1,0:T(8,128)(2,1)} %bitcast.191, bf16[72,2048]{1,0:T(8,128)(2,1)} %bitcast.26.refs_3_, bf16[144,2048]{1,0:T(8,128)(2,1)} %bitcast.27.refs_4_, bf16[72,2048]{1,0:T(8,128)(2,1)} %bitcast.28.refs_5_, ...), custom_call_target="tpu_custom_call" | custom-call | tf_op jit(solution)/shard_map/join/pallas_call | solution.py:127
  114.1 3.4 convolution_convert_fusion
  118.1 2.7 collective-permute-start.31
  126.0 14.6 %forward_two.2 = (f32[128,2048]{1,0:T(8,128)}, bf16[128,2048]{1,0:T(8,128)(2,1)}, bf16[2048,2048]{1,0:T(8,128)(2,1)}) custom-call(bf16[4,2,128,128]{3,2,1,0:T(8,128)(2,1)} %copy-done.4, bf16[4,2,128,128]{3,2,1,0:T(8,128)(2,1)} %copy-done.15, bf16[4,2,128,128]{3,2,1,0:T(8,128)(2,1)} %copy-done.14, bf16[4,2,128,128]{3,2,1,0:T(8,128)(2,1)} %copy-done.13, ...), custom_call_target="tpu_custom_call" | custom-call | tf_op jit(solution)/shard_map/forward_two/pallas_call | solution.py:127
  141.2 3.1 collective-permute-done.29.refs_5_.refs_9_
  145.0 14.4 %forward_two.3 = (f32[128,2048]{1,0:T(8,128)}, bf16[128,2048]{1,0:T(8,128)(2,1)}, bf16[2048,2048]{1,0:T(8,128)(2,1)}) custom-call(bf16[4,2,128,128]{3,2,1,0:T(8,128)(2,1)} %copy-done.4, bf16[4,2,128,128]{3,2,1,0:T(8,128)(2,1)} %copy-done.15, bf16[4,2,128,128]{3,2,1,0:T(8,128)(2,1)} %copy-done.14, bf16[4,2,128,128]{3,2,1,0:T(8,128)(2,1)} %copy-done.13, ...), custom_call_target="tpu_custom_call" | custom-call | tf_op jit(solution)/shard_map/forward_two/pallas_call | solution.py:127
  162.9 8.6 %spread_two.1 = (bf16[256,1152]{1,0:T(8,128)(2,1)}, bf16[256,1152]{1,0:T(8,128)(2,1)}) custom-call(f32[128,2048]{1,0:T(8,128)} %get-tuple-element.67.refs_0_, f32[128,2048]{1,0:T(8,128)} %get-tuple-element.71.refs_1_, bf16[128,2048]{1,0:T(8,128)(2,1)} %copy-done.37, bf16[128,2048]{1,0:T(8,128)(2,1)} %copy-done.36, bf16[256,128]{1,0:T(8,128)(2,1)S(1)} %bitcast.177, ...), custom_call_target="tpu_custom_call" | custom-call | tf_op jit(solution)/shard_map/spread_two/pallas_call | solution.py:127
  172.2 9.0 %layer_two.1 = (f32[256,2048]{1,0:T(8,128)}, bf16[256,2048]{1,0:T(8,128)(2,1)}, bf16[128,128]{1,0:T(8,128)(2,1)S(1)}) custom-call(bf16[256,1152]{1,0:T(8,128)(2,1)} %get-tuple-element.74.gn_ref.refs_0_, bf16[256,1152]{1,0:T(8,128)(2,1)} %get-tuple-element.75.gf_ref.refs_9_, bf16[1152,2048]{1,0:T(8,128)(2,1)} %join.3.wn_ref.refs_3_, ...), custom_call_target="tpu_custom_call" | custom-call | tf_op jit(solution)/shard_map/layer_two/pallas_call | solution.py:127
  181.6 2.8 collective-permute-start.36
  186.6 3.5 collective-permute-done.37
  191.6 2.1 collective-permute-start.40
  193.7 1.7 collective-permute-done.38.refs_9_
  198.2 2.3 logits_parts.1
  203.7 1.8 collective-permute-start.44
  205.5 2.6 collective-permute-start.45
  209.5 2.1 collective-permute-done.45.refs_11_
  211.6 2.3 d_q_parts.1
  213.8 2.6 collective-permute-start.46
  218.7 2.1 collective-permute-done.47.refs_2_
  220.8 1.9 collective-permute-done.48.refs_3_
  222.7 5.3 %d_two.2 = (bf16[256,1024]{1,0:T(8,128)(2,1)}, f32[8,1024]{1,0:T(8,128)S(1)}, f32[1024,128]{1,0:T(8,128)}, bf16[1152,1024]{1,0:T(8,128)(2,1)}) custom-call(f32[128,128]{1,0:T(8,128)S(1)} %get-tuple-element.80.refs_0_, f32[128,128]{1,0:T(8,128)S(1)} %collective-permute-done.46.refs_1_, f32[128,128]{1,0:T(8,128)S(1)} %collective-permute-done.47.refs_2_, ...), custom_call_target="tpu_custom_call" | custom-call | tf_op jit(solution)/shard_map/d_two/pallas_call | solution.py:127
  230.0 5.2 %d_two.3 = (bf16[256,1024]{1,0:T(8,128)(2,1)}, f32[8,1024]{1,0:T(8,128)S(1)}, f32[1024,128]{1,0:T(8,128)}, bf16[1152,1024]{1,0:T(8,128)(2,1)}) custom-call(f32[128,128]{1,0:T(8,128)S(1)} %get-tuple-element.80.refs_0_, f32[128,128]{1,0:T(8,128)S(1)} %collective-permute-done.46.refs_1_, f32[128,128]{1,0:T(8,128)S(1)} %collective-permute-done.47.refs_2_, ...), custom_call_target="tpu_custom_call" | custom-call | tf_op jit(solution)/shard_map/d_two/pallas_call | solution.py:127
  236.6 5.2 %near_part.2 = (f32[576,1024]{1,0:T(8,128)}, bf16[576,1024]{1,0:T(8,128)(2,1)}) custom-call(bf16[256,1152]{1,0:T(8,128)(2,1)} %get-tuple-element.74.gn_ref.refs_0_, bf16[256,1024]{1,0:T(8,128)(2,1)} %get-tuple-element.86.refs_1_.refs_0_, bf16[1152,1024]{1,0:T(8,128)(2,1)} %collective-permute-done.49.refs_2_), custom_call_target="tpu_custom_call" | custom-call | tf_op jit(solution)/shard_map/near_part/pallas_call | solution.py:127
  242.4 5.3 %near_part.3 = (f32[576,1024]{1,0:T(8,128)}, bf16[576,1024]{1,0:T(8,128)(2,1)}) custom-call(bf16[256,1152]{1,0:T(8,128)(2,1)} %get-tuple-element.74.gn_ref.refs_0_, bf16[256,1024]{1,0:T(8,128)(2,1)} %get-tuple-element.90.refs_1_, bf16[1152,1024]{1,0:T(8,128)(2,1)} %collective-permute-done.52.refs_2_), custom_call_target="tpu_custom_call" | custom-call | tf_op jit(solution)/shard_map/near_part/pallas_call | solution.py:127
  252.3 12.3 %d_g_two.1 = bf16[256,2048]{1,0:T(8,128)(2,1)} custom-call(bf16[256,1024]{1,0:T(8,128)(2,1)} %after.35.refs_0_, bf16[256,1024]{1,0:T(8,128)(2,1)} %get-tuple-element.90.refs_1_, s32[2304,1]{1,0:T(8,128)S(1)} %broadcast_add_fusion.refs_2_, bf16[1152,2048]{1,0:T(8,128)(2,1)} %join.3.wn_ref.refs_3_, bf16[1152,2048]{1,0:T(8,128)(2,1)} %collective-permute-done.34.wf_ref.refs_4_), custom_call_target="tpu_custom_call" | custom-call | tf_op jit(solution)/shard_map/d_g_two/pallas_call | solution.py:127
  264.5 5.4 %collective-permute-done.50 = bf16[2,4,72,1024]{3,2,1,0:T(8,128)(2,1)} collective-permute-done((bf16[2,4,72,1024]{3,2,1,0:T(8,128)(2,1)}, bf16[2,4,72,1024]{3,2,1,0:T(8,128)(2,1)}, u32[]{:S(2)}, u32[]{:S(2)}) %collective-permute-start.50) | collective-permute-done | bytes 1179680 | tf_op jit(solution)/shard_map/ppermute | solution.py:38
  270.0 2.0 add_bitcast_fusion.1
  273.1 3.6 collective-permute-done.53
  277.3 2.0 collective-permute-start.54
  281.6 8.1 %backward_one.3 = bf16[128,768]{1,0:T(8,128)(2,1)} custom-call(bf16[4,2,128,128]{3,2,1,0:T(8,128)(2,1)} %copy-done.4, bf16[4,2,128,128]{3,2,1,0:T(8,128)(2,1)} %copy-done.15, bf16[4,2,128,128]{3,2,1,0:T(8,128)(2,1)} %copy-done.14, bf16[4,2,128,128]{3,2,1,0:T(8,128)(2,1)} %copy-done.13, bf16[256,512]{1,0:T(8,128)(2,1)} %get-tuple-element.54.refs_0_.refs_4_, ...), custom_call_target="tpu_custom_call" | custom-call | tf_op jit(solution)/shard_map/backward_one/pallas_call | solution.py:127
  294.1 7.8 %backward_one.4 = bf16[128,768]{1,0:T(8,128)(2,1)} custom-call(bf16[4,2,128,128]{3,2,1,0:T(8,128)(2,1)} %copy-done.4, bf16[4,2,128,128]{3,2,1,0:T(8,128)(2,1)} %copy-done.15, bf16[4,2,128,128]{3,2,1,0:T(8,128)(2,1)} %copy-done.14, bf16[4,2,128,128]{3,2,1,0:T(8,128)(2,1)} %copy-done.13, bf16[256,512]{1,0:T(8,128)(2,1)} %get-tuple-element.54.refs_0_.refs_4_, ...), custom_call_target="tpu_custom_call" | custom-call | tf_op jit(solution)/shard_map/backward_one/pallas_call | solution.py:127
  302.0 4.2 %collective-permute-done.55 = bf16[1,2,72,2048]{3,2,1,0:T(8,128)(2,1)S(1)} collective-permute-done((bf16[1,2,72,2048]{3,2,1,0:T(8,128)(2,1)S(1)}, bf16[1,2,72,2048]{3,2,1,0:T(8,128)(2,1)S(1)}, u32[]{:S(2)}, u32[]{:S(2)}) %collective-permute-start.55) | collective-permute-done | bytes 589856 | tf_op jit(solution)/shard_map/ppermute | solution.py:38
  306.9 1.5 collective-permute-start.56
  308.4 6.1 %backward_one.5 = bf16[128,512]{1,0:T(8,128)(2,1)} custom-call(bf16[4,2,128,128]{3,2,1,0:T(8,128)(2,1)} %copy-done.4, bf16[4,2,128,128]{3,2,1,0:T(8,128)(2,1)} %copy-done.15, bf16[4,2,128,128]{3,2,1,0:T(8,128)(2,1)} %copy-done.14, bf16[4,2,128,128]{3,2,1,0:T(8,128)(2,1)} %copy-done.13, bf16[256,512]{1,0:T(8,128)(2,1)} %get-tuple-element.54.refs_0_.refs_4_, ...), custom_call_target="tpu_custom_call" | custom-call | tf_op jit(solution)/shard_map/backward_one/pallas_call | solution.py:127
  320.2 4.8 %all-to-all-start = ((bf16[32,80,128]{2,1,0:T(8,128)(2,1)}), bf16[32,80,128]{2,1,0:T(8,128)(2,1)S(1)}, u32[]{:S(2)}, u32[]{:S(2)}) async-start(bf16[32,80,128]{2,1,0:T(8,128)(2,1)} %after.39), calls=%async_computation | async-start | bytes 1310720 | tf_op jit(solution)/shard_map/all_to_all | solution.py:870
  326.4 17.8 %all-to-all-done = bf16[32,80,128]{2,1,0:T(8,128)(2,1)S(1)} async-done(((bf16[32,80,128]{2,1,0:T(8,128)(2,1)}), bf16[32,80,128]{2,1,0:T(8,128)(2,1)S(1)}, u32[]{:S(2)}, u32[]{:S(2)}) %all-to-all-start) | async-done | bytes 655392 | tf_op jit(solution)/shard_map/all_to_all | solution.py:870
  347.9 2.6 all-to-all-start.1
  350.6 21.9 %all-to-all-done.1 = bf16[32,96,128]{2,1,0:T(8,128)(2,1)S(1)} async-done(((bf16[32,96,128]{2,1,0:T(8,128)(2,1)}), bf16[32,96,128]{2,1,0:T(8,128)(2,1)S(1)}, u32[]{:S(2)}, u32[]{:S(2)}) %all-to-all-start.1) | async-done | bytes 786464 | tf_op jit(solution)/shard_map/all_to_all | solution.py:879
  375.7 2.6 multiply_subtract_fusion
  (321 shorter events, 82.9 us)
Async XLA Ops:
  1.6 9.5 %collective-permute-start = (bf16[2,128,128]{2,1,0:T(8,128)(2,1)S(1)}, bf16[2,128,128]{2,1,0:T(8,128)(2,1)S(1)}, u32[]{:S(2)}, u32[]{:S(2)}) collective-permute-start(bf16[2,128,128]{2,1,0:T(8,128)(2,1)S(1)} %pad.9.refs_8_), channel_id=1, source_target_pairs={{0,8},{8,0},{16,24},{24,16},{1,9},{9,1},{17,25},{25,17},{2,10},{10... | collective-permute-start | bytes 196616 | tf_op jit(solution)/shard_map/ppermute | solution.py:38
  4.6 6.5 %collective-permute-start.1 = (bf16[2,128,128]{2,1,0:T(8,128)(2,1)S(1)}, bf16[2,128,128]{2,1,0:T(8,128)(2,1)S(1)}, u32[]{:S(2)}, u32[]{:S(2)}) collective-permute-start(bf16[2,128,128]{2,1,0:T(8,128)(2,1)S(1)} %pad.9.refs_8_), channel_id=1, source_target_pairs={{0,16},{8,24},{16,0},{24,8},{1,17},{9,25},{17,1},{25,9},{2,18},{10... | collective-permute-start | bytes 196616 | tf_op jit(solution)/shard_map/ppermute | solution.py:38
  6.1 5.2 %collective-permute-start.2 = (bf16[2,128,128]{2,1,0:T(8,128)(2,1)S(1)}, bf16[2,128,128]{2,1,0:T(8,128)(2,1)S(1)}, u32[]{:S(2)}, u32[]{:S(2)}) collective-permute-start(bf16[2,128,128]{2,1,0:T(8,128)(2,1)S(1)} %pad.9.refs_8_), channel_id=1, source_target_pairs={{0,24},{8,16},{16,8},{24,0},{1,25},{9,17},{17,9},{25,1},{2,26},{10... | collective-permute-start | bytes 196616 | tf_op jit(solution)/shard_map/ppermute | solution.py:38
  13.5 7.1 %collective-permute-start.3 = (f32[4,2,128,128]{3,2,1,0:T(8,128)S(1)}, f32[4,2,128,128]{3,2,1,0:T(8,128)S(1)}, u32[]{:S(2)}, u32[]{:S(2)}) collective-permute-start(f32[4,2,128,128]{3,2,1,0:T(8,128)S(1)} %get-tuple-element.63), channel_id=1, source_target_pairs={{0,1},{1,0},{2,3},{3,2},{4,5},{5,4},{6,7},{7,6},{8,9},{9,8},{10,11... | collective-permute-start | bytes 1572872 | tf_op jit(solution)/shard_map/ppermute | solution.py:38
  16.1 17.4 %collective-permute-start.16 = (bf16[1,72,2048]{2,1,0:T(8,128)(2,1)}, bf16[1,72,2048]{2,1,0:T(8,128)(2,1)S(1)}, u32[]{:S(2)}, u32[]{:S(2)}) collective-permute-start(bf16[1,72,2048]{2,1,0:T(8,128)(2,1)} %after.23.refs_0_), channel_id=1, source_target_pairs={{0,4},{1,5},{2,6},{3,7},{4,0},{5,1},{6,2},{7,3},{8,12},{9,13},{10,... | collective-permute-start | bytes 884744 | tf_op jit(solution)/shard_map/ppermute | solution.py:38
  19.0 16.4 %collective-permute-start.17 = (bf16[1,72,2048]{2,1,0:T(8,128)(2,1)}, bf16[1,72,2048]{2,1,0:T(8,128)(2,1)S(1)}, u32[]{:S(2)}, u32[]{:S(2)}) collective-permute-start(bf16[1,72,2048]{2,1,0:T(8,128)(2,1)} %after.23.refs_0_), channel_id=1, source_target_pairs={{0,2},{1,3},{2,0},{3,1},{4,6},{5,7},{6,4},{7,5},{8,10},{9,11},{10,... | collective-permute-start | bytes 884744 | tf_op jit(solution)/shard_map/ppermute | solution.py:38
  20.7 17.3 %collective-permute-start.4 = (bf16[2,128,128]{2,1,0:T(8,128)(2,1)S(1)}, bf16[2,128,128]{2,1,0:T(8,128)(2,1)S(1)}, u32[]{:S(2)}, u32[]{:S(2)}) collective-permute-start(bf16[2,128,128]{2,1,0:T(8,128)(2,1)S(1)} %get-tuple-element.112), channel_id=1, source_target_pairs={{0,4},{1,5},{2,6},{3,7},{4,0},{5,1},{6,2},{7,3},{8,12},{9,13},{10,... | collective-permute-start | bytes 196616 | tf_op jit(solution)/shard_map/ppermute | solution.py:38
  21.1 16.9 %collective-permute-start.5 = (bf16[2,128,128]{2,1,0:T(8,128)(2,1)S(1)}, bf16[2,128,128]{2,1,0:T(8,128)(2,1)S(1)}, u32[]{:S(2)}, u32[]{:S(2)}) collective-permute-start(bf16[2,128,128]{2,1,0:T(8,128)(2,1)S(1)} %get-tuple-element.114), channel_id=1, source_target_pairs={{0,2},{1,3},{2,0},{3,1},{4,6},{5,7},{6,4},{7,5},{8,10},{9,11},{10,... | collective-permute-start | bytes 196616 | tf_op jit(solution)/shard_map/ppermute | solution.py:38
  21.3 17.4 %collective-permute-start.6 = (bf16[2,128,128]{2,1,0:T(8,128)(2,1)S(1)}, bf16[2,128,128]{2,1,0:T(8,128)(2,1)S(1)}, u32[]{:S(2)}, u32[]{:S(2)}) collective-permute-start(bf16[2,128,128]{2,1,0:T(8,128)(2,1)S(1)} %get-tuple-element.113), channel_id=1, source_target_pairs={{0,6},{1,7},{2,4},{3,5},{4,2},{5,3},{6,0},{7,1},{8,14},{9,15},{10,... | collective-permute-start | bytes 196616 | tf_op jit(solution)/shard_map/ppermute | solution.py:38
  33.6 44.3 %collective-permute-start.19 = (bf16[1,72,2048]{2,1,0:T(8,128)(2,1)S(1)}, bf16[1,72,2048]{2,1,0:T(8,128)(2,1)}, u32[]{:S(2)}, u32[]{:S(2)}) collective-permute-start(bf16[1,72,2048]{2,1,0:T(8,128)(2,1)S(1)} %copy-done.22), channel_id=1, source_target_pairs={{0,8},{8,0},{16,24},{24,16},{1,9},{9,1},{17,25},{25,17},{2,10},{10... | collective-permute-start | bytes 884744 | tf_op jit(solution)/shard_map/ppermute | solution.py:38
  35.4 18.1 %collective-permute-start.18 = (bf16[1,72,2048]{2,1,0:T(8,128)(2,1)S(1)}, bf16[1,72,2048]{2,1,0:T(8,128)(2,1)S(1)}, u32[]{:S(2)}, u32[]{:S(2)}) collective-permute-start(bf16[1,72,2048]{2,1,0:T(8,128)(2,1)S(1)} %collective-permute-done.16.refs_0_), channel_id=1, source_target_pairs={{0,2},{1,3},{2,0},{3,1},{4,6},{5,7},{6,4},{7,5},{8,10},{9,11},{10,... | collective-permute-start | bytes 884744 | tf_op jit(solution)/shard_map/ppermute | solution.py:38
  38.8 9.3 %collective-permute-start.9 = (bf16[2,128,128]{2,1,0:T(8,128)(2,1)S(1)}, bf16[2,128,128]{2,1,0:T(8,128)(2,1)S(1)}, u32[]{:S(2)}, u32[]{:S(2)}) collective-permute-start(bf16[2,128,128]{2,1,0:T(8,128)(2,1)S(1)} %fusion.19), channel_id=1, source_target_pairs={{0,6},{1,7},{2,4},{3,5},{4,2},{5,3},{6,0},{7,1},{8,14},{9,15},{10,... | collective-permute-start | bytes 196616 | tf_op jit(solution)/shard_map/ppermute | solution.py:38
  41.6 8.0 %collective-permute-start.8 = (bf16[2,128,128]{2,1,0:T(8,128)(2,1)S(1)}, bf16[2,128,128]{2,1,0:T(8,128)(2,1)S(1)}, u32[]{:S(2)}, u32[]{:S(2)}) collective-permute-start(bf16[2,128,128]{2,1,0:T(8,128)(2,1)S(1)} %fusion.19), channel_id=1, source_target_pairs={{0,2},{1,3},{2,0},{3,1},{4,6},{5,7},{6,4},{7,5},{8,10},{9,11},{10,... | collective-permute-start | bytes 196616 | tf_op jit(solution)/shard_map/ppermute | solution.py:38
  42.3 7.4 %collective-permute-start.7 = (bf16[2,128,128]{2,1,0:T(8,128)(2,1)S(1)}, bf16[2,128,128]{2,1,0:T(8,128)(2,1)S(1)}, u32[]{:S(2)}, u32[]{:S(2)}) collective-permute-start(bf16[2,128,128]{2,1,0:T(8,128)(2,1)S(1)} %fusion.19), channel_id=1, source_target_pairs={{0,4},{1,5},{2,6},{3,7},{4,0},{5,1},{6,2},{7,3},{8,12},{9,13},{10,... | collective-permute-start | bytes 196616 | tf_op jit(solution)/shard_map/ppermute | solution.py:38
  48.1 35.1 %collective-permute-start.23 = (bf16[2,72,2048]{2,1,0:T(8,128)(2,1)}, bf16[2,72,2048]{2,1,0:T(8,128)(2,1)S(1)}, u32[]{:S(2)}, u32[]{:S(2)}) collective-permute-start(bf16[2,72,2048]{2,1,0:T(8,128)(2,1)} %after.25), channel_id=1, source_target_pairs={{0,16},{8,24},{16,0},{24,8},{1,17},{9,25},{17,1},{25,9},{2,18},{10... | collective-permute-start | bytes 1769480 | tf_op jit(solution)/shard_map/ppermute | solution.py:38
  49.7 33.6 %copy-start.4 = (bf16[4,2,128,128]{3,2,1,0:T(8,128)(2,1)}, bf16[4,2,128,128]{3,2,1,0:T(8,128)(2,1)S(1)}, u32[]{:S(2)}) copy-start(bf16[4,2,128,128]{3,2,1,0:T(8,128)(2,1)S(1)} %pad_maximum_fusion.3.refs_0_) | copy-start | bytes 786436
  49.7 9.7 %collective-permute-start.12 = (bf16[4,2,128,128]{3,2,1,0:T(8,128)(2,1)S(1)}, bf16[4,2,128,128]{3,2,1,0:T(8,128)(2,1)S(1)}, u32[]{:S(2)}, u32[]{:S(2)}) collective-permute-start(bf16[4,2,128,128]{3,2,1,0:T(8,128)(2,1)S(1)} %pad_maximum_fusion.3.refs_0_), channel_id=1, source_target_pairs={{0,24},{8,16},{16,8},{24,0},{1,25},{9,17},{17,9},{25,1},{2,26},{10... | collective-permute-start | bytes 786440 | tf_op jit(solution)/shard_map/ppermute | solution.py:38
  50.8 21.8 %collective-permute-start.11 = (bf16[4,2,128,128]{3,2,1,0:T(8,128)(2,1)S(1)}, bf16[4,2,128,128]{3,2,1,0:T(8,128)(2,1)S(1)}, u32[]{:S(2)}, u32[]{:S(2)}) collective-permute-start(bf16[4,2,128,128]{3,2,1,0:T(8,128)(2,1)S(1)} %pad_maximum_fusion.3.refs_0_), channel_id=1, source_target_pairs={{0,16},{8,24},{16,0},{24,8},{1,17},{9,25},{17,1},{25,9},{2,18},{10... | collective-permute-start | bytes 786440 | tf_op jit(solution)/shard_map/ppermute | solution.py:38
  53.4 19.8 %collective-permute-start.10 = (bf16[4,2,128,128]{3,2,1,0:T(8,128)(2,1)S(1)}, bf16[4,2,128,128]{3,2,1,0:T(8,128)(2,1)S(1)}, u32[]{:S(2)}, u32[]{:S(2)}) collective-permute-start(bf16[4,2,128,128]{3,2,1,0:T(8,128)(2,1)S(1)} %pad_maximum_fusion.3.refs_0_), channel_id=1, source_target_pairs={{0,8},{8,0},{16,24},{24,16},{1,9},{9,1},{17,25},{25,17},{2,10},{10... | collective-permute-start | bytes 786440 | tf_op jit(solution)/shard_map/ppermute | solution.py:38
  55.0 28.2 %copy-start.1 = (bf16[2,72,2048]{2,1,0:T(8,128)(2,1)S(1)}, bf16[2,72,2048]{2,1,0:T(8,128)(2,1)}, u32[]{:S(2)}) copy-start(bf16[2,72,2048]{2,1,0:T(8,128)(2,1)} %after.25) | copy-start | bytes 1769476
  59.3 18.6 %collective-permute-start.21 = (bf16[1,72,2048]{2,1,0:T(8,128)(2,1)}, bf16[1,72,2048]{2,1,0:T(8,128)(2,1)}, u32[]{:S(2)}, u32[]{:S(2)}) collective-permute-start(bf16[1,72,2048]{2,1,0:T(8,128)(2,1)} %after.26), channel_id=1, source_target_pairs={{0,8},{8,0},{16,24},{24,16},{1,9},{9,1},{17,25},{25,17},{2,10},{10... | collective-permute-start | bytes 884744 | tf_op jit(solution)/shard_map/ppermute | solution.py:38
  73.9 11.3 %collective-permute-start.15 = (bf16[256,512]{1,0:T(8,128)(2,1)}, bf16[256,512]{1,0:T(8,128)(2,1)S(1)}, u32[]{:S(2)}, u32[]{:S(2)}) collective-permute-start(bf16[256,512]{1,0:T(8,128)(2,1)} %after.22), channel_id=1, source_target_pairs={{0,6},{1,7},{2,4},{3,5},{4,2},{5,3},{6,0},{7,1},{8,14},{9,15},{10,... | collective-permute-start | bytes 786440 | tf_op jit(solution)/shard_map/ppermute | solution.py:38
  76.4 10.5 %collective-permute-start.22 = (bf16[1,72,2048]{2,1,0:T(8,128)(2,1)S(1)}, bf16[1,72,2048]{2,1,0:T(8,128)(2,1)}, u32[]{:S(2)}, u32[]{:S(2)}) collective-permute-start(bf16[1,72,2048]{2,1,0:T(8,128)(2,1)S(1)} %copy-done.22), channel_id=1, source_target_pairs={{0,16},{8,24},{16,0},{24,8},{1,17},{9,25},{17,1},{25,9},{2,18},{10... | collective-permute-start | bytes 884744 | tf_op jit(solution)/shard_map/ppermute | solution.py:38
  77.9 12.9 %collective-permute-start.14 = (bf16[256,512]{1,0:T(8,128)(2,1)}, bf16[256,512]{1,0:T(8,128)(2,1)S(1)}, u32[]{:S(2)}, u32[]{:S(2)}) collective-permute-start(bf16[256,512]{1,0:T(8,128)(2,1)} %after.21), channel_id=1, source_target_pairs={{0,2},{1,3},{2,0},{3,1},{4,6},{5,7},{6,4},{7,5},{8,10},{9,11},{10,... | collective-permute-start | bytes 786440 | tf_op jit(solution)/shard_map/ppermute | solution.py:38
  77.9 18.0 %collective-permute-start.13 = (bf16[256,512]{1,0:T(8,128)(2,1)}, bf16[256,512]{1,0:T(8,128)(2,1)S(1)}, u32[]{:S(2)}, u32[]{:S(2)}) collective-permute-start(bf16[256,512]{1,0:T(8,128)(2,1)} %after.20), channel_id=1, source_target_pairs={{0,4},{1,5},{2,6},{3,7},{4,0},{5,1},{6,2},{7,3},{8,12},{9,13},{10,... | collective-permute-start | bytes 786440 | tf_op jit(solution)/shard_map/ppermute | solution.py:38
  83.2 16.4 %collective-permute-start.20 = (bf16[2,72,2048]{2,1,0:T(8,128)(2,1)S(1)}, bf16[2,72,2048]{2,1,0:T(8,128)(2,1)}, u32[]{:S(2)}, u32[]{:S(2)}) collective-permute-start(bf16[2,72,2048]{2,1,0:T(8,128)(2,1)S(1)} %copy-done.1), channel_id=1, source_target_pairs={{0,8},{8,0},{16,24},{24,16},{1,9},{9,1},{17,25},{25,17},{2,10},{10... | collective-permute-start | bytes 1769480 | tf_op jit(solution)/shard_map/ppermute | solution.py:38
  85.2 28.5 %copy-start.16 = (bf16[256,512]{1,0:T(8,128)(2,1)}, bf16[256,512]{1,0:T(8,128)(2,1)S(1)}, u32[]{:S(2)}) copy-start(bf16[256,512]{1,0:T(8,128)(2,1)S(1)} %collective-permute-done.15.refs_7_.refs_3_) | copy-start | bytes 786436
  85.2 23.0 %collective-permute-start.26 = (bf16[2,72,2048]{2,1,0:T(8,128)(2,1)}, bf16[2,72,2048]{2,1,0:T(8,128)(2,1)S(1)}, u32[]{:S(2)}, u32[]{:S(2)}) collective-permute-start(bf16[2,72,2048]{2,1,0:T(8,128)(2,1)} %after.28), channel_id=1, source_target_pairs={{0,8},{8,0},{16,24},{24,16},{1,9},{9,1},{17,25},{25,17},{2,10},{10... | collective-permute-start | bytes 1769480 | tf_op jit(solution)/shard_map/ppermute | solution.py:38
  86.8 11.6 %collective-permute-start.24 = (bf16[1,72,2048]{2,1,0:T(8,128)(2,1)}, bf16[1,72,2048]{2,1,0:T(8,128)(2,1)S(1)}, u32[]{:S(2)}, u32[]{:S(2)}) collective-permute-start(bf16[1,72,2048]{2,1,0:T(8,128)(2,1)} %after.26), channel_id=1, source_target_pairs={{0,16},{8,24},{16,0},{24,8},{1,17},{9,25},{17,1},{25,9},{2,18},{10... | collective-permute-start | bytes 884744 | tf_op jit(solution)/shard_map/ppermute | solution.py:38
  90.8 10.1 %collective-permute-start.25 = (bf16[1,72,2048]{2,1,0:T(8,128)(2,1)}, bf16[1,72,2048]{2,1,0:T(8,128)(2,1)S(1)}, u32[]{:S(2)}, u32[]{:S(2)}) collective-permute-start(bf16[1,72,2048]{2,1,0:T(8,128)(2,1)} %after.27), channel_id=1, source_target_pairs={{0,16},{8,24},{16,0},{24,8},{1,17},{9,25},{17,1},{25,9},{2,18},{10... | collective-permute-start | bytes 884744 | tf_op jit(solution)/shard_map/ppermute | solution.py:38
  95.9 10.7 %collective-permute-start.27 = (bf16[1,72,2048]{2,1,0:T(8,128)(2,1)}, bf16[1,72,2048]{2,1,0:T(8,128)(2,1)}, u32[]{:S(2)}, u32[]{:S(2)}) collective-permute-start(bf16[1,72,2048]{2,1,0:T(8,128)(2,1)} %after.29), channel_id=1, source_target_pairs={{0,16},{8,24},{16,0},{24,8},{1,17},{9,25},{17,1},{25,9},{2,18},{10... | collective-permute-start | bytes 884744 | tf_op jit(solution)/shard_map/ppermute | solution.py:38
  113.7 57.9 %collective-permute-start.34 = (bf16[1152,2048]{1,0:T(8,128)(2,1)}, bf16[1152,2048]{1,0:T(8,128)(2,1)}, u32[]{:S(2)}, u32[]{:S(2)}) collective-permute-start(bf16[1152,2048]{1,0:T(8,128)(2,1)} %join.3.wn_ref.refs_3_), channel_id=1, source_target_pairs={{0,1},{1,0},{2,3},{3,2},{4,5},{5,4},{6,7},{7,6},{8,9},{9,8},{10,11... | collective-permute-start | bytes 14155784 | tf_op jit(solution)/shard_map/ppermute | solution.py:38
  117.5 5.1 %collective-permute-start.28 = (bf16[160,2048]{1,0:T(8,128)(2,1)S(1)}, bf16[160,2048]{1,0:T(8,128)(2,1)S(1)}, u32[]{:S(2)}, u32[]{:S(2)}) collective-permute-start(bf16[160,2048]{1,0:T(8,128)(2,1)S(1)} %convolution_convert_fusion), channel_id=1, source_target_pairs={{0,1},{1,0},{2,3},{3,2},{4,5},{5,4},{6,7},{7,6},{8,9},{9,8},{10,11... | collective-permute-start | bytes 1966088 | tf_op jit(solution)/shard_map/ppermute | solution.py:38
  118.1 23.1 %collective-permute-start.31 = (bf16[256,512]{1,0:T(8,128)(2,1)}, bf16[256,512]{1,0:T(8,128)(2,1)S(1)}, u32[]{:S(2)}, u32[]{:S(2)}) collective-permute-start(bf16[256,512]{1,0:T(8,128)(2,1)} %after.32), channel_id=1, source_target_pairs={{0,6},{1,7},{2,4},{3,5},{4,2},{5,3},{6,0},{7,1},{8,14},{9,15},{10,... | collective-permute-start | bytes 786440 | tf_op jit(solution)/shard_map/ppermute | solution.py:38
  120.8 20.4 %collective-permute-start.30 = (bf16[256,512]{1,0:T(8,128)(2,1)}, bf16[256,512]{1,0:T(8,128)(2,1)S(1)}, u32[]{:S(2)}, u32[]{:S(2)}) collective-permute-start(bf16[256,512]{1,0:T(8,128)(2,1)} %after.31), channel_id=1, source_target_pairs={{0,2},{1,3},{2,0},{3,1},{4,6},{5,7},{6,4},{7,5},{8,10},{9,11},{10,... | collective-permute-start | bytes 786440 | tf_op jit(solution)/shard_map/ppermute | solution.py:38
  121.3 23.0 %collective-permute-start.29 = (bf16[256,512]{1,0:T(8,128)(2,1)}, bf16[256,512]{1,0:T(8,128)(2,1)S(1)}, u32[]{:S(2)}, u32[]{:S(2)}) collective-permute-start(bf16[256,512]{1,0:T(8,128)(2,1)} %after.30), channel_id=1, source_target_pairs={{0,4},{1,5},{2,6},{3,7},{4,0},{5,1},{6,2},{7,3},{8,12},{9,13},{10,... | collective-permute-start | bytes 786440 | tf_op jit(solution)/shard_map/ppermute | solution.py:38
  125.9 33.5 %copy-start.6 = (bf16[2048,128]{1,0:T(8,128)(2,1)}, bf16[2048,128]{1,0:T(8,128)(2,1)S(1)}, u32[]{:S(2)}) copy-start(bf16[2048,128]{1,0:T(8,128)(2,1)S(1)} %pad_maximum_fusion.1.w3_ref.refs_8_) | copy-start | bytes 1572868
  159.4 2.2 collective-permute-start.33
  159.5 2.6 collective-permute-start.32
  181.2 5.0 %collective-permute-start.35 = (bf16[128,128]{1,0:T(8,128)(2,1)S(1)}, bf16[128,128]{1,0:T(8,128)(2,1)S(1)}, u32[]{:S(2)}, u32[]{:S(2)}) collective-permute-start(bf16[128,128]{1,0:T(8,128)(2,1)S(1)} %get-tuple-element.76.q_ref), channel_id=1, source_target_pairs={{0,4},{1,5},{2,6},{3,7},{4,0},{5,1},{6,2},{7,3},{8,12},{9,13},{10,... | collective-permute-start | bytes 98312 | tf_op jit(solution)/shard_map/ppermute | solution.py:38
  181.6 5.0 %collective-permute-start.36 = (bf16[128,128]{1,0:T(8,128)(2,1)S(1)}, bf16[128,128]{1,0:T(8,128)(2,1)S(1)}, u32[]{:S(2)}, u32[]{:S(2)}) collective-permute-start(bf16[128,128]{1,0:T(8,128)(2,1)S(1)} %get-tuple-element.76.q_ref), channel_id=1, source_target_pairs={{0,2},{1,3},{2,0},{3,1},{4,6},{5,7},{6,4},{7,5},{8,10},{9,11},{10,... | collective-permute-start | bytes 98312 | tf_op jit(solution)/shard_map/ppermute | solution.py:38
  184.4 5.7 %collective-permute-start.37 = (bf16[128,128]{1,0:T(8,128)(2,1)S(1)}, bf16[128,128]{1,0:T(8,128)(2,1)S(1)}, u32[]{:S(2)}, u32[]{:S(2)}) collective-permute-start(bf16[128,128]{1,0:T(8,128)(2,1)S(1)} %get-tuple-element.76.q_ref), channel_id=1, source_target_pairs={{0,6},{1,7},{2,4},{3,5},{4,2},{5,3},{6,0},{7,1},{8,14},{9,15},{10,... | collective-permute-start | bytes 98312 | tf_op jit(solution)/shard_map/ppermute | solution.py:38
  190.1 5.3 %collective-permute-start.38 = (bf16[4,128,128]{2,1,0:T(8,128)(2,1)S(1)}, bf16[4,128,128]{2,1,0:T(8,128)(2,1)S(1)}, u32[]{:S(2)}, u32[]{:S(2)}) collective-permute-start(bf16[4,128,128]{2,1,0:T(8,128)(2,1)S(1)} %pad_maximum_fusion.4.refs_8_), channel_id=1, source_target_pairs={{0,8},{8,0},{16,24},{24,16},{1,9},{9,1},{17,25},{25,17},{2,10},{10... | collective-permute-start | bytes 393224 | tf_op jit(solution)/shard_map/ppermute | solution.py:38
  190.6 5.6 %collective-permute-start.39 = (bf16[4,128,128]{2,1,0:T(8,128)(2,1)S(1)}, bf16[4,128,128]{2,1,0:T(8,128)(2,1)S(1)}, u32[]{:S(2)}, u32[]{:S(2)}) collective-permute-start(bf16[4,128,128]{2,1,0:T(8,128)(2,1)S(1)} %pad_maximum_fusion.4.refs_8_), channel_id=1, source_target_pairs={{0,16},{8,24},{16,0},{24,8},{1,17},{9,25},{17,1},{25,9},{2,18},{10... | collective-permute-start | bytes 393224 | tf_op jit(solution)/shard_map/ppermute | solution.py:38
  191.6 6.0 %collective-permute-start.40 = (bf16[4,128,128]{2,1,0:T(8,128)(2,1)S(1)}, bf16[4,128,128]{2,1,0:T(8,128)(2,1)S(1)}, u32[]{:S(2)}, u32[]{:S(2)}) collective-permute-start(bf16[4,128,128]{2,1,0:T(8,128)(2,1)S(1)} %pad_maximum_fusion.4.refs_8_), channel_id=1, source_target_pairs={{0,24},{8,16},{16,8},{24,0},{1,25},{9,17},{17,9},{25,1},{2,26},{10... | collective-permute-start | bytes 393224 | tf_op jit(solution)/shard_map/ppermute | solution.py:38
  200.6 1.3 collective-permute-start.41
  202.4 1.2 collective-permute-start.42
  203.6 5.8 %collective-permute-start.43 = (bf16[2,128,128]{2,1,0:T(8,128)(2,1)S(1)}, bf16[2,128,128]{2,1,0:T(8,128)(2,1)S(1)}, u32[]{:S(2)}, u32[]{:S(2)}) collective-permute-start(bf16[2,128,128]{2,1,0:T(8,128)(2,1)S(1)} %pad_maximum_fusion.5.refs_8_), channel_id=1, source_target_pairs={{0,4},{1,5},{2,6},{3,7},{4,0},{5,1},{6,2},{7,3},{8,12},{9,13},{10,... | collective-permute-start | bytes 196616 | tf_op jit(solution)/shard_map/ppermute | solution.py:38
  203.7 5.8 %collective-permute-start.44 = (bf16[2,128,128]{2,1,0:T(8,128)(2,1)S(1)}, bf16[2,128,128]{2,1,0:T(8,128)(2,1)S(1)}, u32[]{:S(2)}, u32[]{:S(2)}) collective-permute-start(bf16[2,128,128]{2,1,0:T(8,128)(2,1)S(1)} %pad_maximum_fusion.5.refs_8_), channel_id=1, source_target_pairs={{0,2},{1,3},{2,0},{3,1},{4,6},{5,7},{6,4},{7,5},{8,10},{9,11},{10,... | collective-permute-start | bytes 196616 | tf_op jit(solution)/shard_map/ppermute | solution.py:38
  205.5 6.1 %collective-permute-start.45 = (bf16[2,128,128]{2,1,0:T(8,128)(2,1)S(1)}, bf16[2,128,128]{2,1,0:T(8,128)(2,1)S(1)}, u32[]{:S(2)}, u32[]{:S(2)}) collective-permute-start(bf16[2,128,128]{2,1,0:T(8,128)(2,1)S(1)} %pad_maximum_fusion.5.refs_8_), channel_id=1, source_target_pairs={{0,6},{1,7},{2,4},{3,5},{4,2},{5,3},{6,0},{7,1},{8,14},{9,15},{10,... | collective-permute-start | bytes 196616 | tf_op jit(solution)/shard_map/ppermute | solution.py:38
  213.8 4.9 %collective-permute-start.46 = (f32[128,128]{1,0:T(8,128)S(1)}, f32[128,128]{1,0:T(8,128)S(1)}, u32[]{:S(2)}, u32[]{:S(2)}) collective-permute-start(f32[128,128]{1,0:T(8,128)S(1)} %get-tuple-element.81), channel_id=1, source_target_pairs={{0,8},{8,0},{16,24},{24,16},{1,9},{9,1},{17,25},{25,17},{2,10},{10... | collective-permute-start | bytes 196616 | tf_op jit(solution)/shard_map/ppermute | solution.py:38
  216.5 4.3 %collective-permute-start.47 = (f32[128,128]{1,0:T(8,128)S(1)}, f32[128,128]{1,0:T(8,128)S(1)}, u32[]{:S(2)}, u32[]{:S(2)}) collective-permute-start(f32[128,128]{1,0:T(8,128)S(1)} %get-tuple-element.82), channel_id=1, source_target_pairs={{0,16},{8,24},{16,0},{24,8},{1,17},{9,25},{17,1},{25,9},{2,18},{10... | collective-permute-start | bytes 196616 | tf_op jit(solution)/shard_map/ppermute | solution.py:38
  217.5 5.2 %collective-permute-start.48 = (f32[128,128]{1,0:T(8,128)S(1)}, f32[128,128]{1,0:T(8,128)S(1)}, u32[]{:S(2)}, u32[]{:S(2)}) collective-permute-start(f32[128,128]{1,0:T(8,128)S(1)} %get-tuple-element.83), channel_id=1, source_target_pairs={{0,24},{8,16},{16,8},{24,0},{1,25},{9,17},{17,9},{25,1},{2,26},{10... | collective-permute-start | bytes 196616 | tf_op jit(solution)/shard_map/ppermute | solution.py:38
  227.9 8.6 %collective-permute-start.49 = (bf16[1152,1024]{1,0:T(8,128)(2,1)}, bf16[1152,1024]{1,0:T(8,128)(2,1)}, u32[]{:S(2)}, u32[]{:S(2)}) collective-permute-start(bf16[1152,1024]{1,0:T(8,128)(2,1)} %get-tuple-element.87), channel_id=1, source_target_pairs={{0,1},{1,0},{2,3},{3,2},{4,5},{5,4},{6,7},{7,6},{8,9},{9,8},{10,11... | collective-permute-start | bytes 7077896 | tf_op jit(solution)/shard_map/ppermute | solution.py:38
  235.2 7.1 %collective-permute-start.52 = (bf16[1152,1024]{1,0:T(8,128)(2,1)}, bf16[1152,1024]{1,0:T(8,128)(2,1)}, u32[]{:S(2)}, u32[]{:S(2)}) collective-permute-start(bf16[1152,1024]{1,0:T(8,128)(2,1)} %get-tuple-element.91), channel_id=1, source_target_pairs={{0,1},{1,0},{2,3},{3,2},{4,5},{5,4},{6,7},{7,6},{8,9},{9,8},{10,11... | collective-permute-start | bytes 7077896 | tf_op jit(solution)/shard_map/ppermute | solution.py:38
  241.8 28.2 %collective-permute-start.50 = (bf16[2,4,72,1024]{3,2,1,0:T(8,128)(2,1)}, bf16[2,4,72,1024]{3,2,1,0:T(8,128)(2,1)}, u32[]{:S(2)}, u32[]{:S(2)}) collective-permute-start(bf16[2,4,72,1024]{3,2,1,0:T(8,128)(2,1)} %bitcast.202), channel_id=1, source_target_pairs={{0,8},{8,0},{16,24},{24,16},{1,9},{9,1},{17,25},{25,17},{2,10},{10... | collective-permute-start | bytes 3538952 | tf_op jit(solution)/shard_map/ppermute | solution.py:38
  247.6 29.1 %collective-permute-start.53 = (bf16[2,4,72,1024]{3,2,1,0:T(8,128)(2,1)}, bf16[2,4,72,1024]{3,2,1,0:T(8,128)(2,1)S(1)}, u32[]{:S(2)}, u32[]{:S(2)}) collective-permute-start(bf16[2,4,72,1024]{3,2,1,0:T(8,128)(2,1)} %bitcast.203), channel_id=1, source_target_pairs={{0,16},{8,24},{16,0},{24,8},{1,17},{9,25},{17,1},{25,9},{2,18},{10... | collective-permute-start | bytes 3538952 | tf_op jit(solution)/shard_map/ppermute | solution.py:38
  264.5 16.1 %collective-permute-start.57 = (bf16[2,128,2048]{2,1,0:T(8,128)(2,1)}, bf16[2,128,2048]{2,1,0:T(8,128)(2,1)S(1)}, u32[]{:S(2)}, u32[]{:S(2)}) collective-permute-start(bf16[2,128,2048]{2,1,0:T(8,128)(2,1)} %bitcast.181), channel_id=1, source_target_pairs={{0,1},{1,0},{2,3},{3,2},{4,5},{5,4},{6,7},{7,6},{8,9},{9,8},{10,11... | collective-permute-start | bytes 3145736 | tf_op jit(solution)/shard_map/ppermute | solution.py:38
  272.1 17.6 %collective-permute-start.51 = (bf16[1,4,72,1024]{3,2,1,0:T(8,128)(2,1)S(1)}, bf16[1,4,72,1024]{3,2,1,0:T(8,128)(2,1)}, u32[]{:S(2)}, u32[]{:S(2)}) collective-permute-start(bf16[1,4,72,1024]{3,2,1,0:T(8,128)(2,1)S(1)} %fusion.6), channel_id=1, source_target_pairs={{0,16},{8,24},{16,0},{24,8},{1,17},{9,25},{17,1},{25,9},{2,18},{10... | collective-permute-start | bytes 1769480 | tf_op jit(solution)/shard_map/ppermute | solution.py:38
  277.3 13.7 %collective-permute-start.54 = (bf16[1,4,72,1024]{3,2,1,0:T(8,128)(2,1)S(1)}, bf16[1,4,72,1024]{3,2,1,0:T(8,128)(2,1)S(1)}, u32[]{:S(2)}, u32[]{:S(2)}) collective-permute-start(bf16[1,4,72,1024]{3,2,1,0:T(8,128)(2,1)S(1)} %fusion.7), channel_id=1, source_target_pairs={{0,8},{8,0},{16,24},{24,16},{1,9},{9,1},{17,25},{25,17},{2,10},{10... | collective-permute-start | bytes 1769480 | tf_op jit(solution)/shard_map/ppermute | solution.py:38
  293.4 12.7 %collective-permute-start.55 = (bf16[1,2,72,2048]{3,2,1,0:T(8,128)(2,1)S(1)}, bf16[1,2,72,2048]{3,2,1,0:T(8,128)(2,1)S(1)}, u32[]{:S(2)}, u32[]{:S(2)}) collective-permute-start(bf16[1,2,72,2048]{3,2,1,0:T(8,128)(2,1)S(1)} %fusion.8), channel_id=1, source_target_pairs={{0,2},{1,3},{2,0},{3,1},{4,6},{5,7},{6,4},{7,5},{8,10},{9,11},{10,... | collective-permute-start | bytes 1769480 | tf_op jit(solution)/shard_map/ppermute | solution.py:38
  306.9 12.6 %collective-permute-start.56 = (bf16[1,1,72,2048]{3,2,1,0:T(8,128)(2,1)S(1)}, bf16[1,1,72,2048]{3,2,1,0:T(8,128)(2,1)S(1)}, u32[]{:S(2)}, u32[]{:S(2)}) collective-permute-start(bf16[1,1,72,2048]{3,2,1,0:T(8,128)(2,1)S(1)} %get-tuple-element.109), channel_id=1, source_target_pairs={{0,4},{1,5},{2,6},{3,7},{4,0},{5,1},{6,2},{7,3},{8,12},{9,13},{10,... | collective-permute-start | bytes 884744 | tf_op jit(solution)/shard_map/ppermute | solution.py:38
  320.2 23.9 %all-to-all-start = ((bf16[32,80,128]{2,1,0:T(8,128)(2,1)}), bf16[32,80,128]{2,1,0:T(8,128)(2,1)S(1)}, u32[]{:S(2)}, u32[]{:S(2)}) async-start(bf16[32,80,128]{2,1,0:T(8,128)(2,1)} %after.39), calls=%async_computation | async-start | bytes 1310720 | tf_op jit(solution)/shard_map/all_to_all | solution.py:870
  347.9 24.6 %all-to-all-start.1 = ((bf16[32,96,128]{2,1,0:T(8,128)(2,1)}), bf16[32,96,128]{2,1,0:T(8,128)(2,1)S(1)}, u32[]{:S(2)}, u32[]{:S(2)}) async-start(bf16[32,96,128]{2,1,0:T(8,128)(2,1)} %broadcast_in_dim.74), calls=%async_computation.1 | async-start | bytes 1572864 | tf_op jit(solution)/shard_map/all_to_all | solution.py:879
  (47 other events, 376.1 us)

commit v2 on v1

--- a/solution.py
+++ b/solution.py
@@ -742,7 +742,8 @@
         highest = 1 << (j.bit_length() - 1)
         hop = [passed[j - bit][i] for i, bit in enumerate((highest, lowest, highest))]
         if lowest != highest:
-            hop = [after(h, *g_all[1:]) for h in hop]
+            once = [x for i in passed if i for x in passed[i]]
+            hop = [after(h, *g_all[1:], *[x for x in once if x is not h]) for h in hop]
         passed[j] = [swap(h, "rows", bit) for h, bit in zip(hop, (highest, lowest, highest))]
     for m in range(1, MB):
         for i, j in enumerate(z_order[1:]):

time: 381 us -> 372 us (0.976)
  waiting for transfers between devices: 123 us -> 112 us
  other arithmetic: 28 us -> 34.6 us
    ppermute x58, waiting for transfers between devices: 82.8 us -> 72.4 us  [swap(): return lax.ppermute(x, axis, [(i, i ^ bit) for i in range(size)])]
    convert_element_type x18 -> x24, other arithmetic: 12.8 us -> 17.3 us  [tip(): return x[:8, :128].astype(F32)]
    unnamed x111 -> x109, local copies, waits for them, and re-layouts: 14.5 us -> 13.6 us
  transfers between devices with their start and end apart: 60 -> 60, of which waited for: 37 -> 33; matrix products, arithmetic and copies ran while one was open for 10% -> 12% of each run, Pallas kernels for 24% -> 25%
where the time goes in v2:
time: 372 us; the launch traced here: 371 us
  Pallas kernels  118 us (32%)
  waiting for transfers between devices  112 us (30%)
  starting transfers between devices  71.4 us (19%)
  other arithmetic  34.6 us (9%)
  local copies, waits for them, and re-layouts  25.9 us (7%)
  between operations  4.8 us (1%)
    pallas_call x20, Pallas kernels, run(): pl.pallas_call(kernel, out_shape=tuple(placed) if isinstance(out_shape, t...  118 us
    ppermute x58, waiting for transfers between devices, swap(): return lax.ppermute(x, axis, [(i, i ^ bit) for i in range(size)])  72.4 us
    ppermute x58, starting transfers between devices, swap(): return lax.ppermute(x, axis, [(i, i ^ bit) for i in range(size)])  65.5 us
    all_to_all x1, waiting for transfers between devices, per_device(): got = lax.all_to_all(sent, BOTH, split_axis=0, concat_axis=0, tiled=True)  21.9 us
    all_to_all x1, waiting for transfers between devices, per_device(): got = lax.all_to_all(d_small, BOTH, split_axis=0, concat_axis=0, tiled=True)  17.8 us
    convert_element_type x24, other arithmetic, tip(): return x[:8, :128].astype(F32)  17.3 us
    unnamed x109, local copies, waits for them, and re-layouts  13.6 us
  transfers between devices with their start and end apart: 60, of which 33 were waited for; matrix products, arithmetic and copies ran while one was open for 12% of the time, Pallas kernels for 25%

profile of v2, /device:TPU:0, one launch (start us, length us, event | category | flops | bytes accessed | tf_op | source)
XLA Modules:
  0.0 370.9 jit_solution(14027848704105639547)
XLA Ops:
  1.6 3.0 collective-permute-start
  4.6 1.5 collective-permute-start.1
  9.9 3.9 %masked_tile.1 = (bf16[256,512]{1,0:T(8,128)(2,1)}, bf16[256,512]{1,0:T(8,128)(2,1)}, bf16[256,512]{1,0:T(8,128)(2,1)}, bf16[256,512]{1,0:T(8,128)(2,1)}, bf16[2...) custom-call(s32[2]{0:T(128)S(1)} %pad_add_fusion.1.refs_0_, ...), custom_call_target="tpu_custom_call" | custom-call | tf_op jit(solution)/shard_map/masked_tile/pallas_call | solution.py:127
  13.9 2.2 layer_one.1
  16.8 1.9 collective-permute-start.19
  18.7 2.6 collective-permute-start.16
  21.3 1.6 collective-permute-start.17
  22.9 1.5 collective-permute-start.22
  24.4 2.2 collective-permute-done.19
  27.3 2.9 collective-permute-start.4
  30.2 1.6 collective-permute-start.5
  33.2 3.3 collective-permute-done.16.refs_0_
  40.8 3.2 collective-permute-start.9
  47.3 1.9 collective-permute-done.9
  50.4 1.9 collective-permute-start.12
  55.8 16.4 %collective-permute-done.12.refs_3_ = bf16[4,2,128,128]{3,2,1,0:T(8,128)(2,1)S(1)} collective-permute-done((bf16[4,2,128,128]{3,2,1,0:T(8,128)(2,1)S(1)}, bf16[4,2,128,128]{3,2,1,0:T(8,128)(2,1)S(1)}, u32[]{:S(2)}, u32[]{:S(2)}) %collective-permute-start.12) | collective-permute-done | bytes 262176 | tf_op jit(solution)/shard_map/ppermute | solution.py:38
  74.6 2.3 collective-permute-done.10.refs_1_
  77.5 2.4 collective-permute-start.15
  81.3 2.9 collective-permute-start.13
  92.1 6.0 %collective-permute-done.13.refs_5_.refs_1_ = bf16[256,512]{1,0:T(8,128)(2,1)S(1)} collective-permute-done((bf16[256,512]{1,0:T(8,128)(2,1)}, bf16[256,512]{1,0:T(8,128)(2,1)S(1)}, u32[]{:S(2)}, u32[]{:S(2)}) %collective-permute-start.13) | collective-permute-done | bytes 262176 | tf_op jit(solution)/shard_map/ppermute | solution.py:38
  99.7 2.1 collective-permute-done.26
  102.6 4.6 %join.3.wn_ref.refs_3_ = bf16[1152,2048]{1,0:T(8,128)(2,1)} custom-call(bf16[72,2048]{1,0:T(8,128)(2,1)} %bitcast.189, bf16[144,2048]{1,0:T(8,128)(2,1)} %bitcast.172, bf16[72,2048]{1,0:T(8,128)(2,1)} %bitcast.200, bf16[72,2048]{1,0:T(8,128)(2,1)} %bitcast.197, bf16[144,2048]{1,0:T(8,128)(2,1)} %bitcast.195, bf16[72,2048]{1,0:T(8,128)(2,1)} %bitcast.199, ...), custom_call_target="tpu_custom_call" | custom-call | tf_op jit(solution)/shard_map/join/pallas_call | solution.py:127
  107.7 3.4 convolution_convert_fusion
  111.7 1.6 collective-permute-start.31
  113.2 2.8 collective-permute-start.29
  119.6 14.6 %forward_two.2 = (f32[128,2048]{1,0:T(8,128)}, bf16[128,2048]{1,0:T(8,128)(2,1)}, bf16[2048,2048]{1,0:T(8,128)(2,1)}) custom-call(bf16[4,2,128,128]{3,2,1,0:T(8,128)(2,1)} %copy-done.3, bf16[4,2,128,128]{3,2,1,0:T(8,128)(2,1)} %copy-done.14, bf16[4,2,128,128]{3,2,1,0:T(8,128)(2,1)} %copy-done.13, bf16[4,2,128,128]{3,2,1,0:T(8,128)(2,1)} %copy-done.12, ...), custom_call_target="tpu_custom_call" | custom-call | tf_op jit(solution)/shard_map/forward_two/pallas_call | solution.py:127
  134.8 1.9 collective-permute-done.29.refs_5_.refs_9_
  137.5 14.4 %forward_two.3 = (f32[128,2048]{1,0:T(8,128)}, bf16[128,2048]{1,0:T(8,128)(2,1)}, bf16[2048,2048]{1,0:T(8,128)(2,1)}) custom-call(bf16[4,2,128,128]{3,2,1,0:T(8,128)(2,1)} %copy-done.3, bf16[4,2,128,128]{3,2,1,0:T(8,128)(2,1)} %copy-done.14, bf16[4,2,128,128]{3,2,1,0:T(8,128)(2,1)} %copy-done.13, bf16[4,2,128,128]{3,2,1,0:T(8,128)(2,1)} %copy-done.12, ...), custom_call_target="tpu_custom_call" | custom-call | tf_op jit(solution)/shard_map/forward_two/pallas_call | solution.py:127
  155.4 8.6 %spread_two.1 = (bf16[256,1152]{1,0:T(8,128)(2,1)}, bf16[256,1152]{1,0:T(8,128)(2,1)}) custom-call(f32[128,2048]{1,0:T(8,128)} %get-tuple-element.67.refs_0_, f32[128,2048]{1,0:T(8,128)} %get-tuple-element.71.refs_1_, bf16[128,2048]{1,0:T(8,128)(2,1)} %copy-done.37, bf16[128,2048]{1,0:T(8,128)(2,1)} %copy-done.36, bf16[256,128]{1,0:T(8,128)(2,1)S(1)} %bitcast.181, ...), custom_call_target="tpu_custom_call" | custom-call | tf_op jit(solution)/shard_map/spread_two/pallas_call | solution.py:127
  164.7 8.8 %layer_two.1 = (f32[256,2048]{1,0:T(8,128)}, bf16[256,2048]{1,0:T(8,128)(2,1)}, bf16[128,128]{1,0:T(8,128)(2,1)S(1)}) custom-call(bf16[256,1152]{1,0:T(8,128)(2,1)} %get-tuple-element.74.gn_ref.refs_0_, bf16[256,1152]{1,0:T(8,128)(2,1)} %get-tuple-element.75.gf_ref.refs_9_, bf16[1152,2048]{1,0:T(8,128)(2,1)} %join.3.wn_ref.refs_3_, ...), custom_call_target="tpu_custom_call" | custom-call | tf_op jit(solution)/shard_map/layer_two/pallas_call | solution.py:127
  173.5 2.1 collective-permute-start.36
  175.6 2.3 collective-permute-start.37
  178.3 3.0 collective-permute-done.37
  182.5 2.4 collective-permute-start.40
  184.9 2.0 collective-permute-done.38.refs_9_
  186.8 1.8 collective-permute-done.39.refs_10_
  190.0 2.3 logits_parts.1
  195.4 2.0 collective-permute-start.44
  197.5 2.3 collective-permute-start.45
  201.2 2.3 collective-permute-done.45.refs_11_
  203.5 2.3 d_q_parts.1
  205.8 2.6 collective-permute-start.46
  210.9 1.7 collective-permute-done.47.refs_2_
  213.9 5.3 %d_two.2 = (bf16[256,1024]{1,0:T(8,128)(2,1)}, f32[8,1024]{1,0:T(8,128)S(1)}, f32[1024,128]{1,0:T(8,128)}, bf16[1152,1024]{1,0:T(8,128)(2,1)}) custom-call(f32[128,128]{1,0:T(8,128)S(1)} %get-tuple-element.80.refs_0_, f32[128,128]{1,0:T(8,128)S(1)} %collective-permute-done.46.refs_1_, f32[128,128]{1,0:T(8,128)S(1)} %collective-permute-done.47.refs_2_, ...), custom_call_target="tpu_custom_call" | custom-call | tf_op jit(solution)/shard_map/d_two/pallas_call | solution.py:127
  221.2 5.2 %d_two.3 = (bf16[256,1024]{1,0:T(8,128)(2,1)}, f32[8,1024]{1,0:T(8,128)S(1)}, f32[1024,128]{1,0:T(8,128)}, bf16[1152,1024]{1,0:T(8,128)(2,1)}) custom-call(f32[128,128]{1,0:T(8,128)S(1)} %get-tuple-element.80.refs_0_, f32[128,128]{1,0:T(8,128)S(1)} %collective-permute-done.46.refs_1_, f32[128,128]{1,0:T(8,128)S(1)} %collective-permute-done.47.refs_2_, ...), custom_call_target="tpu_custom_call" | custom-call | tf_op jit(solution)/shard_map/d_two/pallas_call | solution.py:127
  227.8 5.2 %near_part.2 = (f32[576,1024]{1,0:T(8,128)}, bf16[576,1024]{1,0:T(8,128)(2,1)}) custom-call(bf16[256,1152]{1,0:T(8,128)(2,1)} %get-tuple-element.74.gn_ref.refs_0_, bf16[256,1024]{1,0:T(8,128)(2,1)} %get-tuple-element.86.refs_1_.refs_0_, bf16[1152,1024]{1,0:T(8,128)(2,1)} %collective-permute-done.49.refs_2_), custom_call_target="tpu_custom_call" | custom-call | tf_op jit(solution)/shard_map/near_part/pallas_call | solution.py:127
  233.9 5.3 %near_part.3 = (f32[576,1024]{1,0:T(8,128)}, bf16[576,1024]{1,0:T(8,128)(2,1)}) custom-call(bf16[256,1152]{1,0:T(8,128)(2,1)} %get-tuple-element.74.gn_ref.refs_0_, bf16[256,1024]{1,0:T(8,128)(2,1)} %get-tuple-element.90.refs_1_, bf16[1152,1024]{1,0:T(8,128)(2,1)} %collective-permute-done.52.refs_2_), custom_call_target="tpu_custom_call" | custom-call | tf_op jit(solution)/shard_map/near_part/pallas_call | solution.py:127
  244.2 12.3 %d_g_two.1 = bf16[256,2048]{1,0:T(8,128)(2,1)} custom-call(bf16[256,1024]{1,0:T(8,128)(2,1)} %after.35.refs_0_, bf16[256,1024]{1,0:T(8,128)(2,1)} %get-tuple-element.90.refs_1_, s32[2304,1]{1,0:T(8,128)S(1)} %broadcast_add_fusion.refs_2_, bf16[1152,2048]{1,0:T(8,128)(2,1)} %join.3.wn_ref.refs_3_, bf16[1152,2048]{1,0:T(8,128)(2,1)} %collective-permute-done.34.wf_ref.refs_4_), custom_call_target="tpu_custom_call" | custom-call | tf_op jit(solution)/shard_map/d_g_two/pallas_call | solution.py:127
  256.5 4.7 %collective-permute-done.50 = bf16[2,4,72,1024]{3,2,1,0:T(8,128)(2,1)} collective-permute-done((bf16[2,4,72,1024]{3,2,1,0:T(8,128)(2,1)}, bf16[2,4,72,1024]{3,2,1,0:T(8,128)(2,1)}, u32[]{:S(2)}, u32[]{:S(2)}) %collective-permute-start.50) | collective-permute-done | bytes 1179680 | tf_op jit(solution)/shard_map/ppermute | solution.py:38
  261.2 2.0 add_bitcast_fusion.1
  263.2 1.8 collective-permute-start.51
  265.0 3.4 collective-permute-done.53
  268.4 1.8 add_bitcast_fusion
  270.3 1.6 collective-permute-start.54
  274.2 7.8 %backward_one.3 = bf16[128,768]{1,0:T(8,128)(2,1)} custom-call(bf16[4,2,128,128]{3,2,1,0:T(8,128)(2,1)} %copy-done.3, bf16[4,2,128,128]{3,2,1,0:T(8,128)(2,1)} %copy-done.14, bf16[4,2,128,128]{3,2,1,0:T(8,128)(2,1)} %copy-done.13, bf16[4,2,128,128]{3,2,1,0:T(8,128)(2,1)} %copy-done.12, bf16[256,512]{1,0:T(8,128)(2,1)} %get-tuple-element.54.refs_0_.refs_4_, ...), custom_call_target="tpu_custom_call" | custom-call | tf_op jit(solution)/shard_map/backward_one/pallas_call | solution.py:127
  287.3 7.8 %backward_one.4 = bf16[128,768]{1,0:T(8,128)(2,1)} custom-call(bf16[4,2,128,128]{3,2,1,0:T(8,128)(2,1)} %copy-done.3, bf16[4,2,128,128]{3,2,1,0:T(8,128)(2,1)} %copy-done.14, bf16[4,2,128,128]{3,2,1,0:T(8,128)(2,1)} %copy-done.13, bf16[4,2,128,128]{3,2,1,0:T(8,128)(2,1)} %copy-done.12, bf16[256,512]{1,0:T(8,128)(2,1)} %get-tuple-element.54.refs_0_.refs_4_, ...), custom_call_target="tpu_custom_call" | custom-call | tf_op jit(solution)/shard_map/backward_one/pallas_call | solution.py:127
  295.2 4.0 %collective-permute-done.55 = bf16[1,2,72,2048]{3,2,1,0:T(8,128)(2,1)S(1)} collective-permute-done((bf16[1,2,72,2048]{3,2,1,0:T(8,128)(2,1)S(1)}, bf16[1,2,72,2048]{3,2,1,0:T(8,128)(2,1)S(1)}, u32[]{:S(2)}, u32[]{:S(2)}) %collective-permute-start.55) | collective-permute-done | bytes 589856 | tf_op jit(solution)/shard_map/ppermute | solution.py:38
  301.2 6.1 %backward_one.5 = bf16[128,512]{1,0:T(8,128)(2,1)} custom-call(bf16[4,2,128,128]{3,2,1,0:T(8,128)(2,1)} %copy-done.3, bf16[4,2,128,128]{3,2,1,0:T(8,128)(2,1)} %copy-done.14, bf16[4,2,128,128]{3,2,1,0:T(8,128)(2,1)} %copy-done.13, bf16[4,2,128,128]{3,2,1,0:T(8,128)(2,1)} %copy-done.12, bf16[256,512]{1,0:T(8,128)(2,1)} %get-tuple-element.54.refs_0_.refs_4_, ...), custom_call_target="tpu_custom_call" | custom-call | tf_op jit(solution)/shard_map/backward_one/pallas_call | solution.py:127
  310.9 1.5 collective-permute-done.56
  313.1 3.3 all-to-all-start
  317.8 17.8 %all-to-all-done = bf16[32,80,128]{2,1,0:T(8,128)(2,1)S(1)} async-done(((bf16[32,80,128]{2,1,0:T(8,128)(2,1)}), bf16[32,80,128]{2,1,0:T(8,128)(2,1)S(1)}, u32[]{:S(2)}, u32[]{:S(2)}) %all-to-all-start) | async-done | bytes 655392 | tf_op jit(solution)/shard_map/all_to_all | solution.py:871
  339.3 2.6 all-to-all-start.1
  342.0 21.9 %all-to-all-done.1 = bf16[32,96,128]{2,1,0:T(8,128)(2,1)S(1)} async-done(((bf16[32,96,128]{2,1,0:T(8,128)(2,1)}), bf16[32,96,128]{2,1,0:T(8,128)(2,1)S(1)}, u32[]{:S(2)}, u32[]{:S(2)}) %all-to-all-start.1) | async-done | bytes 786464 | tf_op jit(solution)/shard_map/all_to_all | solution.py:880
  367.2 2.6 multiply_subtract_fusion
  (327 shorter events, 84.7 us)
Async XLA Ops:
  1.6 12.3 %collective-permute-start = (bf16[2,128,128]{2,1,0:T(8,128)(2,1)S(1)}, bf16[2,128,128]{2,1,0:T(8,128)(2,1)S(1)}, u32[]{:S(2)}, u32[]{:S(2)}) collective-permute-start(bf16[2,128,128]{2,1,0:T(8,128)(2,1)S(1)} %pad.9.refs_8_), channel_id=1, source_target_pairs={{0,8},{8,0},{16,24},{24,16},{1,9},{9,1},{17,25},{25,17},{2,10},{10... | collective-permute-start | bytes 196616 | tf_op jit(solution)/shard_map/ppermute | solution.py:38
  4.6 9.3 %collective-permute-start.1 = (bf16[2,128,128]{2,1,0:T(8,128)(2,1)S(1)}, bf16[2,128,128]{2,1,0:T(8,128)(2,1)S(1)}, u32[]{:S(2)}, u32[]{:S(2)}) collective-permute-start(bf16[2,128,128]{2,1,0:T(8,128)(2,1)S(1)} %pad.9.refs_8_), channel_id=1, source_target_pairs={{0,16},{8,24},{16,0},{24,8},{1,17},{9,25},{17,1},{25,9},{2,18},{10... | collective-permute-start | bytes 196616 | tf_op jit(solution)/shard_map/ppermute | solution.py:38
  6.1 7.8 %collective-permute-start.2 = (bf16[2,128,128]{2,1,0:T(8,128)(2,1)S(1)}, bf16[2,128,128]{2,1,0:T(8,128)(2,1)S(1)}, u32[]{:S(2)}, u32[]{:S(2)}) collective-permute-start(bf16[2,128,128]{2,1,0:T(8,128)(2,1)S(1)} %pad.9.refs_8_), channel_id=1, source_target_pairs={{0,24},{8,16},{16,8},{24,0},{1,25},{9,17},{17,9},{25,1},{2,26},{10... | collective-permute-start | bytes 196616 | tf_op jit(solution)/shard_map/ppermute | solution.py:38
  16.1 11.1 %collective-permute-start.3 = (f32[4,2,128,128]{3,2,1,0:T(8,128)S(1)}, f32[4,2,128,128]{3,2,1,0:T(8,128)S(1)}, u32[]{:S(2)}, u32[]{:S(2)}) collective-permute-start(f32[4,2,128,128]{3,2,1,0:T(8,128)S(1)} %get-tuple-element.63), channel_id=1, source_target_pairs={{0,1},{1,0},{2,3},{3,2},{4,5},{5,4},{6,7},{7,6},{8,9},{9,8},{10,11... | collective-permute-start | bytes 1572872 | tf_op jit(solution)/shard_map/ppermute | solution.py:38
  16.8 23.9 %copy-start.44 = (f32[2,128]{1,0:T(2,128)S(1)}, f32[2,128]{1,0:T(2,128)}, u32[]{:S(2)}) copy-start(f32[2,128]{1,0:T(2,128)} %param.14) | copy-start | bytes 3076
  16.8 9.8 %collective-permute-start.19 = (bf16[1,72,2048]{2,1,0:T(8,128)(2,1)}, bf16[1,72,2048]{2,1,0:T(8,128)(2,1)S(1)}, u32[]{:S(2)}, u32[]{:S(2)}) collective-permute-start(bf16[1,72,2048]{2,1,0:T(8,128)(2,1)} %after.23.refs_0_), channel_id=1, source_target_pairs={{0,8},{8,0},{16,24},{24,16},{1,9},{9,1},{17,25},{25,17},{2,10},{10... | collective-permute-start | bytes 884744 | tf_op jit(solution)/shard_map/ppermute | solution.py:38
  18.7 17.8 %collective-permute-start.16 = (bf16[1,72,2048]{2,1,0:T(8,128)(2,1)}, bf16[1,72,2048]{2,1,0:T(8,128)(2,1)}, u32[]{:S(2)}, u32[]{:S(2)}) collective-permute-start(bf16[1,72,2048]{2,1,0:T(8,128)(2,1)} %after.23.refs_0_), channel_id=1, source_target_pairs={{0,4},{1,5},{2,6},{3,7},{4,0},{5,1},{6,2},{7,3},{8,12},{9,13},{10,... | collective-permute-start | bytes 884744 | tf_op jit(solution)/shard_map/ppermute | solution.py:38
  21.3 15.4 %collective-permute-start.17 = (bf16[1,72,2048]{2,1,0:T(8,128)(2,1)}, bf16[1,72,2048]{2,1,0:T(8,128)(2,1)S(1)}, u32[]{:S(2)}, u32[]{:S(2)}) collective-permute-start(bf16[1,72,2048]{2,1,0:T(8,128)(2,1)} %after.23.refs_0_), channel_id=1, source_target_pairs={{0,2},{1,3},{2,0},{3,1},{4,6},{5,7},{6,4},{7,5},{8,10},{9,11},{10,... | collective-permute-start | bytes 884744 | tf_op jit(solution)/shard_map/ppermute | solution.py:38
  22.9 9.0 %collective-permute-start.22 = (bf16[1,72,2048]{2,1,0:T(8,128)(2,1)}, bf16[1,72,2048]{2,1,0:T(8,128)(2,1)S(1)}, u32[]{:S(2)}, u32[]{:S(2)}) collective-permute-start(bf16[1,72,2048]{2,1,0:T(8,128)(2,1)} %after.23.refs_0_), channel_id=1, source_target_pairs={{0,16},{8,24},{16,0},{24,8},{1,17},{9,25},{17,1},{25,9},{2,18},{10... | collective-permute-start | bytes 884744 | tf_op jit(solution)/shard_map/ppermute | solution.py:38
  27.3 11.9 %collective-permute-start.4 = (bf16[2,128,128]{2,1,0:T(8,128)(2,1)S(1)}, bf16[2,128,128]{2,1,0:T(8,128)(2,1)S(1)}, u32[]{:S(2)}, u32[]{:S(2)}) collective-permute-start(bf16[2,128,128]{2,1,0:T(8,128)(2,1)S(1)} %get-tuple-element.112), channel_id=1, source_target_pairs={{0,4},{1,5},{2,6},{3,7},{4,0},{5,1},{6,2},{7,3},{8,12},{9,13},{10,... | collective-permute-start | bytes 196616 | tf_op jit(solution)/shard_map/ppermute | solution.py:38
  30.2 9.0 %collective-permute-start.5 = (bf16[2,128,128]{2,1,0:T(8,128)(2,1)S(1)}, bf16[2,128,128]{2,1,0:T(8,128)(2,1)S(1)}, u32[]{:S(2)}, u32[]{:S(2)}) collective-permute-start(bf16[2,128,128]{2,1,0:T(8,128)(2,1)S(1)} %get-tuple-element.114), channel_id=1, source_target_pairs={{0,2},{1,3},{2,0},{3,1},{4,6},{5,7},{6,4},{7,5},{8,10},{9,11},{10,... | collective-permute-start | bytes 196616 | tf_op jit(solution)/shard_map/ppermute | solution.py:38
  31.8 8.8 %collective-permute-start.6 = (bf16[2,128,128]{2,1,0:T(8,128)(2,1)S(1)}, bf16[2,128,128]{2,1,0:T(8,128)(2,1)S(1)}, u32[]{:S(2)}, u32[]{:S(2)}) collective-permute-start(bf16[2,128,128]{2,1,0:T(8,128)(2,1)S(1)} %get-tuple-element.113), channel_id=1, source_target_pairs={{0,6},{1,7},{2,4},{3,5},{4,2},{5,3},{6,0},{7,1},{8,14},{9,15},{10,... | collective-permute-start | bytes 196616 | tf_op jit(solution)/shard_map/ppermute | solution.py:38
  36.5 18.1 %collective-permute-start.18 = (bf16[1,72,2048]{2,1,0:T(8,128)(2,1)}, bf16[1,72,2048]{2,1,0:T(8,128)(2,1)S(1)}, u32[]{:S(2)}, u32[]{:S(2)}) collective-permute-start(bf16[1,72,2048]{2,1,0:T(8,128)(2,1)} %collective-permute-done.16.refs_0_), channel_id=1, source_target_pairs={{0,2},{1,3},{2,0},{3,1},{4,6},{5,7},{6,4},{7,5},{8,10},{9,11},{10,... | collective-permute-start | bytes 884744 | tf_op jit(solution)/shard_map/ppermute | solution.py:38
  40.8 8.4 %collective-permute-start.9 = (bf16[2,128,128]{2,1,0:T(8,128)(2,1)S(1)}, bf16[2,128,128]{2,1,0:T(8,128)(2,1)S(1)}, u32[]{:S(2)}, u32[]{:S(2)}) collective-permute-start(bf16[2,128,128]{2,1,0:T(8,128)(2,1)S(1)} %fusion.19), channel_id=1, source_target_pairs={{0,6},{1,7},{2,4},{3,5},{4,2},{5,3},{6,0},{7,1},{8,14},{9,15},{10,... | collective-permute-start | bytes 196616 | tf_op jit(solution)/shard_map/ppermute | solution.py:38
  43.9 6.4 %collective-permute-start.8 = (bf16[2,128,128]{2,1,0:T(8,128)(2,1)S(1)}, bf16[2,128,128]{2,1,0:T(8,128)(2,1)S(1)}, u32[]{:S(2)}, u32[]{:S(2)}) collective-permute-start(bf16[2,128,128]{2,1,0:T(8,128)(2,1)S(1)} %fusion.19), channel_id=1, source_target_pairs={{0,2},{1,3},{2,0},{3,1},{4,6},{5,7},{6,4},{7,5},{8,10},{9,11},{10,... | collective-permute-start | bytes 196616 | tf_op jit(solution)/shard_map/ppermute | solution.py:38
  44.3 6.0 %collective-permute-start.7 = (bf16[2,128,128]{2,1,0:T(8,128)(2,1)S(1)}, bf16[2,128,128]{2,1,0:T(8,128)(2,1)S(1)}, u32[]{:S(2)}, u32[]{:S(2)}) collective-permute-start(bf16[2,128,128]{2,1,0:T(8,128)(2,1)S(1)} %fusion.19), channel_id=1, source_target_pairs={{0,4},{1,5},{2,6},{3,7},{4,0},{5,1},{6,2},{7,3},{8,12},{9,13},{10,... | collective-permute-start | bytes 196616 | tf_op jit(solution)/shard_map/ppermute | solution.py:38
  45.8 40.2 %collective-permute-start.23 = (bf16[2,72,2048]{2,1,0:T(8,128)(2,1)}, bf16[2,72,2048]{2,1,0:T(8,128)(2,1)S(1)}, u32[]{:S(2)}, u32[]{:S(2)}) collective-permute-start(bf16[2,72,2048]{2,1,0:T(8,128)(2,1)} %after.25), channel_id=1, source_target_pairs={{0,16},{8,24},{16,0},{24,8},{1,17},{9,25},{17,1},{25,9},{2,18},{10... | collective-permute-start | bytes 1769480 | tf_op jit(solution)/shard_map/ppermute | solution.py:38
  49.2 36.9 %collective-permute-start.20 = (bf16[2,72,2048]{2,1,0:T(8,128)(2,1)}, bf16[2,72,2048]{2,1,0:T(8,128)(2,1)S(1)}, u32[]{:S(2)}, u32[]{:S(2)}) collective-permute-start(bf16[2,72,2048]{2,1,0:T(8,128)(2,1)} %after.25), channel_id=1, source_target_pairs={{0,8},{8,0},{16,24},{24,16},{1,9},{9,1},{17,25},{25,17},{2,10},{10... | collective-permute-start | bytes 1769480 | tf_op jit(solution)/shard_map/ppermute | solution.py:38
  50.4 37.0 %copy-start.3 = (bf16[4,2,128,128]{3,2,1,0:T(8,128)(2,1)}, bf16[4,2,128,128]{3,2,1,0:T(8,128)(2,1)S(1)}, u32[]{:S(2)}) copy-start(bf16[4,2,128,128]{3,2,1,0:T(8,128)(2,1)S(1)} %pad_maximum_fusion.3.refs_0_) | copy-start | bytes 786436
  50.4 21.9 %collective-permute-start.12 = (bf16[4,2,128,128]{3,2,1,0:T(8,128)(2,1)S(1)}, bf16[4,2,128,128]{3,2,1,0:T(8,128)(2,1)S(1)}, u32[]{:S(2)}, u32[]{:S(2)}) collective-permute-start(bf16[4,2,128,128]{3,2,1,0:T(8,128)(2,1)S(1)} %pad_maximum_fusion.3.refs_0_), channel_id=1, source_target_pairs={{0,24},{8,16},{16,8},{24,0},{1,25},{9,17},{17,9},{25,1},{2,26},{10... | collective-permute-start | bytes 786440 | tf_op jit(solution)/shard_map/ppermute | solution.py:38
  52.3 21.1 %collective-permute-start.11 = (bf16[4,2,128,128]{3,2,1,0:T(8,128)(2,1)S(1)}, bf16[4,2,128,128]{3,2,1,0:T(8,128)(2,1)S(1)}, u32[]{:S(2)}, u32[]{:S(2)}) collective-permute-start(bf16[4,2,128,128]{3,2,1,0:T(8,128)(2,1)S(1)} %pad_maximum_fusion.3.refs_0_), channel_id=1, source_target_pairs={{0,16},{8,24},{16,0},{24,8},{1,17},{9,25},{17,1},{25,9},{2,18},{10... | collective-permute-start | bytes 786440 | tf_op jit(solution)/shard_map/ppermute | solution.py:38
  54.6 22.3 %collective-permute-start.10 = (bf16[4,2,128,128]{3,2,1,0:T(8,128)(2,1)S(1)}, bf16[4,2,128,128]{3,2,1,0:T(8,128)(2,1)S(1)}, u32[]{:S(2)}, u32[]{:S(2)}) collective-permute-start(bf16[4,2,128,128]{3,2,1,0:T(8,128)(2,1)S(1)} %pad_maximum_fusion.3.refs_0_), channel_id=1, source_target_pairs={{0,8},{8,0},{16,24},{24,16},{1,9},{9,1},{17,25},{25,17},{2,10},{10... | collective-permute-start | bytes 786440 | tf_op jit(solution)/shard_map/ppermute | solution.py:38
  72.2 8.3 %collective-permute-start.21 = (bf16[1,72,2048]{2,1,0:T(8,128)(2,1)}, bf16[1,72,2048]{2,1,0:T(8,128)(2,1)S(1)}, u32[]{:S(2)}, u32[]{:S(2)}) collective-permute-start(bf16[1,72,2048]{2,1,0:T(8,128)(2,1)} %after.26), channel_id=1, source_target_pairs={{0,8},{8,0},{16,24},{24,16},{1,9},{9,1},{17,25},{25,17},{2,10},{10... | collective-permute-start | bytes 884744 | tf_op jit(solution)/shard_map/ppermute | solution.py:38
  73.4 7.9 %collective-permute-start.24 = (bf16[1,72,2048]{2,1,0:T(8,128)(2,1)}, bf16[1,72,2048]{2,1,0:T(8,128)(2,1)}, u32[]{:S(2)}, u32[]{:S(2)}) collective-permute-start(bf16[1,72,2048]{2,1,0:T(8,128)(2,1)} %after.26), channel_id=1, source_target_pairs={{0,16},{8,24},{16,0},{24,8},{1,17},{9,25},{17,1},{25,9},{2,18},{10... | collective-permute-start | bytes 884744 | tf_op jit(solution)/shard_map/ppermute | solution.py:38
  77.5 12.8 %collective-permute-start.15 = (bf16[256,512]{1,0:T(8,128)(2,1)}, bf16[256,512]{1,0:T(8,128)(2,1)S(1)}, u32[]{:S(2)}, u32[]{:S(2)}) collective-permute-start(bf16[256,512]{1,0:T(8,128)(2,1)} %after.22), channel_id=1, source_target_pairs={{0,6},{1,7},{2,4},{3,5},{4,2},{5,3},{6,0},{7,1},{8,14},{9,15},{10,... | collective-permute-start | bytes 786440 | tf_op jit(solution)/shard_map/ppermute | solution.py:38
  80.5 11.0 %collective-permute-start.14 = (bf16[256,512]{1,0:T(8,128)(2,1)}, bf16[256,512]{1,0:T(8,128)(2,1)S(1)}, u32[]{:S(2)}, u32[]{:S(2)}) collective-permute-start(bf16[256,512]{1,0:T(8,128)(2,1)} %after.21), channel_id=1, source_target_pairs={{0,2},{1,3},{2,0},{3,1},{4,6},{5,7},{6,4},{7,5},{8,10},{9,11},{10,... | collective-permute-start | bytes 786440 | tf_op jit(solution)/shard_map/ppermute | solution.py:38
  81.3 16.9 %collective-permute-start.13 = (bf16[256,512]{1,0:T(8,128)(2,1)}, bf16[256,512]{1,0:T(8,128)(2,1)S(1)}, u32[]{:S(2)}, u32[]{:S(2)}) collective-permute-start(bf16[256,512]{1,0:T(8,128)(2,1)} %after.20), channel_id=1, source_target_pairs={{0,4},{1,5},{2,6},{3,7},{4,0},{5,1},{6,2},{7,3},{8,12},{9,13},{10,... | collective-permute-start | bytes 786440 | tf_op jit(solution)/shard_map/ppermute | solution.py:38
  87.3 11.5 %collective-permute-start.27 = (bf16[1,72,2048]{2,1,0:T(8,128)(2,1)}, bf16[1,72,2048]{2,1,0:T(8,128)(2,1)}, u32[]{:S(2)}, u32[]{:S(2)}) collective-permute-start(bf16[1,72,2048]{2,1,0:T(8,128)(2,1)} %after.29), channel_id=1, source_target_pairs={{0,16},{8,24},{16,0},{24,8},{1,17},{9,25},{17,1},{25,9},{2,18},{10... | collective-permute-start | bytes 884744 | tf_op jit(solution)/shard_map/ppermute | solution.py:38
  89.7 12.1 %collective-permute-start.26 = (bf16[2,72,2048]{2,1,0:T(8,128)(2,1)}, bf16[2,72,2048]{2,1,0:T(8,128)(2,1)S(1)}, u32[]{:S(2)}, u32[]{:S(2)}) collective-permute-start(bf16[2,72,2048]{2,1,0:T(8,128)(2,1)} %after.28), channel_id=1, source_target_pairs={{0,8},{8,0},{16,24},{24,16},{1,9},{9,1},{17,25},{25,17},{2,10},{10... | collective-permute-start | bytes 1769480 | tf_op jit(solution)/shard_map/ppermute | solution.py:38
  90.3 9.4 %collective-permute-start.25 = (bf16[1,72,2048]{2,1,0:T(8,128)(2,1)}, bf16[1,72,2048]{2,1,0:T(8,128)(2,1)S(1)}, u32[]{:S(2)}, u32[]{:S(2)}) collective-permute-start(bf16[1,72,2048]{2,1,0:T(8,128)(2,1)} %after.27), channel_id=1, source_target_pairs={{0,16},{8,24},{16,0},{24,8},{1,17},{9,25},{17,1},{25,9},{2,18},{10... | collective-permute-start | bytes 884744 | tf_op jit(solution)/shard_map/ppermute | solution.py:38
  107.3 56.7 %collective-permute-start.34 = (bf16[1152,2048]{1,0:T(8,128)(2,1)}, bf16[1152,2048]{1,0:T(8,128)(2,1)}, u32[]{:S(2)}, u32[]{:S(2)}) collective-permute-start(bf16[1152,2048]{1,0:T(8,128)(2,1)} %join.3.wn_ref.refs_3_), channel_id=1, source_target_pairs={{0,1},{1,0},{2,3},{3,2},{4,5},{5,4},{6,7},{7,6},{8,9},{9,8},{10,11... | collective-permute-start | bytes 14155784 | tf_op jit(solution)/shard_map/ppermute | solution.py:38
  111.1 5.1 %collective-permute-start.28 = (bf16[160,2048]{1,0:T(8,128)(2,1)S(1)}, bf16[160,2048]{1,0:T(8,128)(2,1)S(1)}, u32[]{:S(2)}, u32[]{:S(2)}) collective-permute-start(bf16[160,2048]{1,0:T(8,128)(2,1)S(1)} %convolution_convert_fusion), channel_id=1, source_target_pairs={{0,1},{1,0},{2,3},{3,2},{4,5},{5,4},{6,7},{7,6},{8,9},{9,8},{10,11... | collective-permute-start | bytes 1966088 | tf_op jit(solution)/shard_map/ppermute | solution.py:38
  111.7 23.1 %collective-permute-start.31 = (bf16[256,512]{1,0:T(8,128)(2,1)}, bf16[256,512]{1,0:T(8,128)(2,1)S(1)}, u32[]{:S(2)}, u32[]{:S(2)}) collective-permute-start(bf16[256,512]{1,0:T(8,128)(2,1)} %after.32), channel_id=1, source_target_pairs={{0,6},{1,7},{2,4},{3,5},{4,2},{5,3},{6,0},{7,1},{8,14},{9,15},{10,... | collective-permute-start | bytes 786440 | tf_op jit(solution)/shard_map/ppermute | solution.py:38
  113.2 21.6 %collective-permute-start.30 = (bf16[256,512]{1,0:T(8,128)(2,1)}, bf16[256,512]{1,0:T(8,128)(2,1)S(1)}, u32[]{:S(2)}, u32[]{:S(2)}) collective-permute-start(bf16[256,512]{1,0:T(8,128)(2,1)} %after.31), channel_id=1, source_target_pairs={{0,2},{1,3},{2,0},{3,1},{4,6},{5,7},{6,4},{7,5},{8,10},{9,11},{10,... | collective-permute-start | bytes 786440 | tf_op jit(solution)/shard_map/ppermute | solution.py:38
  113.2 23.5 %collective-permute-start.29 = (bf16[256,512]{1,0:T(8,128)(2,1)}, bf16[256,512]{1,0:T(8,128)(2,1)S(1)}, u32[]{:S(2)}, u32[]{:S(2)}) collective-permute-start(bf16[256,512]{1,0:T(8,128)(2,1)} %after.30), channel_id=1, source_target_pairs={{0,4},{1,5},{2,6},{3,7},{4,0},{5,1},{6,2},{7,3},{8,12},{9,13},{10,... | collective-permute-start | bytes 786440 | tf_op jit(solution)/shard_map/ppermute | solution.py:38
  119.6 32.3 %copy-start.5 = (bf16[2048,128]{1,0:T(8,128)(2,1)}, bf16[2048,128]{1,0:T(8,128)(2,1)S(1)}, u32[]{:S(2)}) copy-start(bf16[2048,128]{1,0:T(8,128)(2,1)S(1)} %pad_maximum_fusion.1.w3_ref.refs_8_) | copy-start | bytes 1572868
  151.9 2.2 collective-permute-start.33
  152.0 2.6 collective-permute-start.32
  173.5 4.8 %collective-permute-start.35 = (bf16[128,128]{1,0:T(8,128)(2,1)S(1)}, bf16[128,128]{1,0:T(8,128)(2,1)S(1)}, u32[]{:S(2)}, u32[]{:S(2)}) collective-permute-start(bf16[128,128]{1,0:T(8,128)(2,1)S(1)} %get-tuple-element.76.q_ref), channel_id=1, source_target_pairs={{0,4},{1,5},{2,6},{3,7},{4,0},{5,1},{6,2},{7,3},{8,12},{9,13},{10,... | collective-permute-start | bytes 98312 | tf_op jit(solution)/shard_map/ppermute | solution.py:38
  173.5 4.8 %collective-permute-start.36 = (bf16[128,128]{1,0:T(8,128)(2,1)S(1)}, bf16[128,128]{1,0:T(8,128)(2,1)S(1)}, u32[]{:S(2)}, u32[]{:S(2)}) collective-permute-start(bf16[128,128]{1,0:T(8,128)(2,1)S(1)} %get-tuple-element.76.q_ref), channel_id=1, source_target_pairs={{0,2},{1,3},{2,0},{3,1},{4,6},{5,7},{6,4},{7,5},{8,10},{9,11},{10,... | collective-permute-start | bytes 98312 | tf_op jit(solution)/shard_map/ppermute | solution.py:38
  175.6 5.7 %collective-permute-start.37 = (bf16[128,128]{1,0:T(8,128)(2,1)S(1)}, bf16[128,128]{1,0:T(8,128)(2,1)S(1)}, u32[]{:S(2)}, u32[]{:S(2)}) collective-permute-start(bf16[128,128]{1,0:T(8,128)(2,1)S(1)} %get-tuple-element.76.q_ref), channel_id=1, source_target_pairs={{0,6},{1,7},{2,4},{3,5},{4,2},{5,3},{6,0},{7,1},{8,14},{9,15},{10,... | collective-permute-start | bytes 98312 | tf_op jit(solution)/shard_map/ppermute | solution.py:38
  181.3 5.5 %collective-permute-start.38 = (bf16[4,128,128]{2,1,0:T(8,128)(2,1)S(1)}, bf16[4,128,128]{2,1,0:T(8,128)(2,1)S(1)}, u32[]{:S(2)}, u32[]{:S(2)}) collective-permute-start(bf16[4,128,128]{2,1,0:T(8,128)(2,1)S(1)} %pad_maximum_fusion.4.refs_8_), channel_id=1, source_target_pairs={{0,8},{8,0},{16,24},{24,16},{1,9},{9,1},{17,25},{25,17},{2,10},{10... | collective-permute-start | bytes 393224 | tf_op jit(solution)/shard_map/ppermute | solution.py:38
  181.9 6.8 %collective-permute-start.39 = (bf16[4,128,128]{2,1,0:T(8,128)(2,1)S(1)}, bf16[4,128,128]{2,1,0:T(8,128)(2,1)S(1)}, u32[]{:S(2)}, u32[]{:S(2)}) collective-permute-start(bf16[4,128,128]{2,1,0:T(8,128)(2,1)S(1)} %pad_maximum_fusion.4.refs_8_), channel_id=1, source_target_pairs={{0,16},{8,24},{16,0},{24,8},{1,17},{9,25},{17,1},{25,9},{2,18},{10... | collective-permute-start | bytes 393224 | tf_op jit(solution)/shard_map/ppermute | solution.py:38
  182.5 6.2 %collective-permute-start.40 = (bf16[4,128,128]{2,1,0:T(8,128)(2,1)S(1)}, bf16[4,128,128]{2,1,0:T(8,128)(2,1)S(1)}, u32[]{:S(2)}, u32[]{:S(2)}) collective-permute-start(bf16[4,128,128]{2,1,0:T(8,128)(2,1)S(1)} %pad_maximum_fusion.4.refs_8_), channel_id=1, source_target_pairs={{0,24},{8,16},{16,8},{24,0},{1,25},{9,17},{17,9},{25,1},{2,26},{10... | collective-permute-start | bytes 393224 | tf_op jit(solution)/shard_map/ppermute | solution.py:38
  192.3 1.3 collective-permute-start.41
  194.1 25.0 %copy-start.1 = (bf16[128,128]{1,0:T(8,128)(2,1)}, bf16[128,128]{1,0:T(8,128)(2,1)S(1)}, u32[]{:S(2)}) copy-start(bf16[128,128]{1,0:T(8,128)(2,1)S(1)} %get-tuple-element.79.refs_4_.refs_0_) | copy-start | bytes 98308
  194.1 1.2 collective-permute-start.42
  195.3 5.9 %collective-permute-start.43 = (bf16[2,128,128]{2,1,0:T(8,128)(2,1)S(1)}, bf16[2,128,128]{2,1,0:T(8,128)(2,1)S(1)}, u32[]{:S(2)}, u32[]{:S(2)}) collective-permute-start(bf16[2,128,128]{2,1,0:T(8,128)(2,1)S(1)} %pad_maximum_fusion.5.refs_8_), channel_id=1, source_target_pairs={{0,4},{1,5},{2,6},{3,7},{4,0},{5,1},{6,2},{7,3},{8,12},{9,13},{10,... | collective-permute-start | bytes 196616 | tf_op jit(solution)/shard_map/ppermute | solution.py:38
  195.4 5.8 %collective-permute-start.44 = (bf16[2,128,128]{2,1,0:T(8,128)(2,1)S(1)}, bf16[2,128,128]{2,1,0:T(8,128)(2,1)S(1)}, u32[]{:S(2)}, u32[]{:S(2)}) collective-permute-start(bf16[2,128,128]{2,1,0:T(8,128)(2,1)S(1)} %pad_maximum_fusion.5.refs_8_), channel_id=1, source_target_pairs={{0,2},{1,3},{2,0},{3,1},{4,6},{5,7},{6,4},{7,5},{8,10},{9,11},{10,... | collective-permute-start | bytes 196616 | tf_op jit(solution)/shard_map/ppermute | solution.py:38
  197.5 6.1 %collective-permute-start.45 = (bf16[2,128,128]{2,1,0:T(8,128)(2,1)S(1)}, bf16[2,128,128]{2,1,0:T(8,128)(2,1)S(1)}, u32[]{:S(2)}, u32[]{:S(2)}) collective-permute-start(bf16[2,128,128]{2,1,0:T(8,128)(2,1)S(1)} %pad_maximum_fusion.5.refs_8_), channel_id=1, source_target_pairs={{0,6},{1,7},{2,4},{3,5},{4,2},{5,3},{6,0},{7,1},{8,14},{9,15},{10,... | collective-permute-start | bytes 196616 | tf_op jit(solution)/shard_map/ppermute | solution.py:38
  205.8 5.2 %collective-permute-start.46 = (f32[128,128]{1,0:T(8,128)S(1)}, f32[128,128]{1,0:T(8,128)S(1)}, u32[]{:S(2)}, u32[]{:S(2)}) collective-permute-start(f32[128,128]{1,0:T(8,128)S(1)} %get-tuple-element.81), channel_id=1, source_target_pairs={{0,8},{8,0},{16,24},{24,16},{1,9},{9,1},{17,25},{25,17},{2,10},{10... | collective-permute-start | bytes 196616 | tf_op jit(solution)/shard_map/ppermute | solution.py:38
  208.4 4.3 %collective-permute-start.47 = (f32[128,128]{1,0:T(8,128)S(1)}, f32[128,128]{1,0:T(8,128)S(1)}, u32[]{:S(2)}, u32[]{:S(2)}) collective-permute-start(f32[128,128]{1,0:T(8,128)S(1)} %get-tuple-element.82), channel_id=1, source_target_pairs={{0,16},{8,24},{16,0},{24,8},{1,17},{9,25},{17,1},{25,9},{2,18},{10... | collective-permute-start | bytes 196616 | tf_op jit(solution)/shard_map/ppermute | solution.py:38
  208.7 5.2 %collective-permute-start.48 = (f32[128,128]{1,0:T(8,128)S(1)}, f32[128,128]{1,0:T(8,128)S(1)}, u32[]{:S(2)}, u32[]{:S(2)}) collective-permute-start(f32[128,128]{1,0:T(8,128)S(1)} %get-tuple-element.83), channel_id=1, source_target_pairs={{0,24},{8,16},{16,8},{24,0},{1,25},{9,17},{17,9},{25,1},{2,26},{10... | collective-permute-start | bytes 196616 | tf_op jit(solution)/shard_map/ppermute | solution.py:38
  219.1 8.6 %collective-permute-start.49 = (bf16[1152,1024]{1,0:T(8,128)(2,1)}, bf16[1152,1024]{1,0:T(8,128)(2,1)}, u32[]{:S(2)}, u32[]{:S(2)}) collective-permute-start(bf16[1152,1024]{1,0:T(8,128)(2,1)} %get-tuple-element.87), channel_id=1, source_target_pairs={{0,1},{1,0},{2,3},{3,2},{4,5},{5,4},{6,7},{7,6},{8,9},{9,8},{10,11... | collective-permute-start | bytes 7077896 | tf_op jit(solution)/shard_map/ppermute | solution.py:38
  226.4 7.5 %collective-permute-start.52 = (bf16[1152,1024]{1,0:T(8,128)(2,1)}, bf16[1152,1024]{1,0:T(8,128)(2,1)}, u32[]{:S(2)}, u32[]{:S(2)}) collective-permute-start(bf16[1152,1024]{1,0:T(8,128)(2,1)} %get-tuple-element.91), channel_id=1, source_target_pairs={{0,1},{1,0},{2,3},{3,2},{4,5},{5,4},{6,7},{7,6},{8,9},{9,8},{10,11... | collective-permute-start | bytes 7077896 | tf_op jit(solution)/shard_map/ppermute | solution.py:38
  233.0 28.2 %collective-permute-start.50 = (bf16[2,4,72,1024]{3,2,1,0:T(8,128)(2,1)}, bf16[2,4,72,1024]{3,2,1,0:T(8,128)(2,1)}, u32[]{:S(2)}, u32[]{:S(2)}) collective-permute-start(bf16[2,4,72,1024]{3,2,1,0:T(8,128)(2,1)} %bitcast.212), channel_id=1, source_target_pairs={{0,8},{8,0},{16,24},{24,16},{1,9},{9,1},{17,25},{25,17},{2,10},{10... | collective-permute-start | bytes 3538952 | tf_op jit(solution)/shard_map/ppermute | solution.py:38
  239.2 29.2 %collective-permute-start.53 = (bf16[2,4,72,1024]{3,2,1,0:T(8,128)(2,1)}, bf16[2,4,72,1024]{3,2,1,0:T(8,128)(2,1)}, u32[]{:S(2)}, u32[]{:S(2)}) collective-permute-start(bf16[2,4,72,1024]{3,2,1,0:T(8,128)(2,1)} %bitcast.213), channel_id=1, source_target_pairs={{0,16},{8,24},{16,0},{24,8},{1,17},{9,25},{17,1},{25,9},{2,18},{10... | collective-permute-start | bytes 3538952 | tf_op jit(solution)/shard_map/ppermute | solution.py:38
  256.5 16.7 %collective-permute-start.57 = (bf16[2,128,2048]{2,1,0:T(8,128)(2,1)}, bf16[2,128,2048]{2,1,0:T(8,128)(2,1)S(1)}, u32[]{:S(2)}, u32[]{:S(2)}) collective-permute-start(bf16[2,128,2048]{2,1,0:T(8,128)(2,1)} %bitcast.185), channel_id=1, source_target_pairs={{0,1},{1,0},{2,3},{3,2},{4,5},{5,4},{6,7},{7,6},{8,9},{9,8},{10,11... | collective-permute-start | bytes 3145736 | tf_op jit(solution)/shard_map/ppermute | solution.py:38
  263.2 18.8 %collective-permute-start.51 = (bf16[1,4,72,1024]{3,2,1,0:T(8,128)(2,1)S(1)}, bf16[1,4,72,1024]{3,2,1,0:T(8,128)(2,1)S(1)}, u32[]{:S(2)}, u32[]{:S(2)}) collective-permute-start(bf16[1,4,72,1024]{3,2,1,0:T(8,128)(2,1)S(1)} %fusion.6), channel_id=1, source_target_pairs={{0,16},{8,24},{16,0},{24,8},{1,17},{9,25},{17,1},{25,9},{2,18},{10... | collective-permute-start | bytes 1769480 | tf_op jit(solution)/shard_map/ppermute | solution.py:38
  270.3 13.0 %collective-permute-start.54 = (bf16[1,4,72,1024]{3,2,1,0:T(8,128)(2,1)S(1)}, bf16[1,4,72,1024]{3,2,1,0:T(8,128)(2,1)}, u32[]{:S(2)}, u32[]{:S(2)}) collective-permute-start(bf16[1,4,72,1024]{3,2,1,0:T(8,128)(2,1)S(1)} %fusion.7), channel_id=1, source_target_pairs={{0,8},{8,0},{16,24},{24,16},{1,9},{9,1},{17,25},{25,17},{2,10},{10... | collective-permute-start | bytes 1769480 | tf_op jit(solution)/shard_map/ppermute | solution.py:38
  286.6 12.6 %collective-permute-start.55 = (bf16[1,2,72,2048]{3,2,1,0:T(8,128)(2,1)S(1)}, bf16[1,2,72,2048]{3,2,1,0:T(8,128)(2,1)S(1)}, u32[]{:S(2)}, u32[]{:S(2)}) collective-permute-start(bf16[1,2,72,2048]{3,2,1,0:T(8,128)(2,1)S(1)} %fusion.8), channel_id=1, source_target_pairs={{0,2},{1,3},{2,0},{3,1},{4,6},{5,7},{6,4},{7,5},{8,10},{9,11},{10,... | collective-permute-start | bytes 1769480 | tf_op jit(solution)/shard_map/ppermute | solution.py:38
  300.0 12.5 %collective-permute-start.56 = (bf16[1,1,72,2048]{3,2,1,0:T(8,128)(2,1)S(1)}, bf16[1,1,72,2048]{3,2,1,0:T(8,128)(2,1)S(1)}, u32[]{:S(2)}, u32[]{:S(2)}) collective-permute-start(bf16[1,1,72,2048]{3,2,1,0:T(8,128)(2,1)S(1)} %get-tuple-element.109), channel_id=1, source_target_pairs={{0,4},{1,5},{2,6},{3,7},{4,0},{5,1},{6,2},{7,3},{8,12},{9,13},{10,... | collective-permute-start | bytes 884744 | tf_op jit(solution)/shard_map/ppermute | solution.py:38
  313.1 22.4 %all-to-all-start = ((bf16[32,80,128]{2,1,0:T(8,128)(2,1)}), bf16[32,80,128]{2,1,0:T(8,128)(2,1)S(1)}, u32[]{:S(2)}, u32[]{:S(2)}) async-start(bf16[32,80,128]{2,1,0:T(8,128)(2,1)} %after.39), calls=%async_computation | async-start | bytes 1310720 | tf_op jit(solution)/shard_map/all_to_all | solution.py:871
  339.3 24.6 %all-to-all-start.1 = ((bf16[32,96,128]{2,1,0:T(8,128)(2,1)}), bf16[32,96,128]{2,1,0:T(8,128)(2,1)S(1)}, u32[]{:S(2)}, u32[]{:S(2)}) async-start(bf16[32,96,128]{2,1,0:T(8,128)(2,1)} %broadcast_in_dim.74), calls=%async_computation.1 | async-start | bytes 1572864 | tf_op jit(solution)/shard_map/all_to_all | solution.py:880
  (46 other events, 308.4 us)

commit v3 on v2

--- a/solution.py
+++ b/solution.py
@@ -224,7 +224,8 @@
     square = z * z
     t = jnp.tanh(z * (GELU_ONE + GELU_THREE * square))
     slope = z * (GELU_ONE + (3 * GELU_THREE) * square)
-    return z + z * t, (1.0 + t) * (1.0 + (1.0 - t) * slope)
+    above = 1.0 + t
+    return z * above, above * (1.0 + (1.0 - t) * slope)
 
 
 def forward_kernel(n_z, n_rows, m, *refs):
@@ -521,7 +522,8 @@
     )(*d_q, d_s, diag, z_two, h_two, w3, g_far)
 
 
-def near_kernel(keep, send, rows, g_ref, dz_ref, got_ref, keep_ref, send_ref):
+def near_kernel(keep, send, rows, g_ref, dz_ref, got_ref, keep_ref, send_ref, done_ref):
+    done_ref[...] = jnp.zeros_like(done_ref)
     total = mm_t(g_ref[...], dz_ref[...]) + got_ref[...].astype(F32)
     for out_ref, picks in ((keep_ref, keep), (send_ref, send)):
         for i, j in enumerate(picks):
@@ -537,9 +539,9 @@
     return call(
         lambda *refs: near_kernel(keep, send, rows, *refs),
         "near_part",
-        (shaped((n_near // 2, span)), shaped((n_near // 2, span), BF16)),
+        (shaped((n_near // 2, span)), shaped((n_near // 2, span), BF16), shaped((8, LANES))),
         [pl.BlockSpec(g_near.shape, lambda f: (0, 0)), column(g_near.shape[0]), column(n_near)],
-        (column(n_near // 2), column(n_near // 2)),
+        (column(n_near // 2), column(n_near // 2), pl.BlockSpec((8, LANES), lambda f: (0, 0))),
         grid=(span // wide,),
     )(g_near, d_zb, got)
 
@@ -811,15 +813,14 @@
     work = []
     for k, bits in enumerate((row_bits, turned)):
         lo, hi = k * half, (k + 1) * half
-        wait = d_s if k == 0 else after(d_s, work[0]["dz"])
-        d_zb, d_b, d_w3, d_far = d_two(d_q, wait, diag, z_two, h_two, w_third, g_far, lo, hi)
+        d_zb, d_b, d_w3, d_far = d_two(d_q, d_s, diag, z_two, h_two, w_third, g_far, lo, hi)
         item = {"bits": bits, "dz": d_zb, "db": d_b, "dw3": d_w3}
         item["got"] = swap(d_far, "cols", 1)
         item["orders"] = {"rows": [j for j in range(n_rows) if not j & bits[0]], "cols": z_order}
         item["to"] = ("rows", bits[0])
         work.append(item)
     for item in work:
-        kept, send = near_part(g_near, item["dz"], item["got"], n_rows, item["bits"][0])
+        kept, send, item["done"] = near_part(g_near, item["dz"], item["got"], n_rows, item["bits"][0])
         item["kept"], item["send"] = (x.reshape(n_rows // 2, n_z, slot, half) for x in (kept, send))
     d_zb = [item["dz"] for item in work]
     d_bias_two = jnp.concatenate([jnp.sum(item["db"], axis=0) for item in work])
@@ -828,7 +829,7 @@
 
     n_cuts = 3
     cuts = [0, 3 * (HID // 8), 6 * (HID // 8), HID]
-    d_zb[0] = after(d_zb[0], *[item["send"] for item in work])
+    d_zb[0] = after(d_zb[0], *[item["done"] for item in work])
     d_g_near = d_g_two(d_zb, [(0, half), (half, HID)], which[:, None], near, far).reshape(MB, ns, HID)
     d_g_far = swap(d_g_near, "cols", 1)
     d_first = []

time: 372 us -> 370 us (level)
  other arithmetic: 34.6 us -> 30.3 us
    convert_element_type x24 -> x21, other arithmetic: 17.3 us -> 14.1 us  [tip(): return x[:8, :128].astype(F32)]
    unnamed x109 -> x105, local copies, waits for them, and re-layouts: 13.6 us -> 14.7 us
  transfers between devices with their start and end apart: 60 -> 60, of which waited for: 33 -> 30; matrix products, arithmetic and copies ran while one was open for 12% -> 11% of each run, Pallas kernels for 25% -> 25%
where the time goes in v3:
time: 370 us; the launch traced here: 369 us
  Pallas kernels  118 us (32%)
  waiting for transfers between devices  115 us (31%)
  starting transfers between devices  70.1 us (19%)
  other arithmetic  30.3 us (8%)
  local copies, waits for them, and re-layouts  27 us (7%)
  between operations  4.84 us (1%)
    pallas_call x20, Pallas kernels, run(): pl.pallas_call(kernel, out_shape=tuple(placed) if isinstance(out_shape, t...  118 us
    ppermute x58, waiting for transfers between devices, swap(): return lax.ppermute(x, axis, [(i, i ^ bit) for i in range(size)])  75.3 us
    ppermute x58, starting transfers between devices, swap(): return lax.ppermute(x, axis, [(i, i ^ bit) for i in range(size)])  64.9 us
    all_to_all x1, waiting for transfers between devices, per_device(): got = lax.all_to_all(sent, BOTH, split_axis=0, concat_axis=0, tiled=True)  21.9 us
    all_to_all x1, waiting for transfers between devices, per_device(): got = lax.all_to_all(d_small, BOTH, split_axis=0, concat_axis=0, tiled=True)  17.8 us
    unnamed x105, local copies, waits for them, and re-layouts  14.7 us
    convert_element_type x21, other arithmetic, tip(): return x[:8, :128].astype(F32)  14.1 us
  transfers between devices with their start and end apart: 60, of which 30 were waited for; matrix products, arithmetic and copies ran while one was open for 11% of the time, Pallas kernels for 25%

profile of v3, /device:TPU:0, one launch (start us, length us, event | category | flops | bytes accessed | tf_op | source)
XLA Modules:
  0.0 368.6 jit_solution(13089493552609914074)
XLA Ops:
  1.6 3.0 collective-permute-start
  4.6 1.5 collective-permute-start.1
  9.9 4.0 %masked_tile.1 = (bf16[256,512]{1,0:T(8,128)(2,1)}, bf16[256,512]{1,0:T(8,128)(2,1)}, bf16[256,512]{1,0:T(8,128)(2,1)}, bf16[256,512]{1,0:T(8,128)(2,1)}, bf16[2...) custom-call(s32[2]{0:T(128)S(1)} %pad_add_fusion.1.refs_0_, ...), custom_call_target="tpu_custom_call" | custom-call | tf_op jit(solution)/shard_map/masked_tile/pallas_call | solution.py:127
  13.9 2.2 layer_one.1
  16.8 2.0 collective-permute-start.22
  18.8 1.5 collective-permute-start.19
  20.3 1.6 collective-permute-start.17
  21.8 2.6 collective-permute-start.16
  24.4 2.2 collective-permute-done.22
  27.4 3.9 %collective-permute-start.6 = (bf16[2,128,128]{2,1,0:T(8,128)(2,1)S(1)}, bf16[2,128,128]{2,1,0:T(8,128)(2,1)S(1)}, u32[]{:S(2)}, u32[]{:S(2)}) collective-permute-start(bf16[2,128,128]{2,1,0:T(8,128)(2,1)S(1)} %get-tuple-element.117), channel_id=1, source_target_pairs={{0,6},{1,7},{2,4},{3,5},{4,2},{5,3},{6,0},{7,1},{8,14},{9,15},{10,... | collective-permute-start | bytes 196616 | tf_op jit(solution)/shard_map/ppermute | solution.py:38
  33.3 7.6 %collective-permute-done.16.refs_0_ = bf16[1,72,2048]{2,1,0:T(8,128)(2,1)} collective-permute-done((bf16[1,72,2048]{2,1,0:T(8,128)(2,1)}, bf16[1,72,2048]{2,1,0:T(8,128)(2,1)}, u32[]{:S(2)}, u32[]{:S(2)}) %collective-permute-start.16) | collective-permute-done | bytes 294944 | tf_op jit(solution)/shard_map/ppermute | solution.py:38
  44.2 3.2 collective-permute-start.9
  49.5 2.9 collective-permute-done.9
  52.8 1.7 collective-permute-done.7
  57.2 2.6 collective-permute-start.12
  59.8 11.6 %collective-permute-done.10.refs_1_ = bf16[4,2,128,128]{3,2,1,0:T(8,128)(2,1)S(1)} collective-permute-done((bf16[4,2,128,128]{3,2,1,0:T(8,128)(2,1)S(1)}, bf16[4,2,128,128]{3,2,1,0:T(8,128)(2,1)S(1)}, u32[]{:S(2)}, u32[]{:S(2)}) %collective-permute-start.10) | collective-permute-done | bytes 262176 | tf_op jit(solution)/shard_map/ppermute | solution.py:38
  72.2 3.9 %collective-permute-done.11.refs_2_ = bf16[4,2,128,128]{3,2,1,0:T(8,128)(2,1)S(1)} collective-permute-done((bf16[4,2,128,128]{3,2,1,0:T(8,128)(2,1)S(1)}, bf16[4,2,128,128]{3,2,1,0:T(8,128)(2,1)S(1)}, u32[]{:S(2)}, u32[]{:S(2)}) %collective-permute-start.11) | collective-permute-done | bytes 262176 | tf_op jit(solution)/shard_map/ppermute | solution.py:38
  76.1 2.6 collective-permute-start.24
  81.0 1.7 copy.99.refs_0_
  83.9 3.4 collective-permute-start.15
  90.9 1.5 collective-permute-start.26
  92.4 4.2 %collective-permute-done.13.refs_5_.refs_1_ = bf16[256,512]{1,0:T(8,128)(2,1)S(1)} collective-permute-done((bf16[256,512]{1,0:T(8,128)(2,1)}, bf16[256,512]{1,0:T(8,128)(2,1)S(1)}, u32[]{:S(2)}, u32[]{:S(2)}) %collective-permute-start.13) | collective-permute-done | bytes 262176 | tf_op jit(solution)/shard_map/ppermute | solution.py:38
  96.6 1.5 collective-permute-start.27
  99.9 3.6 collective-permute-done.27
  104.5 4.6 %join.3.wn_ref.refs_3_ = bf16[1152,2048]{1,0:T(8,128)(2,1)} custom-call(bf16[72,2048]{1,0:T(8,128)(2,1)} %bitcast.189, bf16[144,2048]{1,0:T(8,128)(2,1)} %bitcast.172, bf16[72,2048]{1,0:T(8,128)(2,1)} %bitcast.25.refs_2_, bf16[72,2048]{1,0:T(8,128)(2,1)} %bitcast.197, bf16[144,2048]{1,0:T(8,128)(2,1)} %bitcast.195, bf16[72,2048]{1,0:T(8,128)(2,1)} %bitcast.28.refs_5_, ...), custom_call_target="tpu_custom_call" | custom-call | tf_op jit(solution)/shard_map/join/pallas_call | solution.py:127
  109.5 3.4 convolution_convert_fusion
  113.6 2.7 collective-permute-start.30
  116.3 1.7 collective-permute-start.31
  121.4 14.1 %forward_two.2 = (f32[128,2048]{1,0:T(8,128)}, bf16[128,2048]{1,0:T(8,128)(2,1)}, bf16[2048,2048]{1,0:T(8,128)(2,1)}) custom-call(bf16[4,2,128,128]{3,2,1,0:T(8,128)(2,1)} %copy-done.3, bf16[4,2,128,128]{3,2,1,0:T(8,128)(2,1)} %copy-done.12, bf16[4,2,128,128]{3,2,1,0:T(8,128)(2,1)} %copy-done.13, bf16[4,2,128,128]{3,2,1,0:T(8,128)(2,1)} %copy-done.14, ...), custom_call_target="tpu_custom_call" | custom-call | tf_op jit(solution)/shard_map/forward_two/pallas_call | solution.py:127
  137.8 13.9 %forward_two.3 = (f32[128,2048]{1,0:T(8,128)}, bf16[128,2048]{1,0:T(8,128)(2,1)}, bf16[2048,2048]{1,0:T(8,128)(2,1)}) custom-call(bf16[4,2,128,128]{3,2,1,0:T(8,128)(2,1)} %copy-done.3, bf16[4,2,128,128]{3,2,1,0:T(8,128)(2,1)} %copy-done.12, bf16[4,2,128,128]{3,2,1,0:T(8,128)(2,1)} %copy-done.13, bf16[4,2,128,128]{3,2,1,0:T(8,128)(2,1)} %copy-done.14, ...), custom_call_target="tpu_custom_call" | custom-call | tf_op jit(solution)/shard_map/forward_two/pallas_call | solution.py:127
  154.7 8.6 %spread_two.1 = (bf16[256,1152]{1,0:T(8,128)(2,1)}, bf16[256,1152]{1,0:T(8,128)(2,1)}) custom-call(f32[128,2048]{1,0:T(8,128)} %get-tuple-element.69.refs_0_, f32[128,2048]{1,0:T(8,128)} %get-tuple-element.73.refs_1_, bf16[128,2048]{1,0:T(8,128)(2,1)} %copy-done.34, bf16[128,2048]{1,0:T(8,128)(2,1)} %copy-done.35, bf16[256,128]{1,0:T(8,128)(2,1)S(1)} %bitcast.181, ...), custom_call_target="tpu_custom_call" | custom-call | tf_op jit(solution)/shard_map/spread_two/pallas_call | solution.py:127
  164.0 8.8 %layer_two.1 = (f32[256,2048]{1,0:T(8,128)}, bf16[256,2048]{1,0:T(8,128)(2,1)}, bf16[128,128]{1,0:T(8,128)(2,1)S(1)}) custom-call(bf16[256,1152]{1,0:T(8,128)(2,1)} %get-tuple-element.76.gn_ref.refs_0_, bf16[256,1152]{1,0:T(8,128)(2,1)} %get-tuple-element.77.gf_ref.refs_9_, bf16[1152,2048]{1,0:T(8,128)(2,1)} %join.3.wn_ref.refs_3_, ...), custom_call_target="tpu_custom_call" | custom-call | tf_op jit(solution)/shard_map/layer_two/pallas_call | solution.py:127
  172.8 2.2 collective-permute-start.37
  178.9 2.5 collective-permute-done.35
  182.0 1.9 collective-permute-start.39
  185.0 1.9 collective-permute-done.38.refs_9_
  188.1 1.6 collective-permute-done.40.refs_11_
  190.5 2.3 logits_parts.1
  197.2 1.9 collective-permute-start.44
  200.3 2.7 collective-permute-done.43.refs_9_
  203.0 2.2 collective-permute-done.45.refs_11_
  205.2 2.3 d_q_parts.1
  208.3 1.5 collective-permute-start.47
  212.8 2.2 collective-permute-done.48.refs_3_
  215.0 5.3 %d_two.3 = (bf16[256,1024]{1,0:T(8,128)(2,1)}, f32[8,1024]{1,0:T(8,128)S(1)}, f32[1024,128]{1,0:T(8,128)}, bf16[1152,1024]{1,0:T(8,128)(2,1)}) custom-call(f32[128,128]{1,0:T(8,128)S(1)} %get-tuple-element.82.refs_0_, f32[128,128]{1,0:T(8,128)S(1)} %collective-permute-done.46.refs_1_, f32[128,128]{1,0:T(8,128)S(1)} %collective-permute-done.47.refs_2_, ...), custom_call_target="tpu_custom_call" | custom-call | tf_op jit(solution)/shard_map/d_two/pallas_call | solution.py:127
  220.2 5.3 %d_two.2 = (bf16[256,1024]{1,0:T(8,128)(2,1)}, f32[8,1024]{1,0:T(8,128)S(1)}, f32[1024,128]{1,0:T(8,128)}, bf16[1152,1024]{1,0:T(8,128)(2,1)}) custom-call(f32[128,128]{1,0:T(8,128)S(1)} %get-tuple-element.82.refs_0_, f32[128,128]{1,0:T(8,128)S(1)} %collective-permute-done.46.refs_1_, f32[128,128]{1,0:T(8,128)S(1)} %collective-permute-done.47.refs_2_, ...), custom_call_target="tpu_custom_call" | custom-call | tf_op jit(solution)/shard_map/d_two/pallas_call | solution.py:127
  226.7 5.3 %near_part.3 = (f32[576,1024]{1,0:T(8,128)}, bf16[576,1024]{1,0:T(8,128)(2,1)}, f32[8,128]{1,0:T(8,128)S(1)}) custom-call(bf16[256,1152]{1,0:T(8,128)(2,1)} %get-tuple-element.76.gn_ref.refs_0_, bf16[256,1024]{1,0:T(8,128)(2,1)} %get-tuple-element.92.refs_1_, bf16[1152,1024]{1,0:T(8,128)(2,1)} %collective-permute-done.52.refs_2_), custom_call_target="tpu_custom_call" | custom-call | tf_op jit(solution)/shard_map/near_part/pallas_call | solution.py:127
  233.6 5.1 %near_part.2 = (f32[576,1024]{1,0:T(8,128)}, bf16[576,1024]{1,0:T(8,128)(2,1)}, f32[8,128]{1,0:T(8,128)S(1)}) custom-call(bf16[256,1152]{1,0:T(8,128)(2,1)} %get-tuple-element.76.gn_ref.refs_0_, bf16[256,1024]{1,0:T(8,128)(2,1)} %get-tuple-element.88.refs_1_.refs_0_, bf16[1152,1024]{1,0:T(8,128)(2,1)} %collective-permute-done.49.refs_2_), custom_call_target="tpu_custom_call" | custom-call | tf_op jit(solution)/shard_map/near_part/pallas_call | solution.py:127
  239.4 1.4 collective-permute-start.50
  242.3 12.5 %d_g_two.1 = bf16[256,2048]{1,0:T(8,128)(2,1)} custom-call(bf16[256,1024]{1,0:T(8,128)(2,1)} %after.33.refs_0_, bf16[256,1024]{1,0:T(8,128)(2,1)} %get-tuple-element.92.refs_1_, s32[2304,1]{1,0:T(8,128)S(1)} %broadcast_add_fusion.refs_2_, bf16[1152,2048]{1,0:T(8,128)(2,1)} %join.3.wn_ref.refs_3_, bf16[1152,2048]{1,0:T(8,128)(2,1)} %collective-permute-done.34.wf_ref.refs_4_), custom_call_target="tpu_custom_call" | custom-call | tf_op jit(solution)/shard_map/d_g_two/pallas_call | solution.py:127
  254.8 6.0 %collective-permute-done.53 = bf16[2,4,72,1024]{3,2,1,0:T(8,128)(2,1)} collective-permute-done((bf16[2,4,72,1024]{3,2,1,0:T(8,128)(2,1)}, bf16[2,4,72,1024]{3,2,1,0:T(8,128)(2,1)}, u32[]{:S(2)}, u32[]{:S(2)}) %collective-permute-start.53) | collective-permute-done | bytes 1179680 | tf_op jit(solution)/shard_map/ppermute | solution.py:38
  260.8 2.0 add_bitcast_fusion
  262.8 1.5 collective-permute-start.54
  264.3 4.1 %collective-permute-done.50 = bf16[2,4,72,1024]{3,2,1,0:T(8,128)(2,1)S(1)} collective-permute-done((bf16[2,4,72,1024]{3,2,1,0:T(8,128)(2,1)}, bf16[2,4,72,1024]{3,2,1,0:T(8,128)(2,1)S(1)}, u32[]{:S(2)}, u32[]{:S(2)}) %collective-permute-start.50) | collective-permute-done | bytes 1179680 | tf_op jit(solution)/shard_map/ppermute | solution.py:38
  272.6 7.8 %backward_one.3 = bf16[128,768]{1,0:T(8,128)(2,1)} custom-call(bf16[4,2,128,128]{3,2,1,0:T(8,128)(2,1)} %copy-done.3, bf16[4,2,128,128]{3,2,1,0:T(8,128)(2,1)} %copy-done.12, bf16[4,2,128,128]{3,2,1,0:T(8,128)(2,1)} %copy-done.13, bf16[4,2,128,128]{3,2,1,0:T(8,128)(2,1)} %copy-done.14, bf16[256,512]{1,0:T(8,128)(2,1)} %get-tuple-element.56.refs_0_.refs_4_, ...), custom_call_target="tpu_custom_call" | custom-call | tf_op jit(solution)/shard_map/backward_one/pallas_call | solution.py:127
  285.2 7.8 %backward_one.4 = bf16[128,768]{1,0:T(8,128)(2,1)} custom-call(bf16[4,2,128,128]{3,2,1,0:T(8,128)(2,1)} %copy-done.3, bf16[4,2,128,128]{3,2,1,0:T(8,128)(2,1)} %copy-done.12, bf16[4,2,128,128]{3,2,1,0:T(8,128)(2,1)} %copy-done.13, bf16[4,2,128,128]{3,2,1,0:T(8,128)(2,1)} %copy-done.14, bf16[256,512]{1,0:T(8,128)(2,1)} %get-tuple-element.56.refs_0_.refs_4_, ...), custom_call_target="tpu_custom_call" | custom-call | tf_op jit(solution)/shard_map/backward_one/pallas_call | solution.py:127
  293.0 4.8 %collective-permute-done.55 = bf16[1,2,72,2048]{3,2,1,0:T(8,128)(2,1)S(1)} collective-permute-done((bf16[1,2,72,2048]{3,2,1,0:T(8,128)(2,1)S(1)}, bf16[1,2,72,2048]{3,2,1,0:T(8,128)(2,1)S(1)}, u32[]{:S(2)}, u32[]{:S(2)}) %collective-permute-start.55) | collective-permute-done | bytes 589856 | tf_op jit(solution)/shard_map/ppermute | solution.py:38
  298.0 1.5 collective-permute-start.56
  300.2 6.1 %backward_one.5 = bf16[128,512]{1,0:T(8,128)(2,1)} custom-call(bf16[4,2,128,128]{3,2,1,0:T(8,128)(2,1)} %copy-done.3, bf16[4,2,128,128]{3,2,1,0:T(8,128)(2,1)} %copy-done.12, bf16[4,2,128,128]{3,2,1,0:T(8,128)(2,1)} %copy-done.13, bf16[4,2,128,128]{3,2,1,0:T(8,128)(2,1)} %copy-done.14, bf16[256,512]{1,0:T(8,128)(2,1)} %get-tuple-element.56.refs_0_.refs_4_, ...), custom_call_target="tpu_custom_call" | custom-call | tf_op jit(solution)/shard_map/backward_one/pallas_call | solution.py:127
  312.0 2.6 all-to-all-start
  316.0 17.8 %all-to-all-done = bf16[32,80,128]{2,1,0:T(8,128)(2,1)S(1)} async-done(((bf16[32,80,128]{2,1,0:T(8,128)(2,1)}), bf16[32,80,128]{2,1,0:T(8,128)(2,1)S(1)}, u32[]{:S(2)}, u32[]{:S(2)}) %all-to-all-start) | async-done | bytes 655392 | tf_op jit(solution)/shard_map/all_to_all | solution.py:872
  337.6 2.6 all-to-all-start.1
  340.2 21.9 %all-to-all-done.1 = bf16[32,96,128]{2,1,0:T(8,128)(2,1)S(1)} async-done(((bf16[32,96,128]{2,1,0:T(8,128)(2,1)}), bf16[32,96,128]{2,1,0:T(8,128)(2,1)S(1)}, u32[]{:S(2)}, u32[]{:S(2)}) %all-to-all-start.1) | async-done | bytes 786464 | tf_op jit(solution)/shard_map/all_to_all | solution.py:881
  364.9 2.6 multiply_subtract_fusion
  (319 shorter events, 80.2 us)
Async XLA Ops:
  1.6 12.3 %collective-permute-start = (bf16[2,128,128]{2,1,0:T(8,128)(2,1)S(1)}, bf16[2,128,128]{2,1,0:T(8,128)(2,1)S(1)}, u32[]{:S(2)}, u32[]{:S(2)}) collective-permute-start(bf16[2,128,128]{2,1,0:T(8,128)(2,1)S(1)} %pad.9.refs_8_), channel_id=1, source_target_pairs={{0,8},{8,0},{16,24},{24,16},{1,9},{9,1},{17,25},{25,17},{2,10},{10... | collective-permute-start | bytes 196616 | tf_op jit(solution)/shard_map/ppermute | solution.py:38
  4.6 9.3 %collective-permute-start.1 = (bf16[2,128,128]{2,1,0:T(8,128)(2,1)S(1)}, bf16[2,128,128]{2,1,0:T(8,128)(2,1)S(1)}, u32[]{:S(2)}, u32[]{:S(2)}) collective-permute-start(bf16[2,128,128]{2,1,0:T(8,128)(2,1)S(1)} %pad.9.refs_8_), channel_id=1, source_target_pairs={{0,16},{8,24},{16,0},{24,8},{1,17},{9,25},{17,1},{25,9},{2,18},{10... | collective-permute-start | bytes 196616 | tf_op jit(solution)/shard_map/ppermute | solution.py:38
  6.1 7.8 %collective-permute-start.2 = (bf16[2,128,128]{2,1,0:T(8,128)(2,1)S(1)}, bf16[2,128,128]{2,1,0:T(8,128)(2,1)S(1)}, u32[]{:S(2)}, u32[]{:S(2)}) collective-permute-start(bf16[2,128,128]{2,1,0:T(8,128)(2,1)S(1)} %pad.9.refs_8_), channel_id=1, source_target_pairs={{0,24},{8,16},{16,8},{24,0},{1,25},{9,17},{17,9},{25,1},{2,26},{10... | collective-permute-start | bytes 196616 | tf_op jit(solution)/shard_map/ppermute | solution.py:38
  16.1 28.0 %copy-start.43 = (f32[2,128]{1,0:T(2,128)S(1)}, f32[2,128]{1,0:T(2,128)}, u32[]{:S(2)}) copy-start(f32[2,128]{1,0:T(2,128)} %param.14) | copy-start | bytes 3076
  16.1 11.2 %collective-permute-start.3 = (f32[4,2,128,128]{3,2,1,0:T(8,128)S(1)}, f32[4,2,128,128]{3,2,1,0:T(8,128)S(1)}, u32[]{:S(2)}, u32[]{:S(2)}) collective-permute-start(f32[4,2,128,128]{3,2,1,0:T(8,128)S(1)} %get-tuple-element.65), channel_id=1, source_target_pairs={{0,1},{1,0},{2,3},{3,2},{4,5},{5,4},{6,7},{7,6},{8,9},{9,8},{10,11... | collective-permute-start | bytes 1572872 | tf_op jit(solution)/shard_map/ppermute | solution.py:38
  16.8 9.8 %collective-permute-start.22 = (bf16[1,72,2048]{2,1,0:T(8,128)(2,1)}, bf16[1,72,2048]{2,1,0:T(8,128)(2,1)S(1)}, u32[]{:S(2)}, u32[]{:S(2)}) collective-permute-start(bf16[1,72,2048]{2,1,0:T(8,128)(2,1)} %after.22.refs_0_), channel_id=1, source_target_pairs={{0,16},{8,24},{16,0},{24,8},{1,17},{9,25},{17,1},{25,9},{2,18},{10... | collective-permute-start | bytes 884744 | tf_op jit(solution)/shard_map/ppermute | solution.py:38
  18.8 12.5 %collective-permute-start.19 = (bf16[1,72,2048]{2,1,0:T(8,128)(2,1)}, bf16[1,72,2048]{2,1,0:T(8,128)(2,1)S(1)}, u32[]{:S(2)}, u32[]{:S(2)}) collective-permute-start(bf16[1,72,2048]{2,1,0:T(8,128)(2,1)} %after.22.refs_0_), channel_id=1, source_target_pairs={{0,8},{8,0},{16,24},{24,16},{1,9},{9,1},{17,25},{25,17},{2,10},{10... | collective-permute-start | bytes 884744 | tf_op jit(solution)/shard_map/ppermute | solution.py:38
  20.3 21.2 %collective-permute-start.17 = (bf16[1,72,2048]{2,1,0:T(8,128)(2,1)}, bf16[1,72,2048]{2,1,0:T(8,128)(2,1)S(1)}, u32[]{:S(2)}, u32[]{:S(2)}) collective-permute-start(bf16[1,72,2048]{2,1,0:T(8,128)(2,1)} %after.22.refs_0_), channel_id=1, source_target_pairs={{0,2},{1,3},{2,0},{3,1},{4,6},{5,7},{6,4},{7,5},{8,10},{9,11},{10,... | collective-permute-start | bytes 884744 | tf_op jit(solution)/shard_map/ppermute | solution.py:38
  21.8 19.1 %collective-permute-start.16 = (bf16[1,72,2048]{2,1,0:T(8,128)(2,1)}, bf16[1,72,2048]{2,1,0:T(8,128)(2,1)}, u32[]{:S(2)}, u32[]{:S(2)}) collective-permute-start(bf16[1,72,2048]{2,1,0:T(8,128)(2,1)} %after.22.refs_0_), channel_id=1, source_target_pairs={{0,4},{1,5},{2,6},{3,7},{4,0},{5,1},{6,2},{7,3},{8,12},{9,13},{10,... | collective-permute-start | bytes 884744 | tf_op jit(solution)/shard_map/ppermute | solution.py:38
  27.4 16.7 %collective-permute-start.6 = (bf16[2,128,128]{2,1,0:T(8,128)(2,1)S(1)}, bf16[2,128,128]{2,1,0:T(8,128)(2,1)S(1)}, u32[]{:S(2)}, u32[]{:S(2)}) collective-permute-start(bf16[2,128,128]{2,1,0:T(8,128)(2,1)S(1)} %get-tuple-element.117), channel_id=1, source_target_pairs={{0,6},{1,7},{2,4},{3,5},{4,2},{5,3},{6,0},{7,1},{8,14},{9,15},{10,... | collective-permute-start | bytes 196616 | tf_op jit(solution)/shard_map/ppermute | solution.py:38
  31.3 12.8 %collective-permute-start.5 = (bf16[2,128,128]{2,1,0:T(8,128)(2,1)S(1)}, bf16[2,128,128]{2,1,0:T(8,128)(2,1)S(1)}, u32[]{:S(2)}, u32[]{:S(2)}) collective-permute-start(bf16[2,128,128]{2,1,0:T(8,128)(2,1)S(1)} %get-tuple-element.118), channel_id=1, source_target_pairs={{0,2},{1,3},{2,0},{3,1},{4,6},{5,7},{6,4},{7,5},{8,10},{9,11},{10,... | collective-permute-start | bytes 196616 | tf_op jit(solution)/shard_map/ppermute | solution.py:38
  31.3 48.7 %copy-start.28 = (bf16[1,72,2048]{2,1,0:T(8,128)(2,1)}, bf16[1,72,2048]{2,1,0:T(8,128)(2,1)S(1)}, u32[]{:S(2)}) copy-start(bf16[1,72,2048]{2,1,0:T(8,128)(2,1)S(1)} %collective-permute-done.19) | copy-start | bytes 884740
  31.3 12.8 %collective-permute-start.4 = (bf16[2,128,128]{2,1,0:T(8,128)(2,1)S(1)}, bf16[2,128,128]{2,1,0:T(8,128)(2,1)S(1)}, u32[]{:S(2)}, u32[]{:S(2)}) collective-permute-start(bf16[2,128,128]{2,1,0:T(8,128)(2,1)S(1)} %get-tuple-element.116), channel_id=1, source_target_pairs={{0,4},{1,5},{2,6},{3,7},{4,0},{5,1},{6,2},{7,3},{8,12},{9,13},{10,... | collective-permute-start | bytes 196616 | tf_op jit(solution)/shard_map/ppermute | solution.py:38
  40.9 16.3 %collective-permute-start.18 = (bf16[1,72,2048]{2,1,0:T(8,128)(2,1)}, bf16[1,72,2048]{2,1,0:T(8,128)(2,1)}, u32[]{:S(2)}, u32[]{:S(2)}) collective-permute-start(bf16[1,72,2048]{2,1,0:T(8,128)(2,1)} %collective-permute-done.16.refs_0_), channel_id=1, source_target_pairs={{0,2},{1,3},{2,0},{3,1},{4,6},{5,7},{6,4},{7,5},{8,10},{9,11},{10,... | collective-permute-start | bytes 884744 | tf_op jit(solution)/shard_map/ppermute | solution.py:38
  44.2 8.2 %collective-permute-start.9 = (bf16[2,128,128]{2,1,0:T(8,128)(2,1)S(1)}, bf16[2,128,128]{2,1,0:T(8,128)(2,1)S(1)}, u32[]{:S(2)}, u32[]{:S(2)}) collective-permute-start(bf16[2,128,128]{2,1,0:T(8,128)(2,1)S(1)} %fusion.19), channel_id=1, source_target_pairs={{0,6},{1,7},{2,4},{3,5},{4,2},{5,3},{6,0},{7,1},{8,14},{9,15},{10,... | collective-permute-start | bytes 196616 | tf_op jit(solution)/shard_map/ppermute | solution.py:38
  47.4 5.3 %collective-permute-start.8 = (bf16[2,128,128]{2,1,0:T(8,128)(2,1)S(1)}, bf16[2,128,128]{2,1,0:T(8,128)(2,1)S(1)}, u32[]{:S(2)}, u32[]{:S(2)}) collective-permute-start(bf16[2,128,128]{2,1,0:T(8,128)(2,1)S(1)} %fusion.19), channel_id=1, source_target_pairs={{0,2},{1,3},{2,0},{3,1},{4,6},{5,7},{6,4},{7,5},{8,10},{9,11},{10,... | collective-permute-start | bytes 196616 | tf_op jit(solution)/shard_map/ppermute | solution.py:38
  48.6 5.9 %collective-permute-start.7 = (bf16[2,128,128]{2,1,0:T(8,128)(2,1)S(1)}, bf16[2,128,128]{2,1,0:T(8,128)(2,1)S(1)}, u32[]{:S(2)}, u32[]{:S(2)}) collective-permute-start(bf16[2,128,128]{2,1,0:T(8,128)(2,1)S(1)} %fusion.19), channel_id=1, source_target_pairs={{0,4},{1,5},{2,6},{3,7},{4,0},{5,1},{6,2},{7,3},{8,12},{9,13},{10,... | collective-permute-start | bytes 196616 | tf_op jit(solution)/shard_map/ppermute | solution.py:38
  49.3 39.3 %collective-permute-start.20 = (bf16[2,72,2048]{2,1,0:T(8,128)(2,1)}, bf16[2,72,2048]{2,1,0:T(8,128)(2,1)S(1)}, u32[]{:S(2)}, u32[]{:S(2)}) collective-permute-start(bf16[2,72,2048]{2,1,0:T(8,128)(2,1)} %after.24), channel_id=1, source_target_pairs={{0,8},{8,0},{16,24},{24,16},{1,9},{9,1},{17,25},{25,17},{2,10},{10... | collective-permute-start | bytes 1769480 | tf_op jit(solution)/shard_map/ppermute | solution.py:38
  52.4 36.2 %collective-permute-start.23 = (bf16[2,72,2048]{2,1,0:T(8,128)(2,1)}, bf16[2,72,2048]{2,1,0:T(8,128)(2,1)S(1)}, u32[]{:S(2)}, u32[]{:S(2)}) collective-permute-start(bf16[2,72,2048]{2,1,0:T(8,128)(2,1)} %after.24), channel_id=1, source_target_pairs={{0,16},{8,24},{16,0},{24,8},{1,17},{9,25},{17,1},{25,9},{2,18},{10... | collective-permute-start | bytes 1769480 | tf_op jit(solution)/shard_map/ppermute | solution.py:38
  54.5 36.4 %copy-start.3 = (bf16[4,2,128,128]{3,2,1,0:T(8,128)(2,1)}, bf16[4,2,128,128]{3,2,1,0:T(8,128)(2,1)S(1)}, u32[]{:S(2)}) copy-start(bf16[4,2,128,128]{3,2,1,0:T(8,128)(2,1)S(1)} %pad_maximum_fusion.3.refs_0_) | copy-start | bytes 786436
  54.5 16.9 %collective-permute-start.10 = (bf16[4,2,128,128]{3,2,1,0:T(8,128)(2,1)S(1)}, bf16[4,2,128,128]{3,2,1,0:T(8,128)(2,1)S(1)}, u32[]{:S(2)}, u32[]{:S(2)}) collective-permute-start(bf16[4,2,128,128]{3,2,1,0:T(8,128)(2,1)S(1)} %pad_maximum_fusion.3.refs_0_), channel_id=1, source_target_pairs={{0,8},{8,0},{16,24},{24,16},{1,9},{9,1},{17,25},{25,17},{2,10},{10... | collective-permute-start | bytes 786440 | tf_op jit(solution)/shard_map/ppermute | solution.py:38
  54.9 21.2 %collective-permute-start.11 = (bf16[4,2,128,128]{3,2,1,0:T(8,128)(2,1)S(1)}, bf16[4,2,128,128]{3,2,1,0:T(8,128)(2,1)S(1)}, u32[]{:S(2)}, u32[]{:S(2)}) collective-permute-start(bf16[4,2,128,128]{3,2,1,0:T(8,128)(2,1)S(1)} %pad_maximum_fusion.3.refs_0_), channel_id=1, source_target_pairs={{0,16},{8,24},{16,0},{24,8},{1,17},{9,25},{17,1},{25,9},{2,18},{10... | collective-permute-start | bytes 786440 | tf_op jit(solution)/shard_map/ppermute | solution.py:38
  57.2 22.1 %collective-permute-start.12 = (bf16[4,2,128,128]{3,2,1,0:T(8,128)(2,1)S(1)}, bf16[4,2,128,128]{3,2,1,0:T(8,128)(2,1)S(1)}, u32[]{:S(2)}, u32[]{:S(2)}) collective-permute-start(bf16[4,2,128,128]{3,2,1,0:T(8,128)(2,1)S(1)} %pad_maximum_fusion.3.refs_0_), channel_id=1, source_target_pairs={{0,24},{8,16},{16,8},{24,0},{1,25},{9,17},{17,9},{25,1},{2,26},{10... | collective-permute-start | bytes 786440 | tf_op jit(solution)/shard_map/ppermute | solution.py:38
  71.4 8.6 %collective-permute-start.21 = (bf16[1,72,2048]{2,1,0:T(8,128)(2,1)}, bf16[1,72,2048]{2,1,0:T(8,128)(2,1)}, u32[]{:S(2)}, u32[]{:S(2)}) collective-permute-start(bf16[1,72,2048]{2,1,0:T(8,128)(2,1)} %after.25), channel_id=1, source_target_pairs={{0,8},{8,0},{16,24},{24,16},{1,9},{9,1},{17,25},{25,17},{2,10},{10... | collective-permute-start | bytes 884744 | tf_op jit(solution)/shard_map/ppermute | solution.py:38
  76.1 7.8 %collective-permute-start.24 = (bf16[1,72,2048]{2,1,0:T(8,128)(2,1)}, bf16[1,72,2048]{2,1,0:T(8,128)(2,1)}, u32[]{:S(2)}, u32[]{:S(2)}) collective-permute-start(bf16[1,72,2048]{2,1,0:T(8,128)(2,1)} %after.25), channel_id=1, source_target_pairs={{0,16},{8,24},{16,0},{24,8},{1,17},{9,25},{17,1},{25,9},{2,18},{10... | collective-permute-start | bytes 884744 | tf_op jit(solution)/shard_map/ppermute | solution.py:38
  80.0 16.6 %collective-permute-start.13 = (bf16[256,512]{1,0:T(8,128)(2,1)}, bf16[256,512]{1,0:T(8,128)(2,1)S(1)}, u32[]{:S(2)}, u32[]{:S(2)}) collective-permute-start(bf16[256,512]{1,0:T(8,128)(2,1)} %after.19), channel_id=1, source_target_pairs={{0,4},{1,5},{2,6},{3,7},{4,0},{5,1},{6,2},{7,3},{8,12},{9,13},{10,... | collective-permute-start | bytes 786440 | tf_op jit(solution)/shard_map/ppermute | solution.py:38
  80.0 18.7 %collective-permute-start.14 = (bf16[256,512]{1,0:T(8,128)(2,1)}, bf16[256,512]{1,0:T(8,128)(2,1)S(1)}, u32[]{:S(2)}, u32[]{:S(2)}) collective-permute-start(bf16[256,512]{1,0:T(8,128)(2,1)} %after.20), channel_id=1, source_target_pairs={{0,2},{1,3},{2,0},{3,1},{4,6},{5,7},{6,4},{7,5},{8,10},{9,11},{10,... | collective-permute-start | bytes 786440 | tf_op jit(solution)/shard_map/ppermute | solution.py:38
  83.9 15.4 %collective-permute-start.15 = (bf16[256,512]{1,0:T(8,128)(2,1)}, bf16[256,512]{1,0:T(8,128)(2,1)S(1)}, u32[]{:S(2)}, u32[]{:S(2)}) collective-permute-start(bf16[256,512]{1,0:T(8,128)(2,1)} %after.21), channel_id=1, source_target_pairs={{0,6},{1,7},{2,4},{3,5},{4,2},{5,3},{6,0},{7,1},{8,14},{9,15},{10,... | collective-permute-start | bytes 786440 | tf_op jit(solution)/shard_map/ppermute | solution.py:38
  90.0 10.0 %collective-permute-start.25 = (bf16[1,72,2048]{2,1,0:T(8,128)(2,1)}, bf16[1,72,2048]{2,1,0:T(8,128)(2,1)S(1)}, u32[]{:S(2)}, u32[]{:S(2)}) collective-permute-start(bf16[1,72,2048]{2,1,0:T(8,128)(2,1)} %after.26), channel_id=1, source_target_pairs={{0,16},{8,24},{16,0},{24,8},{1,17},{9,25},{17,1},{25,9},{2,18},{10... | collective-permute-start | bytes 884744 | tf_op jit(solution)/shard_map/ppermute | solution.py:38
  90.9 12.7 %collective-permute-start.26 = (bf16[2,72,2048]{2,1,0:T(8,128)(2,1)}, bf16[2,72,2048]{2,1,0:T(8,128)(2,1)S(1)}, u32[]{:S(2)}, u32[]{:S(2)}) collective-permute-start(bf16[2,72,2048]{2,1,0:T(8,128)(2,1)} %after.27), channel_id=1, source_target_pairs={{0,8},{8,0},{16,24},{24,16},{1,9},{9,1},{17,25},{25,17},{2,10},{10... | collective-permute-start | bytes 1769480 | tf_op jit(solution)/shard_map/ppermute | solution.py:38
  96.6 6.9 %collective-permute-start.27 = (bf16[1,72,2048]{2,1,0:T(8,128)(2,1)}, bf16[1,72,2048]{2,1,0:T(8,128)(2,1)S(1)}, u32[]{:S(2)}, u32[]{:S(2)}) collective-permute-start(bf16[1,72,2048]{2,1,0:T(8,128)(2,1)} %after.28), channel_id=1, source_target_pairs={{0,16},{8,24},{16,0},{24,8},{1,17},{9,25},{17,1},{25,9},{2,18},{10... | collective-permute-start | bytes 884744 | tf_op jit(solution)/shard_map/ppermute | solution.py:38
  109.1 54.2 %collective-permute-start.34 = (bf16[1152,2048]{1,0:T(8,128)(2,1)}, bf16[1152,2048]{1,0:T(8,128)(2,1)}, u32[]{:S(2)}, u32[]{:S(2)}) collective-permute-start(bf16[1152,2048]{1,0:T(8,128)(2,1)} %join.3.wn_ref.refs_3_), channel_id=1, source_target_pairs={{0,1},{1,0},{2,3},{3,2},{4,5},{5,4},{6,7},{7,6},{8,9},{9,8},{10,11... | collective-permute-start | bytes 14155784 | tf_op jit(solution)/shard_map/ppermute | solution.py:38
  112.9 5.1 %collective-permute-start.28 = (bf16[160,2048]{1,0:T(8,128)(2,1)S(1)}, bf16[160,2048]{1,0:T(8,128)(2,1)S(1)}, u32[]{:S(2)}, u32[]{:S(2)}) collective-permute-start(bf16[160,2048]{1,0:T(8,128)(2,1)S(1)} %convolution_convert_fusion), channel_id=1, source_target_pairs={{0,1},{1,0},{2,3},{3,2},{4,5},{5,4},{6,7},{7,6},{8,9},{9,8},{10,11... | collective-permute-start | bytes 1966088 | tf_op jit(solution)/shard_map/ppermute | solution.py:38
  113.5 22.7 %collective-permute-start.29 = (bf16[256,512]{1,0:T(8,128)(2,1)}, bf16[256,512]{1,0:T(8,128)(2,1)S(1)}, u32[]{:S(2)}, u32[]{:S(2)}) collective-permute-start(bf16[256,512]{1,0:T(8,128)(2,1)} %after.29), channel_id=1, source_target_pairs={{0,4},{1,5},{2,6},{3,7},{4,0},{5,1},{6,2},{7,3},{8,12},{9,13},{10,... | collective-permute-start | bytes 786440 | tf_op jit(solution)/shard_map/ppermute | solution.py:38
  113.6 22.7 %collective-permute-start.30 = (bf16[256,512]{1,0:T(8,128)(2,1)}, bf16[256,512]{1,0:T(8,128)(2,1)S(1)}, u32[]{:S(2)}, u32[]{:S(2)}) collective-permute-start(bf16[256,512]{1,0:T(8,128)(2,1)} %after.30), channel_id=1, source_target_pairs={{0,2},{1,3},{2,0},{3,1},{4,6},{5,7},{6,4},{7,5},{8,10},{9,11},{10,... | collective-permute-start | bytes 786440 | tf_op jit(solution)/shard_map/ppermute | solution.py:38
  116.3 20.0 %collective-permute-start.31 = (bf16[256,512]{1,0:T(8,128)(2,1)}, bf16[256,512]{1,0:T(8,128)(2,1)S(1)}, u32[]{:S(2)}, u32[]{:S(2)}) collective-permute-start(bf16[256,512]{1,0:T(8,128)(2,1)} %after.31), channel_id=1, source_target_pairs={{0,6},{1,7},{2,4},{3,5},{4,2},{5,3},{6,0},{7,1},{8,14},{9,15},{10,... | collective-permute-start | bytes 786440 | tf_op jit(solution)/shard_map/ppermute | solution.py:38
  121.4 30.3 %copy-start.5 = (bf16[2048,128]{1,0:T(8,128)(2,1)}, bf16[2048,128]{1,0:T(8,128)(2,1)S(1)}, u32[]{:S(2)}) copy-start(bf16[2048,128]{1,0:T(8,128)(2,1)S(1)} %pad_maximum_fusion.1.w3_ref.refs_8_) | copy-start | bytes 1572868
  136.1 17.2 %collective-permute-start.32 = (bf16[128,2048]{1,0:T(8,128)(2,1)}, bf16[128,2048]{1,0:T(8,128)(2,1)S(1)}, u32[]{:S(2)}, u32[]{:S(2)}) collective-permute-start(bf16[128,2048]{1,0:T(8,128)(2,1)} %get-tuple-element.74), channel_id=1, source_target_pairs={{0,1},{1,0},{2,3},{3,2},{4,5},{5,4},{6,7},{7,6},{8,9},{9,8},{10,11... | collective-permute-start | bytes 1572872 | tf_op jit(solution)/shard_map/ppermute | solution.py:38
  151.7 2.2 collective-permute-start.33
  172.8 5.8 %collective-permute-start.37 = (bf16[128,128]{1,0:T(8,128)(2,1)S(1)}, bf16[128,128]{1,0:T(8,128)(2,1)S(1)}, u32[]{:S(2)}, u32[]{:S(2)}) collective-permute-start(bf16[128,128]{1,0:T(8,128)(2,1)S(1)} %get-tuple-element.78.q_ref), channel_id=1, source_target_pairs={{0,6},{1,7},{2,4},{3,5},{4,2},{5,3},{6,0},{7,1},{8,14},{9,15},{10,... | collective-permute-start | bytes 98312 | tf_op jit(solution)/shard_map/ppermute | solution.py:38
  174.9 4.0 %collective-permute-start.36 = (bf16[128,128]{1,0:T(8,128)(2,1)S(1)}, bf16[128,128]{1,0:T(8,128)(2,1)S(1)}, u32[]{:S(2)}, u32[]{:S(2)}) collective-permute-start(bf16[128,128]{1,0:T(8,128)(2,1)S(1)} %get-tuple-element.78.q_ref), channel_id=1, source_target_pairs={{0,2},{1,3},{2,0},{3,1},{4,6},{5,7},{6,4},{7,5},{8,10},{9,11},{10,... | collective-permute-start | bytes 98312 | tf_op jit(solution)/shard_map/ppermute | solution.py:38
  176.3 5.2 %collective-permute-start.35 = (bf16[128,128]{1,0:T(8,128)(2,1)S(1)}, bf16[128,128]{1,0:T(8,128)(2,1)S(1)}, u32[]{:S(2)}, u32[]{:S(2)}) collective-permute-start(bf16[128,128]{1,0:T(8,128)(2,1)S(1)} %get-tuple-element.78.q_ref), channel_id=1, source_target_pairs={{0,4},{1,5},{2,6},{3,7},{4,0},{5,1},{6,2},{7,3},{8,12},{9,13},{10,... | collective-permute-start | bytes 98312 | tf_op jit(solution)/shard_map/ppermute | solution.py:38
  181.5 5.5 %collective-permute-start.38 = (bf16[4,128,128]{2,1,0:T(8,128)(2,1)S(1)}, bf16[4,128,128]{2,1,0:T(8,128)(2,1)S(1)}, u32[]{:S(2)}, u32[]{:S(2)}) collective-permute-start(bf16[4,128,128]{2,1,0:T(8,128)(2,1)S(1)} %pad_maximum_fusion.4.refs_8_), channel_id=1, source_target_pairs={{0,8},{8,0},{16,24},{24,16},{1,9},{9,1},{17,25},{25,17},{2,10},{10... | collective-permute-start | bytes 393224 | tf_op jit(solution)/shard_map/ppermute | solution.py:38
  182.0 6.2 %collective-permute-start.39 = (bf16[4,128,128]{2,1,0:T(8,128)(2,1)S(1)}, bf16[4,128,128]{2,1,0:T(8,128)(2,1)S(1)}, u32[]{:S(2)}, u32[]{:S(2)}) collective-permute-start(bf16[4,128,128]{2,1,0:T(8,128)(2,1)S(1)} %pad_maximum_fusion.4.refs_8_), channel_id=1, source_target_pairs={{0,16},{8,24},{16,0},{24,8},{1,17},{9,25},{17,1},{25,9},{2,18},{10... | collective-permute-start | bytes 393224 | tf_op jit(solution)/shard_map/ppermute | solution.py:38
  183.9 5.9 %collective-permute-start.40 = (bf16[4,128,128]{2,1,0:T(8,128)(2,1)S(1)}, bf16[4,128,128]{2,1,0:T(8,128)(2,1)S(1)}, u32[]{:S(2)}, u32[]{:S(2)}) collective-permute-start(bf16[4,128,128]{2,1,0:T(8,128)(2,1)S(1)} %pad_maximum_fusion.4.refs_8_), channel_id=1, source_target_pairs={{0,24},{8,16},{16,8},{24,0},{1,25},{9,17},{17,9},{25,1},{2,26},{10... | collective-permute-start | bytes 393224 | tf_op jit(solution)/shard_map/ppermute | solution.py:38
  192.8 1.3 collective-permute-start.41
  194.6 1.2 collective-permute-start.42
  195.8 7.2 %collective-permute-start.43 = (bf16[2,128,128]{2,1,0:T(8,128)(2,1)S(1)}, bf16[2,128,128]{2,1,0:T(8,128)(2,1)S(1)}, u32[]{:S(2)}, u32[]{:S(2)}) collective-permute-start(bf16[2,128,128]{2,1,0:T(8,128)(2,1)S(1)} %pad_maximum_fusion.5.refs_8_), channel_id=1, source_target_pairs={{0,4},{1,5},{2,6},{3,7},{4,0},{5,1},{6,2},{7,3},{8,12},{9,13},{10,... | collective-permute-start | bytes 196616 | tf_op jit(solution)/shard_map/ppermute | solution.py:38
  197.2 5.8 %collective-permute-start.44 = (bf16[2,128,128]{2,1,0:T(8,128)(2,1)S(1)}, bf16[2,128,128]{2,1,0:T(8,128)(2,1)S(1)}, u32[]{:S(2)}, u32[]{:S(2)}) collective-permute-start(bf16[2,128,128]{2,1,0:T(8,128)(2,1)S(1)} %pad_maximum_fusion.5.refs_8_), channel_id=1, source_target_pairs={{0,2},{1,3},{2,0},{3,1},{4,6},{5,7},{6,4},{7,5},{8,10},{9,11},{10,... | collective-permute-start | bytes 196616 | tf_op jit(solution)/shard_map/ppermute | solution.py:38
  199.1 6.1 %collective-permute-start.45 = (bf16[2,128,128]{2,1,0:T(8,128)(2,1)S(1)}, bf16[2,128,128]{2,1,0:T(8,128)(2,1)S(1)}, u32[]{:S(2)}, u32[]{:S(2)}) collective-permute-start(bf16[2,128,128]{2,1,0:T(8,128)(2,1)S(1)} %pad_maximum_fusion.5.refs_8_), channel_id=1, source_target_pairs={{0,6},{1,7},{2,4},{3,5},{4,2},{5,3},{6,0},{7,1},{8,14},{9,15},{10,... | collective-permute-start | bytes 196616 | tf_op jit(solution)/shard_map/ppermute | solution.py:38
  207.4 4.3 %collective-permute-start.46 = (f32[128,128]{1,0:T(8,128)S(1)}, f32[128,128]{1,0:T(8,128)S(1)}, u32[]{:S(2)}, u32[]{:S(2)}) collective-permute-start(f32[128,128]{1,0:T(8,128)S(1)} %get-tuple-element.83), channel_id=1, source_target_pairs={{0,8},{8,0},{16,24},{24,16},{1,9},{9,1},{17,25},{25,17},{2,10},{10... | collective-permute-start | bytes 196616 | tf_op jit(solution)/shard_map/ppermute | solution.py:38
  208.3 4.5 %collective-permute-start.47 = (f32[128,128]{1,0:T(8,128)S(1)}, f32[128,128]{1,0:T(8,128)S(1)}, u32[]{:S(2)}, u32[]{:S(2)}) collective-permute-start(f32[128,128]{1,0:T(8,128)S(1)} %get-tuple-element.84), channel_id=1, source_target_pairs={{0,16},{8,24},{16,0},{24,8},{1,17},{9,25},{17,1},{25,9},{2,18},{10... | collective-permute-start | bytes 196616 | tf_op jit(solution)/shard_map/ppermute | solution.py:38
  209.8 5.2 %collective-permute-start.48 = (f32[128,128]{1,0:T(8,128)S(1)}, f32[128,128]{1,0:T(8,128)S(1)}, u32[]{:S(2)}, u32[]{:S(2)}) collective-permute-start(f32[128,128]{1,0:T(8,128)S(1)} %get-tuple-element.85), channel_id=1, source_target_pairs={{0,24},{8,16},{16,8},{24,0},{1,25},{9,17},{17,9},{25,1},{2,26},{10... | collective-permute-start | bytes 196616 | tf_op jit(solution)/shard_map/ppermute | solution.py:38
  220.2 6.4 %collective-permute-start.52 = (bf16[1152,1024]{1,0:T(8,128)(2,1)}, bf16[1152,1024]{1,0:T(8,128)(2,1)}, u32[]{:S(2)}, u32[]{:S(2)}) collective-permute-start(bf16[1152,1024]{1,0:T(8,128)(2,1)} %get-tuple-element.93), channel_id=1, source_target_pairs={{0,1},{1,0},{2,3},{3,2},{4,5},{5,4},{6,7},{7,6},{8,9},{9,8},{10,11... | collective-permute-start | bytes 7077896 | tf_op jit(solution)/shard_map/ppermute | solution.py:38
  225.5 8.1 %collective-permute-start.49 = (bf16[1152,1024]{1,0:T(8,128)(2,1)}, bf16[1152,1024]{1,0:T(8,128)(2,1)}, u32[]{:S(2)}, u32[]{:S(2)}) collective-permute-start(bf16[1152,1024]{1,0:T(8,128)(2,1)} %get-tuple-element.89), channel_id=1, source_target_pairs={{0,1},{1,0},{2,3},{3,2},{4,5},{5,4},{6,7},{7,6},{8,9},{9,8},{10,11... | collective-permute-start | bytes 7077896 | tf_op jit(solution)/shard_map/ppermute | solution.py:38
  232.6 28.2 %collective-permute-start.53 = (bf16[2,4,72,1024]{3,2,1,0:T(8,128)(2,1)}, bf16[2,4,72,1024]{3,2,1,0:T(8,128)(2,1)}, u32[]{:S(2)}, u32[]{:S(2)}) collective-permute-start(bf16[2,4,72,1024]{3,2,1,0:T(8,128)(2,1)} %bitcast.210), channel_id=1, source_target_pairs={{0,16},{8,24},{16,0},{24,8},{1,17},{9,25},{17,1},{25,9},{2,18},{10... | collective-permute-start | bytes 3538952 | tf_op jit(solution)/shard_map/ppermute | solution.py:38
  239.4 29.0 %collective-permute-start.50 = (bf16[2,4,72,1024]{3,2,1,0:T(8,128)(2,1)}, bf16[2,4,72,1024]{3,2,1,0:T(8,128)(2,1)S(1)}, u32[]{:S(2)}, u32[]{:S(2)}) collective-permute-start(bf16[2,4,72,1024]{3,2,1,0:T(8,128)(2,1)} %bitcast.211), channel_id=1, source_target_pairs={{0,8},{8,0},{16,24},{24,16},{1,9},{9,1},{17,25},{25,17},{2,10},{10... | collective-permute-start | bytes 3538952 | tf_op jit(solution)/shard_map/ppermute | solution.py:38
  254.8 16.8 %collective-permute-start.57 = (bf16[2,128,2048]{2,1,0:T(8,128)(2,1)}, bf16[2,128,2048]{2,1,0:T(8,128)(2,1)S(1)}, u32[]{:S(2)}, u32[]{:S(2)}) collective-permute-start(bf16[2,128,2048]{2,1,0:T(8,128)(2,1)} %bitcast.185), channel_id=1, source_target_pairs={{0,1},{1,0},{2,3},{3,2},{4,5},{5,4},{6,7},{7,6},{8,9},{9,8},{10,11... | collective-permute-start | bytes 3145736 | tf_op jit(solution)/shard_map/ppermute | solution.py:38
  262.8 17.6 %collective-permute-start.54 = (bf16[1,4,72,1024]{3,2,1,0:T(8,128)(2,1)S(1)}, bf16[1,4,72,1024]{3,2,1,0:T(8,128)(2,1)}, u32[]{:S(2)}, u32[]{:S(2)}) collective-permute-start(bf16[1,4,72,1024]{3,2,1,0:T(8,128)(2,1)S(1)} %fusion.7), channel_id=1, source_target_pairs={{0,8},{8,0},{16,24},{24,16},{1,9},{9,1},{17,25},{25,17},{2,10},{10... | collective-permute-start | bytes 1769480 | tf_op jit(solution)/shard_map/ppermute | solution.py:38
  269.0 13.5 %collective-permute-start.51 = (bf16[1,4,72,1024]{3,2,1,0:T(8,128)(2,1)S(1)}, bf16[1,4,72,1024]{3,2,1,0:T(8,128)(2,1)S(1)}, u32[]{:S(2)}, u32[]{:S(2)}) collective-permute-start(bf16[1,4,72,1024]{3,2,1,0:T(8,128)(2,1)S(1)} %fusion.6), channel_id=1, source_target_pairs={{0,16},{8,24},{16,0},{24,8},{1,17},{9,25},{17,1},{25,9},{2,18},{10... | collective-permute-start | bytes 1769480 | tf_op jit(solution)/shard_map/ppermute | solution.py:38
  284.5 13.3 %collective-permute-start.55 = (bf16[1,2,72,2048]{3,2,1,0:T(8,128)(2,1)S(1)}, bf16[1,2,72,2048]{3,2,1,0:T(8,128)(2,1)S(1)}, u32[]{:S(2)}, u32[]{:S(2)}) collective-permute-start(bf16[1,2,72,2048]{3,2,1,0:T(8,128)(2,1)S(1)} %fusion.8), channel_id=1, source_target_pairs={{0,2},{1,3},{2,0},{3,1},{4,6},{5,7},{6,4},{7,5},{8,10},{9,11},{10,... | collective-permute-start | bytes 1769480 | tf_op jit(solution)/shard_map/ppermute | solution.py:38
  298.0 13.3 %collective-permute-start.56 = (bf16[1,1,72,2048]{3,2,1,0:T(8,128)(2,1)S(1)}, bf16[1,1,72,2048]{3,2,1,0:T(8,128)(2,1)S(1)}, u32[]{:S(2)}, u32[]{:S(2)}) collective-permute-start(bf16[1,1,72,2048]{3,2,1,0:T(8,128)(2,1)S(1)} %get-tuple-element.113), channel_id=1, source_target_pairs={{0,4},{1,5},{2,6},{3,7},{4,0},{5,1},{6,2},{7,3},{8,12},{9,13},{10,... | collective-permute-start | bytes 884744 | tf_op jit(solution)/shard_map/ppermute | solution.py:38
  312.0 21.8 %all-to-all-start = ((bf16[32,80,128]{2,1,0:T(8,128)(2,1)}), bf16[32,80,128]{2,1,0:T(8,128)(2,1)S(1)}, u32[]{:S(2)}, u32[]{:S(2)}) async-start(bf16[32,80,128]{2,1,0:T(8,128)(2,1)} %after.37), calls=%async_computation | async-start | bytes 1310720 | tf_op jit(solution)/shard_map/all_to_all | solution.py:872
  337.6 24.6 %all-to-all-start.1 = ((bf16[32,96,128]{2,1,0:T(8,128)(2,1)}), bf16[32,96,128]{2,1,0:T(8,128)(2,1)S(1)}, u32[]{:S(2)}, u32[]{:S(2)}) async-start(bf16[32,96,128]{2,1,0:T(8,128)(2,1)} %broadcast_in_dim.74), calls=%async_computation.1 | async-start | bytes 1572864 | tf_op jit(solution)/shard_map/all_to_all | solution.py:881
  (44 other events, 263.4 us)

commit v4 on v3

--- a/solution.py
+++ b/solution.py
@@ -749,7 +749,7 @@
         passed[j] = [swap(h, "rows", bit) for h, bit in zip(hop, (highest, lowest, highest))]
     for m in range(1, MB):
         for i, j in enumerate(z_order[1:]):
-            strips[m].append(swap(after(leave[m][i], *strips[m - 1][1:]), "cols", 2 * j))
+            strips[m].append(swap(after(leave[m][i], strips[m - 1][1]), "cols", 2 * j))
     passed[0][0] = after(passed[0][0], *strips[0][1:])
     near = join([g.reshape(-1, HID) for j in range(n_rows) for g in passed[j]])
     far = swap(near, "cols", 1)

time: 370 us -> 370 us (level)
  no operation moved by 1% of the time
where the time goes in v4:
time: 370 us; the launch traced here: 369 us
  Pallas kernels  118 us (32%)
  waiting for transfers between devices  115 us (31%)
  starting transfers between devices  70.1 us (19%)
  other arithmetic  30.3 us (8%)
  local copies, waits for them, and re-layouts  27 us (7%)
  between operations  4.84 us (1%)
    pallas_call x20, Pallas kernels, run(): pl.pallas_call(kernel, out_shape=tuple(placed) if isinstance(out_shape, t...  118 us
    ppermute x58, waiting for transfers between devices, swap(): return lax.ppermute(x, axis, [(i, i ^ bit) for i in range(size)])  75.3 us
    ppermute x58, starting transfers between devices, swap(): return lax.ppermute(x, axis, [(i, i ^ bit) for i in range(size)])  64.9 us
    all_to_all x1, waiting for transfers between devices, per_device(): got = lax.all_to_all(sent, BOTH, split_axis=0, concat_axis=0, tiled=True)  21.9 us
    all_to_all x1, waiting for transfers between devices, per_device(): got = lax.all_to_all(d_small, BOTH, split_axis=0, concat_axis=0, tiled=True)  17.8 us
    unnamed x105, local copies, waits for them, and re-layouts  14.7 us
    convert_element_type x21, other arithmetic, tip(): return x[:8, :128].astype(F32)  14.1 us
  transfers between devices with their start and end apart: 60, of which 30 were waited for; matrix products, arithmetic and copies ran while one was open for 11% of the time, Pallas kernels for 25%

profile of v4, /device:TPU:0, one launch (start us, length us, event | category | flops | bytes accessed | tf_op | source)
XLA Modules:
  0.0 368.6 jit_solution(17994822450733102035)
XLA Ops:
  1.6 3.0 collective-permute-start
  4.6 1.5 collective-permute-start.1
  9.9 4.0 %masked_tile.1 = (bf16[256,512]{1,0:T(8,128)(2,1)}, bf16[256,512]{1,0:T(8,128)(2,1)}, bf16[256,512]{1,0:T(8,128)(2,1)}, bf16[256,512]{1,0:T(8,128)(2,1)}, bf16[2...) custom-call(s32[2]{0:T(128)S(1)} %pad_add_fusion.1.refs_0_, ...), custom_call_target="tpu_custom_call" | custom-call | tf_op jit(solution)/shard_map/masked_tile/pallas_call | solution.py:127
  13.9 2.2 layer_one.1
  16.8 2.0 collective-permute-start.22
  18.8 1.5 collective-permute-start.19
  20.3 1.6 collective-permute-start.17
  21.8 2.6 collective-permute-start.16
  24.4 2.2 collective-permute-done.22
  27.4 3.9 %collective-permute-start.6 = (bf16[2,128,128]{2,1,0:T(8,128)(2,1)S(1)}, bf16[2,128,128]{2,1,0:T(8,128)(2,1)S(1)}, u32[]{:S(2)}, u32[]{:S(2)}) collective-permute-start(bf16[2,128,128]{2,1,0:T(8,128)(2,1)S(1)} %get-tuple-element.117), channel_id=1, source_target_pairs={{0,6},{1,7},{2,4},{3,5},{4,2},{5,3},{6,0},{7,1},{8,14},{9,15},{10,... | collective-permute-start | bytes 196616 | tf_op jit(solution)/shard_map/ppermute | solution.py:38
  33.3 7.6 %collective-permute-done.16.refs_0_ = bf16[1,72,2048]{2,1,0:T(8,128)(2,1)} collective-permute-done((bf16[1,72,2048]{2,1,0:T(8,128)(2,1)}, bf16[1,72,2048]{2,1,0:T(8,128)(2,1)}, u32[]{:S(2)}, u32[]{:S(2)}) %collective-permute-start.16) | collective-permute-done | bytes 294944 | tf_op jit(solution)/shard_map/ppermute | solution.py:38
  44.2 3.2 collective-permute-start.9
  49.5 2.9 collective-permute-done.9
  52.8 1.7 collective-permute-done.7
  57.2 2.6 collective-permute-start.12
  59.8 11.6 %collective-permute-done.10.refs_1_ = bf16[4,2,128,128]{3,2,1,0:T(8,128)(2,1)S(1)} collective-permute-done((bf16[4,2,128,128]{3,2,1,0:T(8,128)(2,1)S(1)}, bf16[4,2,128,128]{3,2,1,0:T(8,128)(2,1)S(1)}, u32[]{:S(2)}, u32[]{:S(2)}) %collective-permute-start.10) | collective-permute-done | bytes 262176 | tf_op jit(solution)/shard_map/ppermute | solution.py:38
  72.2 3.9 %collective-permute-done.11.refs_2_ = bf16[4,2,128,128]{3,2,1,0:T(8,128)(2,1)S(1)} collective-permute-done((bf16[4,2,128,128]{3,2,1,0:T(8,128)(2,1)S(1)}, bf16[4,2,128,128]{3,2,1,0:T(8,128)(2,1)S(1)}, u32[]{:S(2)}, u32[]{:S(2)}) %collective-permute-start.11) | collective-permute-done | bytes 262176 | tf_op jit(solution)/shard_map/ppermute | solution.py:38
  76.1 2.6 collective-permute-start.24
  81.0 1.7 copy.99.refs_0_
  83.9 3.4 collective-permute-start.15
  90.9 1.5 collective-permute-start.26
  92.4 4.2 %collective-permute-done.13.refs_5_.refs_1_ = bf16[256,512]{1,0:T(8,128)(2,1)S(1)} collective-permute-done((bf16[256,512]{1,0:T(8,128)(2,1)}, bf16[256,512]{1,0:T(8,128)(2,1)S(1)}, u32[]{:S(2)}, u32[]{:S(2)}) %collective-permute-start.13) | collective-permute-done | bytes 262176 | tf_op jit(solution)/shard_map/ppermute | solution.py:38
  96.6 1.5 collective-permute-start.27
  99.9 3.6 collective-permute-done.27
  104.5 4.6 %join.3.wn_ref.refs_3_ = bf16[1152,2048]{1,0:T(8,128)(2,1)} custom-call(bf16[72,2048]{1,0:T(8,128)(2,1)} %bitcast.189, bf16[144,2048]{1,0:T(8,128)(2,1)} %bitcast.172, bf16[72,2048]{1,0:T(8,128)(2,1)} %bitcast.25.refs_2_, bf16[72,2048]{1,0:T(8,128)(2,1)} %bitcast.197, bf16[144,2048]{1,0:T(8,128)(2,1)} %bitcast.195, bf16[72,2048]{1,0:T(8,128)(2,1)} %bitcast.28.refs_5_, ...), custom_call_target="tpu_custom_call" | custom-call | tf_op jit(solution)/shard_map/join/pallas_call | solution.py:127
  109.5 3.4 convolution_convert_fusion
  113.6 2.7 collective-permute-start.30
  116.3 1.7 collective-permute-start.31
  121.4 14.1 %forward_two.2 = (f32[128,2048]{1,0:T(8,128)}, bf16[128,2048]{1,0:T(8,128)(2,1)}, bf16[2048,2048]{1,0:T(8,128)(2,1)}) custom-call(bf16[4,2,128,128]{3,2,1,0:T(8,128)(2,1)} %copy-done.3, bf16[4,2,128,128]{3,2,1,0:T(8,128)(2,1)} %copy-done.12, bf16[4,2,128,128]{3,2,1,0:T(8,128)(2,1)} %copy-done.13, bf16[4,2,128,128]{3,2,1,0:T(8,128)(2,1)} %copy-done.14, ...), custom_call_target="tpu_custom_call" | custom-call | tf_op jit(solution)/shard_map/forward_two/pallas_call | solution.py:127
  137.8 13.9 %forward_two.3 = (f32[128,2048]{1,0:T(8,128)}, bf16[128,2048]{1,0:T(8,128)(2,1)}, bf16[2048,2048]{1,0:T(8,128)(2,1)}) custom-call(bf16[4,2,128,128]{3,2,1,0:T(8,128)(2,1)} %copy-done.3, bf16[4,2,128,128]{3,2,1,0:T(8,128)(2,1)} %copy-done.12, bf16[4,2,128,128]{3,2,1,0:T(8,128)(2,1)} %copy-done.13, bf16[4,2,128,128]{3,2,1,0:T(8,128)(2,1)} %copy-done.14, ...), custom_call_target="tpu_custom_call" | custom-call | tf_op jit(solution)/shard_map/forward_two/pallas_call | solution.py:127
  154.7 8.6 %spread_two.1 = (bf16[256,1152]{1,0:T(8,128)(2,1)}, bf16[256,1152]{1,0:T(8,128)(2,1)}) custom-call(f32[128,2048]{1,0:T(8,128)} %get-tuple-element.69.refs_0_, f32[128,2048]{1,0:T(8,128)} %get-tuple-element.73.refs_1_, bf16[128,2048]{1,0:T(8,128)(2,1)} %copy-done.34, bf16[128,2048]{1,0:T(8,128)(2,1)} %copy-done.35, bf16[256,128]{1,0:T(8,128)(2,1)S(1)} %bitcast.181, ...), custom_call_target="tpu_custom_call" | custom-call | tf_op jit(solution)/shard_map/spread_two/pallas_call | solution.py:127
  164.0 8.8 %layer_two.1 = (f32[256,2048]{1,0:T(8,128)}, bf16[256,2048]{1,0:T(8,128)(2,1)}, bf16[128,128]{1,0:T(8,128)(2,1)S(1)}) custom-call(bf16[256,1152]{1,0:T(8,128)(2,1)} %get-tuple-element.76.gn_ref.refs_0_, bf16[256,1152]{1,0:T(8,128)(2,1)} %get-tuple-element.77.gf_ref.refs_9_, bf16[1152,2048]{1,0:T(8,128)(2,1)} %join.3.wn_ref.refs_3_, ...), custom_call_target="tpu_custom_call" | custom-call | tf_op jit(solution)/shard_map/layer_two/pallas_call | solution.py:127
  172.8 2.2 collective-permute-start.37
  178.9 2.5 collective-permute-done.35
  182.0 1.9 collective-permute-start.39
  185.0 1.9 collective-permute-done.38.refs_9_
  188.1 1.6 collective-permute-done.40.refs_11_
  190.5 2.3 logits_parts.1
  197.2 1.9 collective-permute-start.44
  200.3 2.7 collective-permute-done.43.refs_9_
  203.0 2.2 collective-permute-done.45.refs_11_
  205.2 2.3 d_q_parts.1
  208.3 1.5 collective-permute-start.47
  212.8 2.2 collective-permute-done.48.refs_3_
  215.0 5.3 %d_two.3 = (bf16[256,1024]{1,0:T(8,128)(2,1)}, f32[8,1024]{1,0:T(8,128)S(1)}, f32[1024,128]{1,0:T(8,128)}, bf16[1152,1024]{1,0:T(8,128)(2,1)}) custom-call(f32[128,128]{1,0:T(8,128)S(1)} %get-tuple-element.82.refs_0_, f32[128,128]{1,0:T(8,128)S(1)} %collective-permute-done.46.refs_1_, f32[128,128]{1,0:T(8,128)S(1)} %collective-permute-done.47.refs_2_, ...), custom_call_target="tpu_custom_call" | custom-call | tf_op jit(solution)/shard_map/d_two/pallas_call | solution.py:127
  220.2 5.3 %d_two.2 = (bf16[256,1024]{1,0:T(8,128)(2,1)}, f32[8,1024]{1,0:T(8,128)S(1)}, f32[1024,128]{1,0:T(8,128)}, bf16[1152,1024]{1,0:T(8,128)(2,1)}) custom-call(f32[128,128]{1,0:T(8,128)S(1)} %get-tuple-element.82.refs_0_, f32[128,128]{1,0:T(8,128)S(1)} %collective-permute-done.46.refs_1_, f32[128,128]{1,0:T(8,128)S(1)} %collective-permute-done.47.refs_2_, ...), custom_call_target="tpu_custom_call" | custom-call | tf_op jit(solution)/shard_map/d_two/pallas_call | solution.py:127
  226.7 5.3 %near_part.3 = (f32[576,1024]{1,0:T(8,128)}, bf16[576,1024]{1,0:T(8,128)(2,1)}, f32[8,128]{1,0:T(8,128)S(1)}) custom-call(bf16[256,1152]{1,0:T(8,128)(2,1)} %get-tuple-element.76.gn_ref.refs_0_, bf16[256,1024]{1,0:T(8,128)(2,1)} %get-tuple-element.92.refs_1_, bf16[1152,1024]{1,0:T(8,128)(2,1)} %collective-permute-done.52.refs_2_), custom_call_target="tpu_custom_call" | custom-call | tf_op jit(solution)/shard_map/near_part/pallas_call | solution.py:127
  233.6 5.1 %near_part.2 = (f32[576,1024]{1,0:T(8,128)}, bf16[576,1024]{1,0:T(8,128)(2,1)}, f32[8,128]{1,0:T(8,128)S(1)}) custom-call(bf16[256,1152]{1,0:T(8,128)(2,1)} %get-tuple-element.76.gn_ref.refs_0_, bf16[256,1024]{1,0:T(8,128)(2,1)} %get-tuple-element.88.refs_1_.refs_0_, bf16[1152,1024]{1,0:T(8,128)(2,1)} %collective-permute-done.49.refs_2_), custom_call_target="tpu_custom_call" | custom-call | tf_op jit(solution)/shard_map/near_part/pallas_call | solution.py:127
  239.4 1.4 collective-permute-start.50
  242.3 12.5 %d_g_two.1 = bf16[256,2048]{1,0:T(8,128)(2,1)} custom-call(bf16[256,1024]{1,0:T(8,128)(2,1)} %after.33.refs_0_, bf16[256,1024]{1,0:T(8,128)(2,1)} %get-tuple-element.92.refs_1_, s32[2304,1]{1,0:T(8,128)S(1)} %broadcast_add_fusion.refs_2_, bf16[1152,2048]{1,0:T(8,128)(2,1)} %join.3.wn_ref.refs_3_, bf16[1152,2048]{1,0:T(8,128)(2,1)} %collective-permute-done.34.wf_ref.refs_4_), custom_call_target="tpu_custom_call" | custom-call | tf_op jit(solution)/shard_map/d_g_two/pallas_call | solution.py:127
  254.8 6.0 %collective-permute-done.53 = bf16[2,4,72,1024]{3,2,1,0:T(8,128)(2,1)} collective-permute-done((bf16[2,4,72,1024]{3,2,1,0:T(8,128)(2,1)}, bf16[2,4,72,1024]{3,2,1,0:T(8,128)(2,1)}, u32[]{:S(2)}, u32[]{:S(2)}) %collective-permute-start.53) | collective-permute-done | bytes 1179680 | tf_op jit(solution)/shard_map/ppermute | solution.py:38
  260.8 2.0 add_bitcast_fusion
  262.8 1.5 collective-permute-start.54
  264.3 4.1 %collective-permute-done.50 = bf16[2,4,72,1024]{3,2,1,0:T(8,128)(2,1)S(1)} collective-permute-done((bf16[2,4,72,1024]{3,2,1,0:T(8,128)(2,1)}, bf16[2,4,72,1024]{3,2,1,0:T(8,128)(2,1)S(1)}, u32[]{:S(2)}, u32[]{:S(2)}) %collective-permute-start.50) | collective-permute-done | bytes 1179680 | tf_op jit(solution)/shard_map/ppermute | solution.py:38
  272.6 7.8 %backward_one.3 = bf16[128,768]{1,0:T(8,128)(2,1)} custom-call(bf16[4,2,128,128]{3,2,1,0:T(8,128)(2,1)} %copy-done.3, bf16[4,2,128,128]{3,2,1,0:T(8,128)(2,1)} %copy-done.12, bf16[4,2,128,128]{3,2,1,0:T(8,128)(2,1)} %copy-done.13, bf16[4,2,128,128]{3,2,1,0:T(8,128)(2,1)} %copy-done.14, bf16[256,512]{1,0:T(8,128)(2,1)} %get-tuple-element.56.refs_0_.refs_4_, ...), custom_call_target="tpu_custom_call" | custom-call | tf_op jit(solution)/shard_map/backward_one/pallas_call | solution.py:127
  285.2 7.8 %backward_one.4 = bf16[128,768]{1,0:T(8,128)(2,1)} custom-call(bf16[4,2,128,128]{3,2,1,0:T(8,128)(2,1)} %copy-done.3, bf16[4,2,128,128]{3,2,1,0:T(8,128)(2,1)} %copy-done.12, bf16[4,2,128,128]{3,2,1,0:T(8,128)(2,1)} %copy-done.13, bf16[4,2,128,128]{3,2,1,0:T(8,128)(2,1)} %copy-done.14, bf16[256,512]{1,0:T(8,128)(2,1)} %get-tuple-element.56.refs_0_.refs_4_, ...), custom_call_target="tpu_custom_call" | custom-call | tf_op jit(solution)/shard_map/backward_one/pallas_call | solution.py:127
  293.0 4.8 %collective-permute-done.55 = bf16[1,2,72,2048]{3,2,1,0:T(8,128)(2,1)S(1)} collective-permute-done((bf16[1,2,72,2048]{3,2,1,0:T(8,128)(2,1)S(1)}, bf16[1,2,72,2048]{3,2,1,0:T(8,128)(2,1)S(1)}, u32[]{:S(2)}, u32[]{:S(2)}) %collective-permute-start.55) | collective-permute-done | bytes 589856 | tf_op jit(solution)/shard_map/ppermute | solution.py:38
  298.0 1.5 collective-permute-start.56
  300.2 6.1 %backward_one.5 = bf16[128,512]{1,0:T(8,128)(2,1)} custom-call(bf16[4,2,128,128]{3,2,1,0:T(8,128)(2,1)} %copy-done.3, bf16[4,2,128,128]{3,2,1,0:T(8,128)(2,1)} %copy-done.12, bf16[4,2,128,128]{3,2,1,0:T(8,128)(2,1)} %copy-done.13, bf16[4,2,128,128]{3,2,1,0:T(8,128)(2,1)} %copy-done.14, bf16[256,512]{1,0:T(8,128)(2,1)} %get-tuple-element.56.refs_0_.refs_4_, ...), custom_call_target="tpu_custom_call" | custom-call | tf_op jit(solution)/shard_map/backward_one/pallas_call | solution.py:127
  312.0 2.6 all-to-all-start
  316.0 17.8 %all-to-all-done = bf16[32,80,128]{2,1,0:T(8,128)(2,1)S(1)} async-done(((bf16[32,80,128]{2,1,0:T(8,128)(2,1)}), bf16[32,80,128]{2,1,0:T(8,128)(2,1)S(1)}, u32[]{:S(2)}, u32[]{:S(2)}) %all-to-all-start) | async-done | bytes 655392 | tf_op jit(solution)/shard_map/all_to_all | solution.py:872
  337.6 2.6 all-to-all-start.1
  340.2 21.9 %all-to-all-done.1 = bf16[32,96,128]{2,1,0:T(8,128)(2,1)S(1)} async-done(((bf16[32,96,128]{2,1,0:T(8,128)(2,1)}), bf16[32,96,128]{2,1,0:T(8,128)(2,1)S(1)}, u32[]{:S(2)}, u32[]{:S(2)}) %all-to-all-start.1) | async-done | bytes 786464 | tf_op jit(solution)/shard_map/all_to_all | solution.py:881
  364.9 2.6 multiply_subtract_fusion
  (319 shorter events, 80.2 us)
Async XLA Ops:
  1.6 12.3 %collective-permute-start = (bf16[2,128,128]{2,1,0:T(8,128)(2,1)S(1)}, bf16[2,128,128]{2,1,0:T(8,128)(2,1)S(1)}, u32[]{:S(2)}, u32[]{:S(2)}) collective-permute-start(bf16[2,128,128]{2,1,0:T(8,128)(2,1)S(1)} %pad.9.refs_8_), channel_id=1, source_target_pairs={{0,8},{8,0},{16,24},{24,16},{1,9},{9,1},{17,25},{25,17},{2,10},{10... | collective-permute-start | bytes 196616 | tf_op jit(solution)/shard_map/ppermute | solution.py:38
  4.6 9.3 %collective-permute-start.1 = (bf16[2,128,128]{2,1,0:T(8,128)(2,1)S(1)}, bf16[2,128,128]{2,1,0:T(8,128)(2,1)S(1)}, u32[]{:S(2)}, u32[]{:S(2)}) collective-permute-start(bf16[2,128,128]{2,1,0:T(8,128)(2,1)S(1)} %pad.9.refs_8_), channel_id=1, source_target_pairs={{0,16},{8,24},{16,0},{24,8},{1,17},{9,25},{17,1},{25,9},{2,18},{10... | collective-permute-start | bytes 196616 | tf_op jit(solution)/shard_map/ppermute | solution.py:38
  6.1 7.8 %collective-permute-start.2 = (bf16[2,128,128]{2,1,0:T(8,128)(2,1)S(1)}, bf16[2,128,128]{2,1,0:T(8,128)(2,1)S(1)}, u32[]{:S(2)}, u32[]{:S(2)}) collective-permute-start(bf16[2,128,128]{2,1,0:T(8,128)(2,1)S(1)} %pad.9.refs_8_), channel_id=1, source_target_pairs={{0,24},{8,16},{16,8},{24,0},{1,25},{9,17},{17,9},{25,1},{2,26},{10... | collective-permute-start | bytes 196616 | tf_op jit(solution)/shard_map/ppermute | solution.py:38
  16.1 28.0 %copy-start.43 = (f32[2,128]{1,0:T(2,128)S(1)}, f32[2,128]{1,0:T(2,128)}, u32[]{:S(2)}) copy-start(f32[2,128]{1,0:T(2,128)} %param.14) | copy-start | bytes 3076
  16.1 11.2 %collective-permute-start.3 = (f32[4,2,128,128]{3,2,1,0:T(8,128)S(1)}, f32[4,2,128,128]{3,2,1,0:T(8,128)S(1)}, u32[]{:S(2)}, u32[]{:S(2)}) collective-permute-start(f32[4,2,128,128]{3,2,1,0:T(8,128)S(1)} %get-tuple-element.65), channel_id=1, source_target_pairs={{0,1},{1,0},{2,3},{3,2},{4,5},{5,4},{6,7},{7,6},{8,9},{9,8},{10,11... | collective-permute-start | bytes 1572872 | tf_op jit(solution)/shard_map/ppermute | solution.py:38
  16.8 9.8 %collective-permute-start.22 = (bf16[1,72,2048]{2,1,0:T(8,128)(2,1)}, bf16[1,72,2048]{2,1,0:T(8,128)(2,1)S(1)}, u32[]{:S(2)}, u32[]{:S(2)}) collective-permute-start(bf16[1,72,2048]{2,1,0:T(8,128)(2,1)} %after.22.refs_0_), channel_id=1, source_target_pairs={{0,16},{8,24},{16,0},{24,8},{1,17},{9,25},{17,1},{25,9},{2,18},{10... | collective-permute-start | bytes 884744 | tf_op jit(solution)/shard_map/ppermute | solution.py:38
  18.8 12.5 %collective-permute-start.19 = (bf16[1,72,2048]{2,1,0:T(8,128)(2,1)}, bf16[1,72,2048]{2,1,0:T(8,128)(2,1)S(1)}, u32[]{:S(2)}, u32[]{:S(2)}) collective-permute-start(bf16[1,72,2048]{2,1,0:T(8,128)(2,1)} %after.22.refs_0_), channel_id=1, source_target_pairs={{0,8},{8,0},{16,24},{24,16},{1,9},{9,1},{17,25},{25,17},{2,10},{10... | collective-permute-start | bytes 884744 | tf_op jit(solution)/shard_map/ppermute | solution.py:38
  20.3 21.2 %collective-permute-start.17 = (bf16[1,72,2048]{2,1,0:T(8,128)(2,1)}, bf16[1,72,2048]{2,1,0:T(8,128)(2,1)S(1)}, u32[]{:S(2)}, u32[]{:S(2)}) collective-permute-start(bf16[1,72,2048]{2,1,0:T(8,128)(2,1)} %after.22.refs_0_), channel_id=1, source_target_pairs={{0,2},{1,3},{2,0},{3,1},{4,6},{5,7},{6,4},{7,5},{8,10},{9,11},{10,... | collective-permute-start | bytes 884744 | tf_op jit(solution)/shard_map/ppermute | solution.py:38
  21.8 19.1 %collective-permute-start.16 = (bf16[1,72,2048]{2,1,0:T(8,128)(2,1)}, bf16[1,72,2048]{2,1,0:T(8,128)(2,1)}, u32[]{:S(2)}, u32[]{:S(2)}) collective-permute-start(bf16[1,72,2048]{2,1,0:T(8,128)(2,1)} %after.22.refs_0_), channel_id=1, source_target_pairs={{0,4},{1,5},{2,6},{3,7},{4,0},{5,1},{6,2},{7,3},{8,12},{9,13},{10,... | collective-permute-start | bytes 884744 | tf_op jit(solution)/shard_map/ppermute | solution.py:38
  27.4 16.7 %collective-permute-start.6 = (bf16[2,128,128]{2,1,0:T(8,128)(2,1)S(1)}, bf16[2,128,128]{2,1,0:T(8,128)(2,1)S(1)}, u32[]{:S(2)}, u32[]{:S(2)}) collective-permute-start(bf16[2,128,128]{2,1,0:T(8,128)(2,1)S(1)} %get-tuple-element.117), channel_id=1, source_target_pairs={{0,6},{1,7},{2,4},{3,5},{4,2},{5,3},{6,0},{7,1},{8,14},{9,15},{10,... | collective-permute-start | bytes 196616 | tf_op jit(solution)/shard_map/ppermute | solution.py:38
  31.3 12.8 %collective-permute-start.5 = (bf16[2,128,128]{2,1,0:T(8,128)(2,1)S(1)}, bf16[2,128,128]{2,1,0:T(8,128)(2,1)S(1)}, u32[]{:S(2)}, u32[]{:S(2)}) collective-permute-start(bf16[2,128,128]{2,1,0:T(8,128)(2,1)S(1)} %get-tuple-element.118), channel_id=1, source_target_pairs={{0,2},{1,3},{2,0},{3,1},{4,6},{5,7},{6,4},{7,5},{8,10},{9,11},{10,... | collective-permute-start | bytes 196616 | tf_op jit(solution)/shard_map/ppermute | solution.py:38
  31.3 48.7 %copy-start.28 = (bf16[1,72,2048]{2,1,0:T(8,128)(2,1)}, bf16[1,72,2048]{2,1,0:T(8,128)(2,1)S(1)}, u32[]{:S(2)}) copy-start(bf16[1,72,2048]{2,1,0:T(8,128)(2,1)S(1)} %collective-permute-done.19) | copy-start | bytes 884740
  31.3 12.8 %collective-permute-start.4 = (bf16[2,128,128]{2,1,0:T(8,128)(2,1)S(1)}, bf16[2,128,128]{2,1,0:T(8,128)(2,1)S(1)}, u32[]{:S(2)}, u32[]{:S(2)}) collective-permute-start(bf16[2,128,128]{2,1,0:T(8,128)(2,1)S(1)} %get-tuple-element.116), channel_id=1, source_target_pairs={{0,4},{1,5},{2,6},{3,7},{4,0},{5,1},{6,2},{7,3},{8,12},{9,13},{10,... | collective-permute-start | bytes 196616 | tf_op jit(solution)/shard_map/ppermute | solution.py:38
  40.9 16.3 %collective-permute-start.18 = (bf16[1,72,2048]{2,1,0:T(8,128)(2,1)}, bf16[1,72,2048]{2,1,0:T(8,128)(2,1)}, u32[]{:S(2)}, u32[]{:S(2)}) collective-permute-start(bf16[1,72,2048]{2,1,0:T(8,128)(2,1)} %collective-permute-done.16.refs_0_), channel_id=1, source_target_pairs={{0,2},{1,3},{2,0},{3,1},{4,6},{5,7},{6,4},{7,5},{8,10},{9,11},{10,... | collective-permute-start | bytes 884744 | tf_op jit(solution)/shard_map/ppermute | solution.py:38
  44.2 8.2 %collective-permute-start.9 = (bf16[2,128,128]{2,1,0:T(8,128)(2,1)S(1)}, bf16[2,128,128]{2,1,0:T(8,128)(2,1)S(1)}, u32[]{:S(2)}, u32[]{:S(2)}) collective-permute-start(bf16[2,128,128]{2,1,0:T(8,128)(2,1)S(1)} %fusion.19), channel_id=1, source_target_pairs={{0,6},{1,7},{2,4},{3,5},{4,2},{5,3},{6,0},{7,1},{8,14},{9,15},{10,... | collective-permute-start | bytes 196616 | tf_op jit(solution)/shard_map/ppermute | solution.py:38
  47.4 5.3 %collective-permute-start.8 = (bf16[2,128,128]{2,1,0:T(8,128)(2,1)S(1)}, bf16[2,128,128]{2,1,0:T(8,128)(2,1)S(1)}, u32[]{:S(2)}, u32[]{:S(2)}) collective-permute-start(bf16[2,128,128]{2,1,0:T(8,128)(2,1)S(1)} %fusion.19), channel_id=1, source_target_pairs={{0,2},{1,3},{2,0},{3,1},{4,6},{5,7},{6,4},{7,5},{8,10},{9,11},{10,... | collective-permute-start | bytes 196616 | tf_op jit(solution)/shard_map/ppermute | solution.py:38
  48.6 5.9 %collective-permute-start.7 = (bf16[2,128,128]{2,1,0:T(8,128)(2,1)S(1)}, bf16[2,128,128]{2,1,0:T(8,128)(2,1)S(1)}, u32[]{:S(2)}, u32[]{:S(2)}) collective-permute-start(bf16[2,128,128]{2,1,0:T(8,128)(2,1)S(1)} %fusion.19), channel_id=1, source_target_pairs={{0,4},{1,5},{2,6},{3,7},{4,0},{5,1},{6,2},{7,3},{8,12},{9,13},{10,... | collective-permute-start | bytes 196616 | tf_op jit(solution)/shard_map/ppermute | solution.py:38
  49.3 39.3 %collective-permute-start.20 = (bf16[2,72,2048]{2,1,0:T(8,128)(2,1)}, bf16[2,72,2048]{2,1,0:T(8,128)(2,1)S(1)}, u32[]{:S(2)}, u32[]{:S(2)}) collective-permute-start(bf16[2,72,2048]{2,1,0:T(8,128)(2,1)} %after.24), channel_id=1, source_target_pairs={{0,8},{8,0},{16,24},{24,16},{1,9},{9,1},{17,25},{25,17},{2,10},{10... | collective-permute-start | bytes 1769480 | tf_op jit(solution)/shard_map/ppermute | solution.py:38
  52.4 36.2 %collective-permute-start.23 = (bf16[2,72,2048]{2,1,0:T(8,128)(2,1)}, bf16[2,72,2048]{2,1,0:T(8,128)(2,1)S(1)}, u32[]{:S(2)}, u32[]{:S(2)}) collective-permute-start(bf16[2,72,2048]{2,1,0:T(8,128)(2,1)} %after.24), channel_id=1, source_target_pairs={{0,16},{8,24},{16,0},{24,8},{1,17},{9,25},{17,1},{25,9},{2,18},{10... | collective-permute-start | bytes 1769480 | tf_op jit(solution)/shard_map/ppermute | solution.py:38
  54.5 36.4 %copy-start.3 = (bf16[4,2,128,128]{3,2,1,0:T(8,128)(2,1)}, bf16[4,2,128,128]{3,2,1,0:T(8,128)(2,1)S(1)}, u32[]{:S(2)}) copy-start(bf16[4,2,128,128]{3,2,1,0:T(8,128)(2,1)S(1)} %pad_maximum_fusion.3.refs_0_) | copy-start | bytes 786436
  54.5 16.9 %collective-permute-start.10 = (bf16[4,2,128,128]{3,2,1,0:T(8,128)(2,1)S(1)}, bf16[4,2,128,128]{3,2,1,0:T(8,128)(2,1)S(1)}, u32[]{:S(2)}, u32[]{:S(2)}) collective-permute-start(bf16[4,2,128,128]{3,2,1,0:T(8,128)(2,1)S(1)} %pad_maximum_fusion.3.refs_0_), channel_id=1, source_target_pairs={{0,8},{8,0},{16,24},{24,16},{1,9},{9,1},{17,25},{25,17},{2,10},{10... | collective-permute-start | bytes 786440 | tf_op jit(solution)/shard_map/ppermute | solution.py:38
  54.9 21.2 %collective-permute-start.11 = (bf16[4,2,128,128]{3,2,1,0:T(8,128)(2,1)S(1)}, bf16[4,2,128,128]{3,2,1,0:T(8,128)(2,1)S(1)}, u32[]{:S(2)}, u32[]{:S(2)}) collective-permute-start(bf16[4,2,128,128]{3,2,1,0:T(8,128)(2,1)S(1)} %pad_maximum_fusion.3.refs_0_), channel_id=1, source_target_pairs={{0,16},{8,24},{16,0},{24,8},{1,17},{9,25},{17,1},{25,9},{2,18},{10... | collective-permute-start | bytes 786440 | tf_op jit(solution)/shard_map/ppermute | solution.py:38
  57.2 22.1 %collective-permute-start.12 = (bf16[4,2,128,128]{3,2,1,0:T(8,128)(2,1)S(1)}, bf16[4,2,128,128]{3,2,1,0:T(8,128)(2,1)S(1)}, u32[]{:S(2)}, u32[]{:S(2)}) collective-permute-start(bf16[4,2,128,128]{3,2,1,0:T(8,128)(2,1)S(1)} %pad_maximum_fusion.3.refs_0_), channel_id=1, source_target_pairs={{0,24},{8,16},{16,8},{24,0},{1,25},{9,17},{17,9},{25,1},{2,26},{10... | collective-permute-start | bytes 786440 | tf_op jit(solution)/shard_map/ppermute | solution.py:38
  71.4 8.6 %collective-permute-start.21 = (bf16[1,72,2048]{2,1,0:T(8,128)(2,1)}, bf16[1,72,2048]{2,1,0:T(8,128)(2,1)}, u32[]{:S(2)}, u32[]{:S(2)}) collective-permute-start(bf16[1,72,2048]{2,1,0:T(8,128)(2,1)} %after.25), channel_id=1, source_target_pairs={{0,8},{8,0},{16,24},{24,16},{1,9},{9,1},{17,25},{25,17},{2,10},{10... | collective-permute-start | bytes 884744 | tf_op jit(solution)/shard_map/ppermute | solution.py:38
  76.1 7.8 %collective-permute-start.24 = (bf16[1,72,2048]{2,1,0:T(8,128)(2,1)}, bf16[1,72,2048]{2,1,0:T(8,128)(2,1)}, u32[]{:S(2)}, u32[]{:S(2)}) collective-permute-start(bf16[1,72,2048]{2,1,0:T(8,128)(2,1)} %after.25), channel_id=1, source_target_pairs={{0,16},{8,24},{16,0},{24,8},{1,17},{9,25},{17,1},{25,9},{2,18},{10... | collective-permute-start | bytes 884744 | tf_op jit(solution)/shard_map/ppermute | solution.py:38
  80.0 16.6 %collective-permute-start.13 = (bf16[256,512]{1,0:T(8,128)(2,1)}, bf16[256,512]{1,0:T(8,128)(2,1)S(1)}, u32[]{:S(2)}, u32[]{:S(2)}) collective-permute-start(bf16[256,512]{1,0:T(8,128)(2,1)} %after.19), channel_id=1, source_target_pairs={{0,4},{1,5},{2,6},{3,7},{4,0},{5,1},{6,2},{7,3},{8,12},{9,13},{10,... | collective-permute-start | bytes 786440 | tf_op jit(solution)/shard_map/ppermute | solution.py:38
  80.0 18.7 %collective-permute-start.14 = (bf16[256,512]{1,0:T(8,128)(2,1)}, bf16[256,512]{1,0:T(8,128)(2,1)S(1)}, u32[]{:S(2)}, u32[]{:S(2)}) collective-permute-start(bf16[256,512]{1,0:T(8,128)(2,1)} %after.20), channel_id=1, source_target_pairs={{0,2},{1,3},{2,0},{3,1},{4,6},{5,7},{6,4},{7,5},{8,10},{9,11},{10,... | collective-permute-start | bytes 786440 | tf_op jit(solution)/shard_map/ppermute | solution.py:38
  83.9 15.4 %collective-permute-start.15 = (bf16[256,512]{1,0:T(8,128)(2,1)}, bf16[256,512]{1,0:T(8,128)(2,1)S(1)}, u32[]{:S(2)}, u32[]{:S(2)}) collective-permute-start(bf16[256,512]{1,0:T(8,128)(2,1)} %after.21), channel_id=1, source_target_pairs={{0,6},{1,7},{2,4},{3,5},{4,2},{5,3},{6,0},{7,1},{8,14},{9,15},{10,... | collective-permute-start | bytes 786440 | tf_op jit(solution)/shard_map/ppermute | solution.py:38
  90.0 10.0 %collective-permute-start.25 = (bf16[1,72,2048]{2,1,0:T(8,128)(2,1)}, bf16[1,72,2048]{2,1,0:T(8,128)(2,1)S(1)}, u32[]{:S(2)}, u32[]{:S(2)}) collective-permute-start(bf16[1,72,2048]{2,1,0:T(8,128)(2,1)} %after.26), channel_id=1, source_target_pairs={{0,16},{8,24},{16,0},{24,8},{1,17},{9,25},{17,1},{25,9},{2,18},{10... | collective-permute-start | bytes 884744 | tf_op jit(solution)/shard_map/ppermute | solution.py:38
  90.9 12.7 %collective-permute-start.26 = (bf16[2,72,2048]{2,1,0:T(8,128)(2,1)}, bf16[2,72,2048]{2,1,0:T(8,128)(2,1)S(1)}, u32[]{:S(2)}, u32[]{:S(2)}) collective-permute-start(bf16[2,72,2048]{2,1,0:T(8,128)(2,1)} %after.27), channel_id=1, source_target_pairs={{0,8},{8,0},{16,24},{24,16},{1,9},{9,1},{17,25},{25,17},{2,10},{10... | collective-permute-start | bytes 1769480 | tf_op jit(solution)/shard_map/ppermute | solution.py:38
  96.6 6.9 %collective-permute-start.27 = (bf16[1,72,2048]{2,1,0:T(8,128)(2,1)}, bf16[1,72,2048]{2,1,0:T(8,128)(2,1)S(1)}, u32[]{:S(2)}, u32[]{:S(2)}) collective-permute-start(bf16[1,72,2048]{2,1,0:T(8,128)(2,1)} %after.28), channel_id=1, source_target_pairs={{0,16},{8,24},{16,0},{24,8},{1,17},{9,25},{17,1},{25,9},{2,18},{10... | collective-permute-start | bytes 884744 | tf_op jit(solution)/shard_map/ppermute | solution.py:38
  109.1 54.2 %collective-permute-start.34 = (bf16[1152,2048]{1,0:T(8,128)(2,1)}, bf16[1152,2048]{1,0:T(8,128)(2,1)}, u32[]{:S(2)}, u32[]{:S(2)}) collective-permute-start(bf16[1152,2048]{1,0:T(8,128)(2,1)} %join.3.wn_ref.refs_3_), channel_id=1, source_target_pairs={{0,1},{1,0},{2,3},{3,2},{4,5},{5,4},{6,7},{7,6},{8,9},{9,8},{10,11... | collective-permute-start | bytes 14155784 | tf_op jit(solution)/shard_map/ppermute | solution.py:38
  112.9 5.1 %collective-permute-start.28 = (bf16[160,2048]{1,0:T(8,128)(2,1)S(1)}, bf16[160,2048]{1,0:T(8,128)(2,1)S(1)}, u32[]{:S(2)}, u32[]{:S(2)}) collective-permute-start(bf16[160,2048]{1,0:T(8,128)(2,1)S(1)} %convolution_convert_fusion), channel_id=1, source_target_pairs={{0,1},{1,0},{2,3},{3,2},{4,5},{5,4},{6,7},{7,6},{8,9},{9,8},{10,11... | collective-permute-start | bytes 1966088 | tf_op jit(solution)/shard_map/ppermute | solution.py:38
  113.5 22.7 %collective-permute-start.29 = (bf16[256,512]{1,0:T(8,128)(2,1)}, bf16[256,512]{1,0:T(8,128)(2,1)S(1)}, u32[]{:S(2)}, u32[]{:S(2)}) collective-permute-start(bf16[256,512]{1,0:T(8,128)(2,1)} %after.29), channel_id=1, source_target_pairs={{0,4},{1,5},{2,6},{3,7},{4,0},{5,1},{6,2},{7,3},{8,12},{9,13},{10,... | collective-permute-start | bytes 786440 | tf_op jit(solution)/shard_map/ppermute | solution.py:38
  113.6 22.7 %collective-permute-start.30 = (bf16[256,512]{1,0:T(8,128)(2,1)}, bf16[256,512]{1,0:T(8,128)(2,1)S(1)}, u32[]{:S(2)}, u32[]{:S(2)}) collective-permute-start(bf16[256,512]{1,0:T(8,128)(2,1)} %after.30), channel_id=1, source_target_pairs={{0,2},{1,3},{2,0},{3,1},{4,6},{5,7},{6,4},{7,5},{8,10},{9,11},{10,... | collective-permute-start | bytes 786440 | tf_op jit(solution)/shard_map/ppermute | solution.py:38
  116.3 20.0 %collective-permute-start.31 = (bf16[256,512]{1,0:T(8,128)(2,1)}, bf16[256,512]{1,0:T(8,128)(2,1)S(1)}, u32[]{:S(2)}, u32[]{:S(2)}) collective-permute-start(bf16[256,512]{1,0:T(8,128)(2,1)} %after.31), channel_id=1, source_target_pairs={{0,6},{1,7},{2,4},{3,5},{4,2},{5,3},{6,0},{7,1},{8,14},{9,15},{10,... | collective-permute-start | bytes 786440 | tf_op jit(solution)/shard_map/ppermute | solution.py:38
  121.4 30.3 %copy-start.5 = (bf16[2048,128]{1,0:T(8,128)(2,1)}, bf16[2048,128]{1,0:T(8,128)(2,1)S(1)}, u32[]{:S(2)}) copy-start(bf16[2048,128]{1,0:T(8,128)(2,1)S(1)} %pad_maximum_fusion.1.w3_ref.refs_8_) | copy-start | bytes 1572868
  136.1 17.2 %collective-permute-start.32 = (bf16[128,2048]{1,0:T(8,128)(2,1)}, bf16[128,2048]{1,0:T(8,128)(2,1)S(1)}, u32[]{:S(2)}, u32[]{:S(2)}) collective-permute-start(bf16[128,2048]{1,0:T(8,128)(2,1)} %get-tuple-element.74), channel_id=1, source_target_pairs={{0,1},{1,0},{2,3},{3,2},{4,5},{5,4},{6,7},{7,6},{8,9},{9,8},{10,11... | collective-permute-start | bytes 1572872 | tf_op jit(solution)/shard_map/ppermute | solution.py:38
  151.7 2.2 collective-permute-start.33
  172.8 5.8 %collective-permute-start.37 = (bf16[128,128]{1,0:T(8,128)(2,1)S(1)}, bf16[128,128]{1,0:T(8,128)(2,1)S(1)}, u32[]{:S(2)}, u32[]{:S(2)}) collective-permute-start(bf16[128,128]{1,0:T(8,128)(2,1)S(1)} %get-tuple-element.78.q_ref), channel_id=1, source_target_pairs={{0,6},{1,7},{2,4},{3,5},{4,2},{5,3},{6,0},{7,1},{8,14},{9,15},{10,... | collective-permute-start | bytes 98312 | tf_op jit(solution)/shard_map/ppermute | solution.py:38
  174.9 4.0 %collective-permute-start.36 = (bf16[128,128]{1,0:T(8,128)(2,1)S(1)}, bf16[128,128]{1,0:T(8,128)(2,1)S(1)}, u32[]{:S(2)}, u32[]{:S(2)}) collective-permute-start(bf16[128,128]{1,0:T(8,128)(2,1)S(1)} %get-tuple-element.78.q_ref), channel_id=1, source_target_pairs={{0,2},{1,3},{2,0},{3,1},{4,6},{5,7},{6,4},{7,5},{8,10},{9,11},{10,... | collective-permute-start | bytes 98312 | tf_op jit(solution)/shard_map/ppermute | solution.py:38
  176.3 5.2 %collective-permute-start.35 = (bf16[128,128]{1,0:T(8,128)(2,1)S(1)}, bf16[128,128]{1,0:T(8,128)(2,1)S(1)}, u32[]{:S(2)}, u32[]{:S(2)}) collective-permute-start(bf16[128,128]{1,0:T(8,128)(2,1)S(1)} %get-tuple-element.78.q_ref), channel_id=1, source_target_pairs={{0,4},{1,5},{2,6},{3,7},{4,0},{5,1},{6,2},{7,3},{8,12},{9,13},{10,... | collective-permute-start | bytes 98312 | tf_op jit(solution)/shard_map/ppermute | solution.py:38
  181.5 5.5 %collective-permute-start.38 = (bf16[4,128,128]{2,1,0:T(8,128)(2,1)S(1)}, bf16[4,128,128]{2,1,0:T(8,128)(2,1)S(1)}, u32[]{:S(2)}, u32[]{:S(2)}) collective-permute-start(bf16[4,128,128]{2,1,0:T(8,128)(2,1)S(1)} %pad_maximum_fusion.4.refs_8_), channel_id=1, source_target_pairs={{0,8},{8,0},{16,24},{24,16},{1,9},{9,1},{17,25},{25,17},{2,10},{10... | collective-permute-start | bytes 393224 | tf_op jit(solution)/shard_map/ppermute | solution.py:38
  182.0 6.2 %collective-permute-start.39 = (bf16[4,128,128]{2,1,0:T(8,128)(2,1)S(1)}, bf16[4,128,128]{2,1,0:T(8,128)(2,1)S(1)}, u32[]{:S(2)}, u32[]{:S(2)}) collective-permute-start(bf16[4,128,128]{2,1,0:T(8,128)(2,1)S(1)} %pad_maximum_fusion.4.refs_8_), channel_id=1, source_target_pairs={{0,16},{8,24},{16,0},{24,8},{1,17},{9,25},{17,1},{25,9},{2,18},{10... | collective-permute-start | bytes 393224 | tf_op jit(solution)/shard_map/ppermute | solution.py:38
  183.9 5.9 %collective-permute-start.40 = (bf16[4,128,128]{2,1,0:T(8,128)(2,1)S(1)}, bf16[4,128,128]{2,1,0:T(8,128)(2,1)S(1)}, u32[]{:S(2)}, u32[]{:S(2)}) collective-permute-start(bf16[4,128,128]{2,1,0:T(8,128)(2,1)S(1)} %pad_maximum_fusion.4.refs_8_), channel_id=1, source_target_pairs={{0,24},{8,16},{16,8},{24,0},{1,25},{9,17},{17,9},{25,1},{2,26},{10... | collective-permute-start | bytes 393224 | tf_op jit(solution)/shard_map/ppermute | solution.py:38
  192.8 1.3 collective-permute-start.41
  194.6 1.2 collective-permute-start.42
  195.8 7.2 %collective-permute-start.43 = (bf16[2,128,128]{2,1,0:T(8,128)(2,1)S(1)}, bf16[2,128,128]{2,1,0:T(8,128)(2,1)S(1)}, u32[]{:S(2)}, u32[]{:S(2)}) collective-permute-start(bf16[2,128,128]{2,1,0:T(8,128)(2,1)S(1)} %pad_maximum_fusion.5.refs_8_), channel_id=1, source_target_pairs={{0,4},{1,5},{2,6},{3,7},{4,0},{5,1},{6,2},{7,3},{8,12},{9,13},{10,... | collective-permute-start | bytes 196616 | tf_op jit(solution)/shard_map/ppermute | solution.py:38
  197.2 5.8 %collective-permute-start.44 = (bf16[2,128,128]{2,1,0:T(8,128)(2,1)S(1)}, bf16[2,128,128]{2,1,0:T(8,128)(2,1)S(1)}, u32[]{:S(2)}, u32[]{:S(2)}) collective-permute-start(bf16[2,128,128]{2,1,0:T(8,128)(2,1)S(1)} %pad_maximum_fusion.5.refs_8_), channel_id=1, source_target_pairs={{0,2},{1,3},{2,0},{3,1},{4,6},{5,7},{6,4},{7,5},{8,10},{9,11},{10,... | collective-permute-start | bytes 196616 | tf_op jit(solution)/shard_map/ppermute | solution.py:38
  199.1 6.1 %collective-permute-start.45 = (bf16[2,128,128]{2,1,0:T(8,128)(2,1)S(1)}, bf16[2,128,128]{2,1,0:T(8,128)(2,1)S(1)}, u32[]{:S(2)}, u32[]{:S(2)}) collective-permute-start(bf16[2,128,128]{2,1,0:T(8,128)(2,1)S(1)} %pad_maximum_fusion.5.refs_8_), channel_id=1, source_target_pairs={{0,6},{1,7},{2,4},{3,5},{4,2},{5,3},{6,0},{7,1},{8,14},{9,15},{10,... | collective-permute-start | bytes 196616 | tf_op jit(solution)/shard_map/ppermute | solution.py:38
  207.4 4.3 %collective-permute-start.46 = (f32[128,128]{1,0:T(8,128)S(1)}, f32[128,128]{1,0:T(8,128)S(1)}, u32[]{:S(2)}, u32[]{:S(2)}) collective-permute-start(f32[128,128]{1,0:T(8,128)S(1)} %get-tuple-element.83), channel_id=1, source_target_pairs={{0,8},{8,0},{16,24},{24,16},{1,9},{9,1},{17,25},{25,17},{2,10},{10... | collective-permute-start | bytes 196616 | tf_op jit(solution)/shard_map/ppermute | solution.py:38
  208.3 4.5 %collective-permute-start.47 = (f32[128,128]{1,0:T(8,128)S(1)}, f32[128,128]{1,0:T(8,128)S(1)}, u32[]{:S(2)}, u32[]{:S(2)}) collective-permute-start(f32[128,128]{1,0:T(8,128)S(1)} %get-tuple-element.84), channel_id=1, source_target_pairs={{0,16},{8,24},{16,0},{24,8},{1,17},{9,25},{17,1},{25,9},{2,18},{10... | collective-permute-start | bytes 196616 | tf_op jit(solution)/shard_map/ppermute | solution.py:38
  209.8 5.2 %collective-permute-start.48 = (f32[128,128]{1,0:T(8,128)S(1)}, f32[128,128]{1,0:T(8,128)S(1)}, u32[]{:S(2)}, u32[]{:S(2)}) collective-permute-start(f32[128,128]{1,0:T(8,128)S(1)} %get-tuple-element.85), channel_id=1, source_target_pairs={{0,24},{8,16},{16,8},{24,0},{1,25},{9,17},{17,9},{25,1},{2,26},{10... | collective-permute-start | bytes 196616 | tf_op jit(solution)/shard_map/ppermute | solution.py:38
  220.2 6.4 %collective-permute-start.52 = (bf16[1152,1024]{1,0:T(8,128)(2,1)}, bf16[1152,1024]{1,0:T(8,128)(2,1)}, u32[]{:S(2)}, u32[]{:S(2)}) collective-permute-start(bf16[1152,1024]{1,0:T(8,128)(2,1)} %get-tuple-element.93), channel_id=1, source_target_pairs={{0,1},{1,0},{2,3},{3,2},{4,5},{5,4},{6,7},{7,6},{8,9},{9,8},{10,11... | collective-permute-start | bytes 7077896 | tf_op jit(solution)/shard_map/ppermute | solution.py:38
  225.5 8.1 %collective-permute-start.49 = (bf16[1152,1024]{1,0:T(8,128)(2,1)}, bf16[1152,1024]{1,0:T(8,128)(2,1)}, u32[]{:S(2)}, u32[]{:S(2)}) collective-permute-start(bf16[1152,1024]{1,0:T(8,128)(2,1)} %get-tuple-element.89), channel_id=1, source_target_pairs={{0,1},{1,0},{2,3},{3,2},{4,5},{5,4},{6,7},{7,6},{8,9},{9,8},{10,11... | collective-permute-start | bytes 7077896 | tf_op jit(solution)/shard_map/ppermute | solution.py:38
  232.6 28.2 %collective-permute-start.53 = (bf16[2,4,72,1024]{3,2,1,0:T(8,128)(2,1)}, bf16[2,4,72,1024]{3,2,1,0:T(8,128)(2,1)}, u32[]{:S(2)}, u32[]{:S(2)}) collective-permute-start(bf16[2,4,72,1024]{3,2,1,0:T(8,128)(2,1)} %bitcast.210), channel_id=1, source_target_pairs={{0,16},{8,24},{16,0},{24,8},{1,17},{9,25},{17,1},{25,9},{2,18},{10... | collective-permute-start | bytes 3538952 | tf_op jit(solution)/shard_map/ppermute | solution.py:38
  239.4 29.0 %collective-permute-start.50 = (bf16[2,4,72,1024]{3,2,1,0:T(8,128)(2,1)}, bf16[2,4,72,1024]{3,2,1,0:T(8,128)(2,1)S(1)}, u32[]{:S(2)}, u32[]{:S(2)}) collective-permute-start(bf16[2,4,72,1024]{3,2,1,0:T(8,128)(2,1)} %bitcast.211), channel_id=1, source_target_pairs={{0,8},{8,0},{16,24},{24,16},{1,9},{9,1},{17,25},{25,17},{2,10},{10... | collective-permute-start | bytes 3538952 | tf_op jit(solution)/shard_map/ppermute | solution.py:38
  254.8 16.8 %collective-permute-start.57 = (bf16[2,128,2048]{2,1,0:T(8,128)(2,1)}, bf16[2,128,2048]{2,1,0:T(8,128)(2,1)S(1)}, u32[]{:S(2)}, u32[]{:S(2)}) collective-permute-start(bf16[2,128,2048]{2,1,0:T(8,128)(2,1)} %bitcast.185), channel_id=1, source_target_pairs={{0,1},{1,0},{2,3},{3,2},{4,5},{5,4},{6,7},{7,6},{8,9},{9,8},{10,11... | collective-permute-start | bytes 3145736 | tf_op jit(solution)/shard_map/ppermute | solution.py:38
  262.8 17.6 %collective-permute-start.54 = (bf16[1,4,72,1024]{3,2,1,0:T(8,128)(2,1)S(1)}, bf16[1,4,72,1024]{3,2,1,0:T(8,128)(2,1)}, u32[]{:S(2)}, u32[]{:S(2)}) collective-permute-start(bf16[1,4,72,1024]{3,2,1,0:T(8,128)(2,1)S(1)} %fusion.7), channel_id=1, source_target_pairs={{0,8},{8,0},{16,24},{24,16},{1,9},{9,1},{17,25},{25,17},{2,10},{10... | collective-permute-start | bytes 1769480 | tf_op jit(solution)/shard_map/ppermute | solution.py:38
  269.0 13.5 %collective-permute-start.51 = (bf16[1,4,72,1024]{3,2,1,0:T(8,128)(2,1)S(1)}, bf16[1,4,72,1024]{3,2,1,0:T(8,128)(2,1)S(1)}, u32[]{:S(2)}, u32[]{:S(2)}) collective-permute-start(bf16[1,4,72,1024]{3,2,1,0:T(8,128)(2,1)S(1)} %fusion.6), channel_id=1, source_target_pairs={{0,16},{8,24},{16,0},{24,8},{1,17},{9,25},{17,1},{25,9},{2,18},{10... | collective-permute-start | bytes 1769480 | tf_op jit(solution)/shard_map/ppermute | solution.py:38
  284.5 13.3 %collective-permute-start.55 = (bf16[1,2,72,2048]{3,2,1,0:T(8,128)(2,1)S(1)}, bf16[1,2,72,2048]{3,2,1,0:T(8,128)(2,1)S(1)}, u32[]{:S(2)}, u32[]{:S(2)}) collective-permute-start(bf16[1,2,72,2048]{3,2,1,0:T(8,128)(2,1)S(1)} %fusion.8), channel_id=1, source_target_pairs={{0,2},{1,3},{2,0},{3,1},{4,6},{5,7},{6,4},{7,5},{8,10},{9,11},{10,... | collective-permute-start | bytes 1769480 | tf_op jit(solution)/shard_map/ppermute | solution.py:38
  298.0 13.3 %collective-permute-start.56 = (bf16[1,1,72,2048]{3,2,1,0:T(8,128)(2,1)S(1)}, bf16[1,1,72,2048]{3,2,1,0:T(8,128)(2,1)S(1)}, u32[]{:S(2)}, u32[]{:S(2)}) collective-permute-start(bf16[1,1,72,2048]{3,2,1,0:T(8,128)(2,1)S(1)} %get-tuple-element.113), channel_id=1, source_target_pairs={{0,4},{1,5},{2,6},{3,7},{4,0},{5,1},{6,2},{7,3},{8,12},{9,13},{10,... | collective-permute-start | bytes 884744 | tf_op jit(solution)/shard_map/ppermute | solution.py:38
  312.0 21.8 %all-to-all-start = ((bf16[32,80,128]{2,1,0:T(8,128)(2,1)}), bf16[32,80,128]{2,1,0:T(8,128)(2,1)S(1)}, u32[]{:S(2)}, u32[]{:S(2)}) async-start(bf16[32,80,128]{2,1,0:T(8,128)(2,1)} %after.37), calls=%async_computation | async-start | bytes 1310720 | tf_op jit(solution)/shard_map/all_to_all | solution.py:872
  337.6 24.6 %all-to-all-start.1 = ((bf16[32,96,128]{2,1,0:T(8,128)(2,1)}), bf16[32,96,128]{2,1,0:T(8,128)(2,1)S(1)}, u32[]{:S(2)}, u32[]{:S(2)}) async-start(bf16[32,96,128]{2,1,0:T(8,128)(2,1)} %broadcast_in_dim.74), calls=%async_computation.1 | async-start | bytes 1572864 | tf_op jit(solution)/shard_map/all_to_all | solution.py:881
  (44 other events, 263.4 us)
